TPU v7x, 32 devices: a whole 2x2x4 slice. The times are simulated.
32 devices in a mesh: dp: 4 (over x, core), fsdp: 8 (over z, y).
Axes of the slice: x: 2, y: 2, z: 4, core: 2. Of those that a mesh axis runs over, the one named last changes fastest.
Arguments:
- slot_states: bfloat16 [64, 288, 768], P(('dp', 'fsdp')), may hold values from -6 to 6
- answer_tags: int32 [64, 288], P(('dp', 'fsdp')), may hold values 0 or 1
- slot_mask: int32 [8, 8], replicated, may hold values from 0 to 1, as said below
- retrieval: float32 [8, 8], replicated, may hold values from -4 to 4
- query_emb: bfloat16 [8, 768], P(None, ('dp', 'fsdp')), may hold values from -0.21875 to 0.21875
- qkv_weight: bfloat16 [768, 2304], P(('dp', 'fsdp')), may hold values from -0.21875 to 0.21875
- qkv_bias: bfloat16 [1536], P(('dp', 'fsdp')), may hold values from -1.5 to 1.5
- out_weight: bfloat16 [768, 768], P(('dp', 'fsdp')), may hold values from -0.875 to 0.875
- out_bias: bfloat16 [768], P(('dp', 'fsdp')), may hold values from -1.5 to 1.5
- attn_gain: bfloat16 [768], P(('dp', 'fsdp')), may hold values from 0.5 to 1.5
- attn_shift: bfloat16 [768], P(('dp', 'fsdp')), may hold values from -1.5 to 1.5
- up_weight: bfloat16 [768, 3072], P(('dp', 'fsdp')), may hold values from -0.21875 to 0.21875
- up_bias: bfloat16 [3072], P(('dp', 'fsdp')), may hold values from -1.5 to 1.5
- down_weight: bfloat16 [3072, 768], P(('dp', 'fsdp')), may hold values from -0.109375 to 0.109375
- down_bias: bfloat16 [768], P(('dp', 'fsdp')), may hold values from -1.5 to 1.5
- ffn_gain: bfloat16 [768], P(('dp', 'fsdp')), may hold values from 0.5 to 1.5
- ffn_shift: bfloat16 [768], P(('dp', 'fsdp')), may hold values from -1.5 to 1.5
Outputs:
- mixed_out: bfloat16 [64, 288, 768], P(('dp', 'fsdp'))
- loss: float32 [], replicated
- states_grad: bfloat16 [64, 288, 768], P(('dp', 'fsdp'))
- query_grad: float32 [8, 768], P(None, ('dp', 'fsdp'))
- qkv_weight_grad: float32 [768, 2304], P(('dp', 'fsdp'))
- qkv_bias_grad: float32 [1536], P(('dp', 'fsdp'))
- out_weight_grad: float32 [768, 768], P(('dp', 'fsdp'))
- out_bias_grad: float32 [768], P(('dp', 'fsdp'))
- attn_gain_grad: float32 [768], P(('dp', 'fsdp'))
- attn_shift_grad: float32 [768], P(('dp', 'fsdp'))
- up_weight_grad: float32 [768, 3072], P(('dp', 'fsdp'))
- up_bias_grad: float32 [3072], P(('dp', 'fsdp'))
- down_weight_grad: float32 [3072, 768], P(('dp', 'fsdp'))
- down_bias_grad: float32 [768], P(('dp', 'fsdp'))
- ffn_gain_grad: float32 [768], P(('dp', 'fsdp'))
- ffn_shift_grad: float32 [768], P(('dp', 'fsdp'))
Inputs may be any that keep to these rules, and one draw needn't show every extreme that they name: `slot_mask`: each row holds 4 to 8 ones and 48 ones lie in the whole array; some row has 8 and some row has 4.
All inputs are finite; a program needn't handle non-finite values. No bound on the sum of `answer_tags` on one device may be relied on, other than what follows from the above.
Results may differ from a plain program's by a relative error of at most 0.01.
Values may be sent and summed in bfloat16 or wider, within the bound.
No kernel may reach another device: no remote copies, remote signals or barrier semaphores. Data moves between devices by JAX's collectives and lax.ppermute only.
A program may use at most 192 MiB of HBM per device.

v0:
```python
import math

import jax
import jax.numpy as jnp
from jax import lax
from jax.sharding import PartitionSpec as P

HEAD = 64


eps_norm = 1e-12
loss_scale = 65536.0
neg_fill = -1e30
highest = lax.Precision.HIGHEST


def merged_2(value, axis, join):
    pieces = jax.tree.map(lambda part: lax.all_gather(part, axis), value)
    head = jax.tree.map(lambda part: part[0], pieces)
    tail = jax.tree.map(lambda part: part[1:], pieces)
    running, _ = lax.scan(lambda running, slab: (join(running, slab), None), head, tail)
    return running


def norm_forward(residual, norm_gain, norm_shift):
    center = residual - jnp.mean(residual, axis=-1, keepdims=True)
    spread = jnp.mean(center * center, axis=-1, keepdims=True)
    inverse = lax.rsqrt(spread + eps_norm)
    normed = center * inverse
    return (normed * norm_gain + norm_shift, normed, inverse)


def norm_backward(grad_out, normed, inverse):
    mean_grad = jnp.mean(grad_out, axis=-1, keepdims=True)
    mean_cross = jnp.mean(grad_out * normed, axis=-1, keepdims=True)
    return inverse * (grad_out - mean_grad - normed * mean_cross)


def merge_parts(first, second):
    peak = jnp.maximum(first[0], second[0])
    return (peak, first[1] * jnp.exp(first[0] - peak) + second[1] * jnp.exp(second[0] - peak))


def gelu_exact(values):
    return jax.nn.gelu(values, approximate=False)


def layer_forward(params, slot_states):
    (
        qkv_weight,
        qkv_bias,
        out_weight,
        out_bias,
        attn_gain,
        attn_shift,
        up_weight,
        up_bias,
        down_weight,
        down_bias,
        ffn_gain,
        ffn_shift,
    ) = params
    model_width = slot_states.shape[-1]
    bias_float = qkv_bias.astype(jnp.float32)
    bias_full = jnp.concatenate(
        [bias_float[:model_width], jnp.zeros((model_width,), jnp.float32), bias_float[model_width:]]
    )
    pre_proj = (
        jnp.einsum("bld,de->ble", slot_states, qkv_weight, preferred_element_type=jnp.float32)
        + bias_full
    )
    qkv_low = pre_proj.astype(jnp.bfloat16)
    head_shape = slot_states.shape[:2] + (model_width // HEAD, HEAD)
    query_heads = qkv_low[..., :model_width].reshape(head_shape)
    key_heads = qkv_low[..., model_width : 2 * model_width].reshape(head_shape)
    value_heads = qkv_low[..., 2 * model_width :].reshape(head_shape)
    score_scale = 1.0 / math.sqrt(HEAD)
    raw_scores = (
        jnp.einsum("bqhd,bkhd->bhqk", query_heads, key_heads, preferred_element_type=jnp.float32)
        * score_scale
    )
    row_peak = jnp.max(raw_scores, axis=-1, keepdims=True)
    exp_scores = jnp.exp(raw_scores - row_peak)
    attn_soft = exp_scores / jnp.sum(exp_scores, axis=-1, keepdims=True)
    soft_low = attn_soft.astype(jnp.bfloat16)
    context = (
        jnp.einsum("bhqk,bkhd->bqhd", soft_low, value_heads, preferred_element_type=jnp.float32)
        .astype(jnp.bfloat16)
        .reshape(slot_states.shape)
    )
    attn_out = jnp.einsum(
        "bld,de->ble", context, out_weight, preferred_element_type=jnp.float32
    ) + out_bias.astype(jnp.float32)
    hidden, normed_attn, inverse_attn = norm_forward(
        slot_states.astype(jnp.float32) + attn_out,
        attn_gain.astype(jnp.float32),
        attn_shift.astype(jnp.float32),
    )
    hidden_low = hidden.astype(jnp.bfloat16)
    up_proj = jnp.einsum(
        "bld,df->blf", hidden_low, up_weight, preferred_element_type=jnp.float32
    ) + up_bias.astype(jnp.float32)
    act_low = gelu_exact(up_proj).astype(jnp.bfloat16)
    down_proj = jnp.einsum(
        "blf,fd->bld", act_low, down_weight, preferred_element_type=jnp.float32
    ) + down_bias.astype(jnp.float32)
    mixed, normed_ffn, inverse_ffn = norm_forward(
        hidden_low.astype(jnp.float32) + down_proj,
        ffn_gain.astype(jnp.float32),
        ffn_shift.astype(jnp.float32),
    )
    return (
        query_heads,
        key_heads,
        value_heads,
        attn_soft,
        soft_low,
        context,
        hidden_low,
        normed_attn,
        inverse_attn,
        up_proj,
        act_low,
        normed_ffn,
        inverse_ffn,
        mixed.astype(jnp.bfloat16),
    )


def body(
    slot_states,
    answer_tags,
    slot_mask,
    retrieval,
    query_emb,
    qkv_weight,
    qkv_bias,
    out_weight,
    out_bias,
    attn_gain,
    attn_shift,
    up_weight,
    up_bias,
    down_weight,
    down_bias,
    ffn_gain,
    ffn_shift,
):
    gathered = (
        lax.all_gather(qkv_weight, ("dp", "fsdp"), axis=0, tiled=True),
        lax.all_gather(qkv_bias, ("dp", "fsdp"), axis=0, tiled=True),
        lax.all_gather(out_weight, ("dp", "fsdp"), axis=0, tiled=True),
        lax.all_gather(out_bias, ("dp", "fsdp"), axis=0, tiled=True),
        lax.all_gather(attn_gain, ("dp", "fsdp"), axis=0, tiled=True),
        lax.all_gather(attn_shift, ("dp", "fsdp"), axis=0, tiled=True),
        lax.all_gather(up_weight, ("dp", "fsdp"), axis=0, tiled=True),
        lax.all_gather(up_bias, ("dp", "fsdp"), axis=0, tiled=True),
        lax.all_gather(down_weight, ("dp", "fsdp"), axis=0, tiled=True),
        lax.all_gather(down_bias, ("dp", "fsdp"), axis=0, tiled=True),
        lax.all_gather(ffn_gain, ("dp", "fsdp"), axis=0, tiled=True),
        lax.all_gather(ffn_shift, ("dp", "fsdp"), axis=0, tiled=True),
        lax.all_gather(query_emb, ("dp", "fsdp"), axis=1, tiled=True),
    )
    params = tuple(gathered[:12])
    query_table = gathered[12]
    group_count = lax.axis_size(("dp", "fsdp"))
    device_index = lax.axis_index(("dp", "fsdp"))
    local_count = slot_states.shape[0]
    token_count = slot_states.shape[1]
    query_count, slot_count = slot_mask.shape
    running = jnp.cumsum(slot_mask.reshape(-1), dtype=jnp.int32)
    slot_ranks = jnp.arange(local_count, dtype=jnp.int32) * group_count + device_index
    places = jnp.sum(
        (running[None, :] <= slot_ranks[:, None]).astype(jnp.int32), axis=1, dtype=jnp.int32
    )
    slot_pick = (
        places[:, None] == jnp.arange(query_count * slot_count, dtype=jnp.int32)[None, :]
    ).astype(jnp.float32)
    owner_mask = (places // slot_count)[:, None] == jnp.arange(query_count, dtype=jnp.int32)[
        None, :
    ]
    owner_float = owner_mask.astype(jnp.float32)
    prior_score = jnp.dot(slot_pick, retrieval.reshape(-1), precision=highest)
    chosen_low = jnp.dot(
        owner_mask.astype(jnp.bfloat16), query_table, preferred_element_type=jnp.float32
    ).astype(jnp.bfloat16)
    labels = answer_tags.astype(jnp.float32)
    first_pass = layer_forward(params, slot_states)
    mixed_low = first_pass[13]
    logits = jnp.einsum("bld,bd->bl", mixed_low, chosen_low, preferred_element_type=jnp.float32)
    likelihood = jnp.mean(
        labels * jax.nn.log_sigmoid(logits) + (1.0 - labels) * jax.nn.log_sigmoid(-logits), axis=-1
    )
    scores = likelihood + prior_score
    masked = jnp.where(owner_mask, scores[:, None], neg_fill)
    local_peak = jnp.max(masked, axis=0)
    local_total = jnp.sum(jnp.where(owner_mask, jnp.exp(masked - local_peak[None, :]), 0.0), axis=0)
    merged = merged_2((local_peak, local_total), ("dp", "fsdp"), merge_parts)
    totals = merged[0] + jnp.log(merged[1])
    loss = -jnp.sum(totals)
    doc_weight = jnp.sum(
        jnp.where(owner_mask, jnp.exp(scores[:, None] - totals[None, :]), 0.0), axis=1
    )
    grad_score = -loss_scale * doc_weight
    grad_logit = grad_score[:, None] * (labels - jax.nn.sigmoid(logits)) / token_count
    grad_mixed = grad_logit[..., None] * chosen_low.astype(jnp.float32)[:, None, :]
    grad_chosen = jnp.einsum(
        "bl,bld->bd", grad_logit, mixed_low.astype(jnp.float32), precision=highest
    )
    grad_query = jnp.dot(owner_float.T, grad_chosen, precision=highest)
    params_back = tuple(
        (
            lax.all_gather(qkv_weight, ("dp", "fsdp"), axis=0, tiled=True),
            lax.all_gather(qkv_bias, ("dp", "fsdp"), axis=0, tiled=True),
            lax.all_gather(out_weight, ("dp", "fsdp"), axis=0, tiled=True),
            lax.all_gather(out_bias, ("dp", "fsdp"), axis=0, tiled=True),
            lax.all_gather(attn_gain, ("dp", "fsdp"), axis=0, tiled=True),
            lax.all_gather(attn_shift, ("dp", "fsdp"), axis=0, tiled=True),
            lax.all_gather(up_weight, ("dp", "fsdp"), axis=0, tiled=True),
            lax.all_gather(up_bias, ("dp", "fsdp"), axis=0, tiled=True),
            lax.all_gather(down_weight, ("dp", "fsdp"), axis=0, tiled=True),
            lax.all_gather(down_bias, ("dp", "fsdp"), axis=0, tiled=True),
            lax.all_gather(ffn_gain, ("dp", "fsdp"), axis=0, tiled=True),
            lax.all_gather(ffn_shift, ("dp", "fsdp"), axis=0, tiled=True),
        )
    )
    (
        qkv_full,
        qkv_bias_full,
        out_full,
        out_bias_full,
        attn_gain_full,
        attn_shift_full,
        up_full,
        up_bias_full,
        down_full,
        down_bias_full,
        ffn_gain_full,
        ffn_shift_full,
    ) = params_back
    (
        query_heads,
        key_heads,
        value_heads,
        attn_soft,
        soft_low,
        context,
        hidden_low,
        normed_attn,
        inverse_attn,
        up_proj,
        act_low,
        normed_ffn,
        inverse_ffn,
        mixed_again,
    ) = layer_forward(params_back, slot_states)
    grad_ffn_gain = jnp.sum(grad_mixed * normed_ffn, axis=(0, 1))
    grad_ffn_shift = jnp.sum(grad_mixed, axis=(0, 1))
    grad_res_ffn = norm_backward(
        grad_mixed * ffn_gain_full.astype(jnp.float32), normed_ffn, inverse_ffn
    )
    grad_down_low = grad_res_ffn.astype(jnp.bfloat16)
    grad_down_bias = jnp.sum(grad_down_low, axis=(0, 1), dtype=jnp.float32)
    grad_down_weight = jnp.einsum(
        "blf,bld->fd", act_low, grad_down_low, preferred_element_type=jnp.float32
    )
    grad_act = jnp.einsum(
        "bld,fd->blf", grad_down_low, down_full, preferred_element_type=jnp.float32
    )
    gelu_value, gelu_pull = jax.vjp(gelu_exact, up_proj)
    grad_up_low = gelu_pull(grad_act)[0].astype(jnp.bfloat16)
    grad_up_bias = jnp.sum(grad_up_low, axis=(0, 1), dtype=jnp.float32)
    grad_up_weight = jnp.einsum(
        "bld,blf->df", hidden_low, grad_up_low, preferred_element_type=jnp.float32
    )
    grad_hidden = grad_res_ffn + jnp.einsum(
        "blf,df->bld", grad_up_low, up_full, preferred_element_type=jnp.float32
    )
    grad_attn_gain = jnp.sum(grad_hidden * normed_attn, axis=(0, 1))
    grad_attn_shift = jnp.sum(grad_hidden, axis=(0, 1))
    grad_res_attn = norm_backward(
        grad_hidden * attn_gain_full.astype(jnp.float32), normed_attn, inverse_attn
    )
    grad_attn_low = grad_res_attn.astype(jnp.bfloat16)
    grad_out_bias = jnp.sum(grad_attn_low, axis=(0, 1), dtype=jnp.float32)
    grad_out_weight = jnp.einsum(
        "bld,ble->de", context, grad_attn_low, preferred_element_type=jnp.float32
    )
    grad_context = (
        jnp.einsum("ble,de->bld", grad_attn_low, out_full, preferred_element_type=jnp.float32)
        .astype(jnp.bfloat16)
        .reshape(query_heads.shape)
    )
    grad_soft = jnp.einsum(
        "bqhd,bkhd->bhqk", grad_context, value_heads, preferred_element_type=jnp.float32
    )
    grad_value = jnp.einsum(
        "bhqk,bqhd->bkhd", soft_low, grad_context, preferred_element_type=jnp.float32
    )
    row_cross = jnp.sum(grad_soft * attn_soft, axis=-1, keepdims=True)
    grad_scores_low = (attn_soft * (grad_soft - row_cross)).astype(jnp.bfloat16)
    score_scale = 1.0 / math.sqrt(HEAD)
    grad_qheads = (
        jnp.einsum(
            "bhqk,bkhd->bqhd", grad_scores_low, key_heads, preferred_element_type=jnp.float32
        )
        * score_scale
    )
    grad_kheads = (
        jnp.einsum(
            "bhqk,bqhd->bkhd", grad_scores_low, query_heads, preferred_element_type=jnp.float32
        )
        * score_scale
    )
    flat_shape = slot_states.shape
    grad_pre_low = jnp.concatenate(
        [
            grad_qheads.reshape(flat_shape),
            grad_kheads.reshape(flat_shape),
            grad_value.reshape(flat_shape),
        ],
        axis=-1,
    ).astype(jnp.bfloat16)
    model_width = flat_shape[-1]
    grad_qkv_bias = jnp.concatenate(
        [
            jnp.sum(grad_pre_low[..., :model_width], axis=(0, 1), dtype=jnp.float32),
            jnp.sum(grad_pre_low[..., 2 * model_width :], axis=(0, 1), dtype=jnp.float32),
        ]
    )
    grad_qkv_weight = jnp.einsum(
        "bld,ble->de", slot_states, grad_pre_low, preferred_element_type=jnp.float32
    )
    states_grad = (
        grad_res_attn
        + jnp.einsum("ble,de->bld", grad_pre_low, qkv_full, preferred_element_type=jnp.float32)
    ).astype(jnp.bfloat16)
    all_sums = (
        lax.psum_scatter(grad_qkv_weight, ("dp", "fsdp"), scatter_dimension=0, tiled=True),
        lax.psum_scatter(grad_qkv_bias, ("dp", "fsdp"), scatter_dimension=0, tiled=True),
        lax.psum_scatter(grad_out_weight, ("dp", "fsdp"), scatter_dimension=0, tiled=True),
        lax.psum_scatter(grad_out_bias, ("dp", "fsdp"), scatter_dimension=0, tiled=True),
        lax.psum_scatter(grad_attn_gain, ("dp", "fsdp"), scatter_dimension=0, tiled=True),
        lax.psum_scatter(grad_attn_shift, ("dp", "fsdp"), scatter_dimension=0, tiled=True),
        lax.psum_scatter(grad_up_weight, ("dp", "fsdp"), scatter_dimension=0, tiled=True),
        lax.psum_scatter(grad_up_bias, ("dp", "fsdp"), scatter_dimension=0, tiled=True),
        lax.psum_scatter(grad_down_weight, ("dp", "fsdp"), scatter_dimension=0, tiled=True),
        lax.psum_scatter(grad_down_bias, ("dp", "fsdp"), scatter_dimension=0, tiled=True),
        lax.psum_scatter(grad_ffn_gain, ("dp", "fsdp"), scatter_dimension=0, tiled=True),
        lax.psum_scatter(grad_ffn_shift, ("dp", "fsdp"), scatter_dimension=0, tiled=True),
        lax.psum_scatter(grad_query, ("dp", "fsdp"), scatter_dimension=1, tiled=True),
    )
    summed = tuple(all_sums[:12])
    query_part = all_sums[12]
    return (
        mixed_low,
        loss,
        states_grad,
        query_part,
        summed[0],
        summed[1],
        summed[2],
        summed[3],
        summed[4],
        summed[5],
        summed[6],
        summed[7],
        summed[8],
        summed[9],
        summed[10],
        summed[11],
    )


def solution(mesh):
    in_specs = (
        P(("dp", "fsdp"), None, None),
        P(("dp", "fsdp"), None),
        P(),
        P(),
        P(None, ("dp", "fsdp")),
        P(("dp", "fsdp"), None),
        P(("dp", "fsdp")),
        P(("dp", "fsdp"), None),
        P(("dp", "fsdp")),
        P(("dp", "fsdp")),
        P(("dp", "fsdp")),
        P(("dp", "fsdp"), None),
        P(("dp", "fsdp")),
        P(("dp", "fsdp"), None),
        P(("dp", "fsdp")),
        P(("dp", "fsdp")),
        P(("dp", "fsdp")),
    )
    out_specs = (
        P(("dp", "fsdp"), None, None),
        P(),
        P(("dp", "fsdp"), None, None),
        P(None, ("dp", "fsdp")),
        P(("dp", "fsdp"), None),
        P(("dp", "fsdp")),
        P(("dp", "fsdp"), None),
        P(("dp", "fsdp")),
        P(("dp", "fsdp")),
        P(("dp", "fsdp")),
        P(("dp", "fsdp"), None),
        P(("dp", "fsdp")),
        P(("dp", "fsdp"), None),
        P(("dp", "fsdp")),
        P(("dp", "fsdp")),
        P(("dp", "fsdp")),
    )
    return jax.shard_map(body, mesh=mesh, in_specs=in_specs, out_specs=out_specs, check_vma=False)
```

profile of v0, /device:TPU:0, one launch (start us, length us, event | category | flops | bytes accessed | tf_op | source)
XLA Modules:
  0.0 921.6 jit_solution(4558887351546666139)
XLA Ops:
  16.8 42.5 %all-reduce.21 = (bf16[1536]{0:T(1024)(128)(2,1)S(1)}, bf16[768]{0:T(1024)(128)(2,1)S(1)}, bf16[768]{0:T(1024)(128)(2,1)S(1)}, bf16[768]{0:T(1024)(128)(2,1)S(1)...) all-reduce(bf16[1536]{0:T(1024)(128)(2,1)S(1)} %dynamic-update-slic, ...), channel_id=1, replica_groups=mesh['dp'=4,'fsdp'=8] {'dp','fsdp'}, use_global_device_ids=true, to_apply=%add | all-reduce | flops 9216 | bytes 36864
  62.4 66.6 %all-gather.2 = bf16[32,24,8]{1,2,0:T(8,128)(2,1)S(1)} all-gather(bf16[1,24,8]{1,2,0:T(8,128)(2,1)} %bitcast.170), channel_id=1, replica_groups=mesh['dp'=4,'fsdp'=8] {'dp','fsdp'}, dimensions={0}, use_global_device_ids=true | all-gather | bytes 12672 | tf_op jit(solution)/shard_map/all_gather | solution.py:162
  140.3 5.9 fusion.99
  146.2 6.7 fusion.42
  156.3 39.2 %all-gather.12.cloned.1.call-done = bf16[768,3072]{1,0:T(8,128)(2,1)} async-done(((bf16[24,3072]{1,0:T(8,128)(2,1)}), bf16[768,3072]{1,0:T(8,128)(2,1)}) %all-gather.12.cloned.1.call-update) | async-done | bytes 4718608 | tf_op jit(solution)/shard_map/all_gather | solution.py:156
  195.5 7.3 fusion.41
  205.7 17.6 %multiply_convert_fusion.1 = (bf16[2,288,3072]{2,1,0:T(8,128)(2,1)}, f32[2,288,3072]{2,1,0:T(8,128)}) fusion(f32[2,288,3072]{2,1,0:T(8,128)S(1)} %get-tuple-element.168, f32[3072]{0:T(1024)S(1)} %convert_element_type.127, u8[288,3072]{1,0:T(8,128)(4,1)S(1)} %get-tuple-element.111, u8[288,3072]{1,0:T(8,128)(4,1)S(1)} %get-tuple-element.110), kind=kLoop, calls=%fused_computation.22 | loop fusion | flops 125632512 | bytes 19476480 | tf_op jit(solution)/shard_map/convert_element_type | solution.py:103
  223.2 37.5 %all-gather.14.cloned.1.call-done = bf16[3072,768]{1,0:T(8,128)(2,1)} async-done(((bf16[96,768]{1,0:T(8,128)(2,1)}), bf16[3072,768]{1,0:T(8,128)(2,1)}) %all-gather.14.cloned.1.call-update) | async-done | bytes 4718608 | tf_op jit(solution)/shard_map/all_gather | solution.py:158
  260.8 6.6 fusion.101
  274.9 39.9 %all-reduce.20 = (f32[256]{0:T(256)}, f32[256]{0:T(256)}) all-reduce(f32[256]{0:T(256)} %dynamic-update-slice.8, f32[256]{0:T(256)} %dynamic-update-slice.9), channel_id=2, replica_groups=mesh['dp'=4,'fsdp'=8] {'dp','fsdp'}, use_global_device_ids=true, to_apply=%add.8 | all-reduce | flops 512 | bytes 4096
  322.5 39.2 %while.12 = (s32[]{:T(128)}, f32[8]{0:T(128)}, f32[8]{0:T(128)}, f32[31,8]{1,0:T(8,128)}, f32[31,8]{1,0:T(8,128)}, /*index=5*/s32[]{:T(128)}) while((s32[]{:T(128)}, f32[8]{0:T(128)}, f32[8]{0:T(128)}, f32[31,8]{1,0:T(8,128)}, f32[31,8]{1,0:T(8,128)}, /*index=5*/s32[]{:T(128)}) %tuple.52), condition=%wide.region_12.13_spmd, body=%wide.region_11.12_spmd.sunk | while | flops 50 | bytes 273 | solution.py:21
  368.9 10.3 %convert_reduce_fusion = (f32[3072]{0:T(1024)}, bf16[2,288,3072]{2,1,0:T(8,128)(2,1)S(1)}) fusion(f32[2,288,3072]{2,1,0:T(8,128)} %get-tuple-element.158, bf16[2,288,768]{2,1,0:T(8,128)(2,1)S(1)} %get-tuple-element.152, bf16[3072,768]{1,0:T(8,128)(2,1)} %all-gather.14.cloned.1.call-done, f32[2,288,3072]{2,1,0:T(8,128)} %copy-done.2, f32[3072]{0:T(1024)S(1)} %copy-done.16), kind=kOutput, calls=%fused_computation.20 | convolution fusion | flops 2747986944 | bytes 23322624 | tf_op jit(solution)/shard_map/bld,fd->blf/dot_general | solution.py:267
  394.9 10.0 %multiply_reduce_fusion = (f32[2,12,288]{2,1,0:T(8,128)S(1)}, f32[2,12,288,288]{2,3,1,0:T(8,128)}) fusion(f32[2,12,288,288]{2,3,1,0:T(8,128)} %get-tuple-element.165, f32[2,12,288]{2,1,0:T(8,128)S(1)} %copy-done.14, bf16[2,288,12,64]{1,3,2,0:T(8,128)(2,1)} %bitcast.166, bf16[2,288,12,64]{1,3,2,0:T(8,128)(2,1)S(1)} %bitcast.165), kind=kOutput, calls=%fused_computation.9 | convolution fusion | flops 260769024 | bytes 17750016 | tf_op jit(solution)/shard_map/bqhd,bkhd->bhqk/dot_general | solution.py:294
  405.0 6.3 fusion.45
  412.7 8.6 multiply_convert_fusion
  432.1 7.9 convolution_bitcast_fusion.2
  440.0 8.1 copy.112
  448.5 9.8 %convolution_bitcast_fusion.1 = f32[768,3072]{1,0:T(8,128)} fusion(bf16[2,288,768]{2,1,0:T(8,128)(2,1)} %copy-done.8, bf16[2,288,3072]{2,1,0:T(8,128)(2,1)} %copy-done.7), kind=kOutput, calls=%fused_computation.36 | convolution fusion | flops 2717908992 | bytes 13860864 | tf_op jit(solution)/shard_map/bld,blf->df/dot_general | solution.py:273
  458.4 9.8 %convolution_bitcast_fusion = f32[3072,768]{1,0:T(8,128)} fusion(bf16[2,288,3072]{2,1,0:T(8,128)(2,1)} %get-tuple-element.157, bf16[2,288,768]{2,1,0:T(8,128)(2,1)} %copy-done.11), kind=kOutput, calls=%fused_computation.35 | convolution fusion | flops 2717908992 | bytes 13860864 | tf_op jit(solution)/shard_map/blf,bld->fd/dot_general | solution.py:264
  472.7 41.7 %all-reduce.19 = (f32[8,768]{1,0:T(8,128)S(1)}, f32[1536]{0:T(1024)S(1)}, f32[768]{0:T(1024)S(1)}, f32[768]{0:T(1024)S(1)}, f32[768]{0:T(1024)S(1)}, /*index=5*/...) all-reduce(f32[8,768]{1,0:T(8,128)S(1)} %fusion.62, ...), channel_id=4, replica_groups=mesh['dp'=4,'fsdp'=8] {'dp','fsdp'}, use_global_device_ids=true, to_apply=%region_20.21.clone | all-reduce | flops 15360 | bytes 122880
  519.8 6.8 add_convert_fusion.2
  526.6 103.4 %reduce-scatter.14.cloned.1.call-done = f32[24,2304]{1,0:T(8,128)} async-done(((f32[768,2304]{1,0:T(8,128)}), f32[24,2304]{1,0:T(8,128)}) %reduce-scatter.14.cloned.1.call-update) | async-done | bytes 221200
  630.0 141.3 %reduce-scatter.10.cloned.1.call-done = f32[24,3072]{1,0:T(8,128)} async-done(((f32[768,3072]{1,0:T(8,128)}), f32[24,3072]{1,0:T(8,128)}) %reduce-scatter.10.cloned.1.call-update) | async-done | bytes 294928 | tf_op jit(solution)/shard_map/reduce_scatter | solution.py:345
  771.3 142.1 %reduce-scatter.12.cloned.1.call-done = f32[96,768]{1,0:T(8,128)} async-done(((f32[3072,768]{1,0:T(8,128)}), f32[96,768]{1,0:T(8,128)}) %reduce-scatter.12.cloned.1.call-update) | async-done | bytes 294928 | tf_op jit(solution)/shard_map/reduce_scatter | solution.py:347
  (245 shorter events, 128.8 us)
Async XLA Ops:
  7.2 122.8 %all-gather.8.cloned.1.call-start = ((), (), s32[]{:S(2)}) async-start(), calls=%async_computation.4 | async-start | bytes 3649536 | tf_op jit(solution)/shard_map/all_gather | solution.py:150
  7.9 145.0 %all-gather.10.cloned.1.call-start = ((), (), s32[]{:S(2)}) async-start(), calls=%async_computation.5 | async-start | bytes 1216512 | tf_op jit(solution)/shard_map/all_gather | solution.py:152
  8.7 186.8 %all-gather.12.cloned.1.call-start = ((), (), s32[]{:S(2)}) async-start(), calls=%async_computation.6 | async-start | bytes 4866048 | tf_op jit(solution)/shard_map/all_gather | solution.py:156
  9.4 251.4 %all-gather.14.cloned.1.call-start = ((), (), s32[]{:S(2)}) async-start(), calls=%async_computation.7 | async-start | bytes 4866048 | tf_op jit(solution)/shard_map/all_gather | solution.py:158
  10.0 516.6 %reduce-scatter.8.cloned.1.call-start = ((), (), s32[]{:S(2)}) async-start(), calls=%async_computation.8 | async-start | bytes 2433024 | tf_op jit(solution)/shard_map/reduce_scatter | solution.py:341
  59.3 143.6 %copy-start.15 = (f32[3072]{0:T(1024)}, f32[3072]{0:T(1024)S(1)}, u32[]{:S(2)}) copy-start(f32[3072]{0:T(1024)S(1)} %convert_element_type.127) | copy-start | bytes 36868
  59.3 96.6 %copy-start.19 = (f32[768]{0:T(1024)}, f32[768]{0:T(1024)S(1)}, u32[]{:S(2)}) copy-start(f32[768]{0:T(1024)S(1)} %convert_element_type.123) | copy-start | bytes 9220
  61.1 67.9 %copy-start.44 = (s32[2]{0:T(128)}, s32[2]{0:T(128)S(1)}, u32[]{:S(2)}) copy-start(s32[2]{0:T(128)S(1)} %fusion.84) | copy-start | bytes 28
  61.1 68.9 %copy-start.36 = (s32[2]{0:T(128)}, s32[2]{0:T(128)S(1)}, u32[]{:S(2)}) copy-start(s32[2]{0:T(128)S(1)} %and_select_fusion) | copy-start | bytes 28
  156.0 46.9 %copy-start.22 = (f32[2,288]{1,0:T(2,128)}, f32[2,288]{1,0:T(2,128)S(1)}, u32[]{:S(2)}) copy-start(f32[2,288]{1,0:T(2,128)S(1)} %add_rsqrt_fusion.1) | copy-start | bytes 6916
  156.3 46.5 %copy-start.8 = (bf16[2,288,768]{2,1,0:T(8,128)(2,1)}, bf16[2,288,768]{2,1,0:T(8,128)(2,1)S(1)}, u32[]{:S(2)}) copy-start(bf16[2,288,768]{2,1,0:T(8,128)(2,1)S(1)} %add_convert_fusion.4) | copy-start | bytes 2654212
  364.6 14.7 %copy-start.17 = (f32[2,288]{1,0:T(2,128)}, f32[2,288]{1,0:T(2,128)S(1)}, u32[]{:S(2)}) copy-start(f32[2,288]{1,0:T(2,128)S(1)} %multiply_multiply_fusion.7) | copy-start | bytes 6916
  366.8 12.4 %slice-start = ((s8[4718592]{0:T(1024)(128)(4,1)}), s8[4194304]{0:T(1024)(128)(4,1)S(1)}, s32[]{:S(2)}) async-start(s8[4718592]{0:T(1024)(128)(4,1)} %bitcast.171), calls=%async_computation.12 | async-start | bytes 8388608
  368.9 10.4 %copy-start.11 = (bf16[2,288,768]{2,1,0:T(8,128)(2,1)}, bf16[2,288,768]{2,1,0:T(8,128)(2,1)S(1)}, u32[]{:S(2)}) copy-start(bf16[2,288,768]{2,1,0:T(8,128)(2,1)S(1)} %get-tuple-element.152) | copy-start | bytes 2654212
  368.9 10.4 %copy-start.20 = (f32[768]{0:T(1024)S(1)}, f32[768]{0:T(1024)}, u32[]{:S(2)}) copy-start(f32[768]{0:T(1024)} %copy-done.19) | copy-start | bytes 9220
  368.9 10.4 %copy-start.23 = (f32[2,288]{1,0:T(2,128)S(1)}, f32[2,288]{1,0:T(2,128)}, u32[]{:S(2)}) copy-start(f32[2,288]{1,0:T(2,128)} %copy-done.22) | copy-start | bytes 6916
  368.9 10.4 %copy-start.26 = (f32[2,768]{1,0:T(2,128)S(1)}, f32[2,768]{1,0:T(2,128)}, u32[]{:S(2)}) copy-start(f32[2,768]{1,0:T(2,128)} %get-tuple-element.171) | copy-start | bytes 18436
  368.9 10.4 %slice-start.1 = ((s8[4718592]{0:T(1024)(128)(4,1)}), s8[524288]{0:T(1024)(128)(4,1)S(1)}, s32[]{:S(2)}) async-start(s8[4718592]{0:T(1024)(128)(4,1)} %bitcast.171), calls=%async_computation.13 | async-start | bytes 1048576
  404.9 225.0 %reduce-scatter.14.cloned.1.call-start = ((), (), s32[]{:S(2)}) async-start(), calls=%async_computation.11 | async-start | bytes 7299072
  411.3 9.9 %copy-start.3 = (bf16[2,12,64,288]{3,2,1,0:T(8,128)(2,1)}, bf16[2,12,64,288]{3,2,1,0:T(8,128)(2,1)S(1)}, u32[]{:S(2)}) copy-start(bf16[2,12,64,288]{3,2,1,0:T(8,128)(2,1)S(1)} %fusion.45) | copy-start | bytes 2654212
  448.0 323.3 %reduce-scatter.10.cloned.1.call-start = ((), (), s32[]{:S(2)}) async-start(), calls=%async_computation.9 | async-start | bytes 9732096 | tf_op jit(solution)/shard_map/reduce_scatter | solution.py:345
  458.3 455.1 %reduce-scatter.12.cloned.1.call-start = ((), (), s32[]{:S(2)}) async-start(), calls=%async_computation.10 | async-start | bytes 9732096 | tf_op jit(solution)/shard_map/reduce_scatter | solution.py:347
  468.2 51.5 %copy-start.21 = (f32[768]{0:T(1024)S(1)}, f32[768]{0:T(1024)}, u32[]{:S(2)}) copy-start(f32[768]{0:T(1024)} %copy-done.19) | copy-start | bytes 9220
  468.2 51.5 %copy-start.24 = (f32[2,288]{1,0:T(2,128)S(1)}, f32[2,288]{1,0:T(2,128)}, u32[]{:S(2)}) copy-start(f32[2,288]{1,0:T(2,128)} %copy-done.22) | copy-start | bytes 6916
  (32 other events, 126.7 us)
Sparse Core Ops, SparseCore 0:
  10.9 63.1 all-gather.7
  77.0 52.8 all-gather.9
  132.8 62.6 all-gather.11
  198.2 62.4 all-gather.13
  405.1 99.4 reduce-scatter.7
  511.6 118.3 reduce-scatter.13
  636.4 134.8 reduce-scatter.9
  778.8 134.5 reduce-scatter.11
where the time goes:
time: 928 us; the launch traced here: 922 us
  waiting for transfers between devices  466 us (50%)
  blocking collectives  191 us (21%)
  matrix products  115 us (12%)
  other arithmetic  78.2 us (8%)
  local copies, waits for them, and re-layouts  53.6 us (6%)
  between operations  16.8 us (2%)
    reduce_scatter x1, waiting for transfers between devices, body(): lax.psum_scatter(grad_down_weight, ('dp', 'fsdp'), scatter_dimension=0, t...  142 us
    reduce_scatter x1, waiting for transfers between devices, body(): lax.psum_scatter(grad_up_weight, ('dp', 'fsdp'), scatter_dimension=0, til...  141 us
    unnamed x3, blocking collectives  124 us
    unnamed x9, waiting for transfers between devices  106 us
    all_gather x1, blocking collectives, body(): lax.all_gather(query_emb, ('dp', 'fsdp'), axis=1, tiled=True)  66.6 us
    all_gather x1, waiting for transfers between devices, body(): lax.all_gather(up_weight, ('dp', 'fsdp'), axis=0, tiled=True)  39.2 us
    add x31, other arithmetic, merge_parts(): first[1] * jnp.exp(first[0] - peak) + second[1] * jnp.exp(second[0] - peak)  39.1 us
    all_gather x1, waiting for transfers between devices, body(): lax.all_gather(down_weight, ('dp', 'fsdp'), axis=0, tiled=True)  37.5 us
  transfers between devices with their start and end apart: 8, of which 5 were waited for; matrix products, arithmetic and copies ran while one was open for 15% of the time, Pallas kernels for 0%

commit v1 on v0

--- a/solution.py
+++ b/solution.py
@@ -1,8 +1,12 @@
+import functools
 import math
 
 import jax
 import jax.numpy as jnp
+import numpy as np
 from jax import lax
+from jax.experimental import pallas as pl
+from jax.experimental.pallas import tpu as pltpu
 from jax.sharding import PartitionSpec as P
 
 HEAD = 64
@@ -12,14 +16,6 @@
 loss_scale = 65536.0
 neg_fill = -1e30
 highest = lax.Precision.HIGHEST
-
-
-def merged_2(value, axis, join):
-    pieces = jax.tree.map(lambda part: lax.all_gather(part, axis), value)
-    head = jax.tree.map(lambda part: part[0], pieces)
-    tail = jax.tree.map(lambda part: part[1:], pieces)
-    running, _ = lax.scan(lambda running, slab: (join(running, slab), None), head, tail)
-    return running
 
 
 def norm_forward(residual, norm_gain, norm_shift):
@@ -126,6 +122,217 @@
         mixed.astype(jnp.bfloat16),
     )
 
+AXES = ("dp", "fsdp")
+X_BIT, CORE_BIT, Z_FAR, Z_NEAR, Y_BIT = 16, 8, 4, 2, 1
+LINE = 128
+SMALL = 20
+
+
+def device_offsets(first, second):
+    masks = (Z_FAR, Z_NEAR, first, second)
+    return np.array(
+        [sum(m for k, m in enumerate(masks) if p >> k & 1) for p in range(16)], np.int32
+    )
+
+
+def position_table(device_index):
+    even = device_offsets(X_BIT, Y_BIT)
+    odd = device_offsets(Y_BIT, X_BIT)
+    table_even = jnp.asarray(np.concatenate([even, odd ^ CORE_BIT]))
+    table_odd = jnp.asarray(np.concatenate([odd, even ^ CORE_BIT]))
+    core = (device_index // CORE_BIT) % 2
+    return jnp.where(core == 0, table_even, table_odd) ^ device_index
+
+
+def exchange(value, even_mask, odd_mask):
+    pairs = [(i, i ^ (odd_mask if i & CORE_BIT else even_mask)) for i in range(32)]
+    return lax.ppermute(value, AXES, pairs)
+
+
+def gather_blocks(shard):
+    held = shard[None]
+    for even_mask, odd_mask in ((Z_FAR, Z_FAR), (Z_NEAR, Z_NEAR), (X_BIT, Y_BIT)):
+        held = jnp.concatenate([held, exchange(held, even_mask, odd_mask)])
+    last = exchange(held, Y_BIT, X_BIT)
+    return (held, last, exchange(held, CORE_BIT, CORE_BIT), exchange(last, CORE_BIT, CORE_BIT))
+
+
+def add_low(first, second):
+    return (first.astype(jnp.float32) + second.astype(jnp.float32)).astype(jnp.bfloat16)
+
+
+def scatter_blocks(keep, send):
+    held = add_low(keep, exchange(send, CORE_BIT, CORE_BIT))
+    for even_mask, odd_mask in ((Y_BIT, X_BIT), (X_BIT, Y_BIT), (Z_NEAR, Z_NEAR), (Z_FAR, Z_FAR)):
+        half = held.shape[0] // 2
+        got = exchange(held[half:], even_mask, odd_mask)
+        held = add_low(held[:half], got)
+    return held[0]
+
+
+def place_kernel(widths, table_ref, *refs):
+    pieces, outs, sems = refs[:4], refs[4:-1], refs[-1]
+    copies = []
+    for spot in range(32):
+        start = 0
+        for out, width in zip(outs, widths):
+            copies.append(
+                pltpu.make_async_copy(
+                    pieces[spot // 8].at[spot % 8, :, pl.ds(start, width)],
+                    out.at[table_ref[spot]],
+                    sems.at[len(copies)],
+                )
+            )
+            start += width
+    for copy in copies:
+        copy.start()
+    for copy in copies:
+        copy.wait()
+
+
+def place_blocks(table, pieces, widths):
+    rows = pieces[0].shape[1]
+    return pl.pallas_call(
+        functools.partial(place_kernel, widths),
+        out_shape=[jax.ShapeDtypeStruct((32, rows, width), jnp.bfloat16) for width in widths],
+        in_specs=[pl.BlockSpec(memory_space=pltpu.SMEM)] + [pl.BlockSpec(memory_space=pl.ANY)] * 4,
+        out_specs=[pl.BlockSpec(memory_space=pl.ANY)] * len(widths),
+        scratch_shapes=[pltpu.SemaphoreType.DMA((32 * len(widths),))],
+        name="place_blocks",
+    )(table, *pieces)
+
+
+def pick_kernel(widths, table_ref, *refs):
+    count = len(widths)
+    sources, outs, sems = refs[:count], refs[count:-1], refs[-1]
+    copies = []
+    for spot in range(32):
+        start = 0
+        for source, width in zip(sources, widths):
+            copies.append(
+                pltpu.make_async_copy(
+                    source.at[table_ref[spot]],
+                    outs[spot // 16].at[spot % 16, :, pl.ds(start, width)],
+                    sems.at[len(copies)],
+                )
+            )
+            start += width
+    for copy in copies:
+        copy.start()
+    for copy in copies:
+        copy.wait()
+
+
+def pick_blocks(table, sources):
+    widths = tuple(source.shape[2] for source in sources)
+    rows = sources[0].shape[1]
+    return pl.pallas_call(
+        functools.partial(pick_kernel, widths),
+        out_shape=[jax.ShapeDtypeStruct((16, rows, sum(widths)), jnp.bfloat16)] * 2,
+        in_specs=[pl.BlockSpec(memory_space=pltpu.SMEM)]
+        + [pl.BlockSpec(memory_space=pl.ANY)] * len(widths),
+        out_specs=[pl.BlockSpec(memory_space=pl.ANY)] * 2,
+        scratch_shapes=[pltpu.SemaphoreType.DMA((32 * len(widths),))],
+        name="pick_blocks",
+    )(table, *sources)
+
+
+def merge_all(pair, device_count):
+    if device_count == 32:
+        for mask in (CORE_BIT, X_BIT, Y_BIT, Z_NEAR, Z_FAR):
+            both = jnp.stack(pair)
+            got = exchange(both, mask, mask)
+            pair = merge_parts(pair, (got[0], got[1]))
+        return pair
+    peak = lax.pmax(pair[0], AXES)
+    return (peak, lax.psum(pair[1] * jnp.exp(pair[0] - peak), AXES))
+
+
+def gather_all(arrays, table):
+    (qkv_weight, qkv_bias, out_weight, out_bias, attn_gain, attn_shift, up_weight, up_bias, down_weight, down_bias, ffn_gain, ffn_shift, query_emb) = arrays
+    if table is None:
+        return tuple(
+            lax.all_gather(part, AXES, axis=0, tiled=True) for part in arrays[:-1]
+        ) + (lax.all_gather(query_emb, AXES, axis=1, tiled=True),)
+    rows = qkv_weight.shape[0]
+    small = jnp.concatenate(
+        [
+            jnp.stack([out_bias, attn_gain, attn_shift, down_bias, ffn_gain, ffn_shift], axis=1),
+            qkv_bias.reshape(rows, 2),
+            up_bias.reshape(rows, 4),
+            query_emb.T,
+        ],
+        axis=1,
+    )
+    small = jnp.pad(small, ((0, 0), (0, LINE - small.shape[1])))
+    first = gather_blocks(jnp.concatenate([qkv_weight, out_weight, small], axis=1))
+    second = gather_blocks(up_weight)
+    third = gather_blocks(down_weight)
+    widths = (qkv_weight.shape[1], out_weight.shape[1], LINE)
+    qkv_all, out_all, small_all = place_blocks(table, first, widths)
+    (up_all,) = place_blocks(table, second, (up_weight.shape[1],))
+    (down_all,) = place_blocks(table, third, (down_weight.shape[1],))
+    flat = lambda part: part.reshape(-1, part.shape[2])
+    small_all = flat(small_all)
+    rows6 = small_all[:, :6].T
+    return (
+        flat(qkv_all),
+        small_all[:, 6:8].reshape(-1),
+        flat(out_all),
+        rows6[0],
+        rows6[1],
+        rows6[2],
+        flat(up_all),
+        small_all[:, 8:12].reshape(-1),
+        flat(down_all),
+        rows6[3],
+        rows6[4],
+        rows6[5],
+        small_all[:, 12:20].T,
+    )
+
+
+def scatter_all(grads, table):
+    if table is None:
+        return tuple(
+            lax.psum_scatter(part, AXES, scatter_dimension=0, tiled=True) for part in grads[:-1]
+        ) + (lax.psum_scatter(grads[-1], AXES, scatter_dimension=1, tiled=True),)
+    (qkv_weight, qkv_bias, out_weight, out_bias, attn_gain, attn_shift, up_weight, up_bias, down_weight, down_bias, ffn_gain, ffn_shift, query_emb) = grads
+    blocks = lambda part: part.astype(jnp.bfloat16).reshape(32, -1, part.shape[1])
+    small = jnp.concatenate(
+        [
+            jnp.stack([out_bias, attn_gain, attn_shift, down_bias, ffn_gain, ffn_shift], axis=1),
+            qkv_bias.reshape(-1, 2),
+            up_bias.reshape(-1, 4),
+            query_emb.T,
+        ],
+        axis=1,
+    )
+    small = jnp.pad(small, ((0, 0), (0, LINE - small.shape[1])))
+    down_part = scatter_blocks(*pick_blocks(table, [blocks(down_weight)]))
+    up_part = scatter_blocks(*pick_blocks(table, [blocks(up_weight)]))
+    first = scatter_blocks(
+        *pick_blocks(table, [blocks(qkv_weight), blocks(out_weight), blocks(small)])
+    )
+    first = first.astype(jnp.float32)
+    qkv_width, out_width = qkv_weight.shape[1], out_weight.shape[1]
+    small = first[:, qkv_width + out_width :]
+    return (
+        first[:, :qkv_width],
+        small[:, 6:8].reshape(-1),
+        first[:, qkv_width : qkv_width + out_width],
+        small[:, 0],
+        small[:, 1],
+        small[:, 2],
+        up_part.astype(jnp.float32),
+        small[:, 8:12].reshape(-1),
+        down_part.astype(jnp.float32),
+        small[:, 3],
+        small[:, 4],
+        small[:, 5],
+        small[:, 12:20].T,
+    )
+
 
 def body(
     slot_states,
@@ -146,25 +353,29 @@
     ffn_gain,
     ffn_shift,
 ):
-    gathered = (
-        lax.all_gather(qkv_weight, ("dp", "fsdp"), axis=0, tiled=True),
-        lax.all_gather(qkv_bias, ("dp", "fsdp"), axis=0, tiled=True),
-        lax.all_gather(out_weight, ("dp", "fsdp"), axis=0, tiled=True),
-        lax.all_gather(out_bias, ("dp", "fsdp"), axis=0, tiled=True),
-        lax.all_gather(attn_gain, ("dp", "fsdp"), axis=0, tiled=True),
-        lax.all_gather(attn_shift, ("dp", "fsdp"), axis=0, tiled=True),
-        lax.all_gather(up_weight, ("dp", "fsdp"), axis=0, tiled=True),
-        lax.all_gather(up_bias, ("dp", "fsdp"), axis=0, tiled=True),
-        lax.all_gather(down_weight, ("dp", "fsdp"), axis=0, tiled=True),
-        lax.all_gather(down_bias, ("dp", "fsdp"), axis=0, tiled=True),
-        lax.all_gather(ffn_gain, ("dp", "fsdp"), axis=0, tiled=True),
-        lax.all_gather(ffn_shift, ("dp", "fsdp"), axis=0, tiled=True),
-        lax.all_gather(query_emb, ("dp", "fsdp"), axis=1, tiled=True),
+    group_count = lax.axis_size(AXES)
+    device_index = lax.axis_index(AXES)
+    table = position_table(device_index) if group_count == 32 else None
+    gathered = gather_all(
+        (
+            qkv_weight,
+            qkv_bias,
+            out_weight,
+            out_bias,
+            attn_gain,
+            attn_shift,
+            up_weight,
+            up_bias,
+            down_weight,
+            down_bias,
+            ffn_gain,
+            ffn_shift,
+            query_emb,
+        ),
+        table,
     )
     params = tuple(gathered[:12])
     query_table = gathered[12]
-    group_count = lax.axis_size(("dp", "fsdp"))
-    device_index = lax.axis_index(("dp", "fsdp"))
     local_count = slot_states.shape[0]
     token_count = slot_states.shape[1]
     query_count, slot_count = slot_mask.shape
@@ -195,7 +406,7 @@
     masked = jnp.where(owner_mask, scores[:, None], neg_fill)
     local_peak = jnp.max(masked, axis=0)
     local_total = jnp.sum(jnp.where(owner_mask, jnp.exp(masked - local_peak[None, :]), 0.0), axis=0)
-    merged = merged_2((local_peak, local_total), ("dp", "fsdp"), merge_parts)
+    merged = merge_all((local_peak, local_total), group_count)
     totals = merged[0] + jnp.log(merged[1])
     loss = -jnp.sum(totals)
     doc_weight = jnp.sum(
@@ -208,22 +419,7 @@
         "bl,bld->bd", grad_logit, mixed_low.astype(jnp.float32), precision=highest
     )
     grad_query = jnp.dot(owner_float.T, grad_chosen, precision=highest)
-    params_back = tuple(
-        (
-            lax.all_gather(qkv_weight, ("dp", "fsdp"), axis=0, tiled=True),
-            lax.all_gather(qkv_bias, ("dp", "fsdp"), axis=0, tiled=True),
-            lax.all_gather(out_weight, ("dp", "fsdp"), axis=0, tiled=True),
-            lax.all_gather(out_bias, ("dp", "fsdp"), axis=0, tiled=True),
-            lax.all_gather(attn_gain, ("dp", "fsdp"), axis=0, tiled=True),
-            lax.all_gather(attn_shift, ("dp", "fsdp"), axis=0, tiled=True),
-            lax.all_gather(up_weight, ("dp", "fsdp"), axis=0, tiled=True),
-            lax.all_gather(up_bias, ("dp", "fsdp"), axis=0, tiled=True),
-            lax.all_gather(down_weight, ("dp", "fsdp"), axis=0, tiled=True),
-            lax.all_gather(down_bias, ("dp", "fsdp"), axis=0, tiled=True),
-            lax.all_gather(ffn_gain, ("dp", "fsdp"), axis=0, tiled=True),
-            lax.all_gather(ffn_shift, ("dp", "fsdp"), axis=0, tiled=True),
-        )
-    )
+    params_back = params
     (
         qkv_full,
         qkv_bias_full,
@@ -253,7 +449,7 @@
         normed_ffn,
         inverse_ffn,
         mixed_again,
-    ) = layer_forward(params_back, slot_states)
+    ) = first_pass
     grad_ffn_gain = jnp.sum(grad_mixed * normed_ffn, axis=(0, 1))
     grad_ffn_shift = jnp.sum(grad_mixed, axis=(0, 1))
     grad_res_ffn = norm_backward(
@@ -335,20 +531,23 @@
         grad_res_attn
         + jnp.einsum("ble,de->bld", grad_pre_low, qkv_full, preferred_element_type=jnp.float32)
     ).astype(jnp.bfloat16)
-    all_sums = (
-        lax.psum_scatter(grad_qkv_weight, ("dp", "fsdp"), scatter_dimension=0, tiled=True),
-        lax.psum_scatter(grad_qkv_bias, ("dp", "fsdp"), scatter_dimension=0, tiled=True),
-        lax.psum_scatter(grad_out_weight, ("dp", "fsdp"), scatter_dimension=0, tiled=True),
-        lax.psum_scatter(grad_out_bias, ("dp", "fsdp"), scatter_dimension=0, tiled=True),
-        lax.psum_scatter(grad_attn_gain, ("dp", "fsdp"), scatter_dimension=0, tiled=True),
-        lax.psum_scatter(grad_attn_shift, ("dp", "fsdp"), scatter_dimension=0, tiled=True),
-        lax.psum_scatter(grad_up_weight, ("dp", "fsdp"), scatter_dimension=0, tiled=True),
-        lax.psum_scatter(grad_up_bias, ("dp", "fsdp"), scatter_dimension=0, tiled=True),
-        lax.psum_scatter(grad_down_weight, ("dp", "fsdp"), scatter_dimension=0, tiled=True),
-        lax.psum_scatter(grad_down_bias, ("dp", "fsdp"), scatter_dimension=0, tiled=True),
-        lax.psum_scatter(grad_ffn_gain, ("dp", "fsdp"), scatter_dimension=0, tiled=True),
-        lax.psum_scatter(grad_ffn_shift, ("dp", "fsdp"), scatter_dimension=0, tiled=True),
-        lax.psum_scatter(grad_query, ("dp", "fsdp"), scatter_dimension=1, tiled=True),
+    all_sums = scatter_all(
+        (
+            grad_qkv_weight,
+            grad_qkv_bias,
+            grad_out_weight,
+            grad_out_bias,
+            grad_attn_gain,
+            grad_attn_shift,
+            grad_up_weight,
+            grad_up_bias,
+            grad_down_weight,
+            grad_down_bias,
+            grad_ffn_gain,
+            grad_ffn_shift,
+            grad_query,
+        ),
+        table,
     )
     summed = tuple(all_sums[:12])
     query_part = all_sums[12]

time: 928 us -> 1250 us (1.35)
  Pallas kernels: 0 us -> 883 us
  waiting for transfers between devices: 466 us -> 127 us
  blocking collectives: 191 us -> 0 us
  starting transfers between devices: 0.72 us -> 48.9 us
  other arithmetic: 78.2 us -> 48.2 us
  matrix products: 115 us -> 94.3 us
  local copies, waits for them, and re-layouts: 53.6 us -> 39.9 us
  between operations: 16.8 us -> 4.24 us
    pallas_call x0 -> x6, Pallas kernels: none -> 883 us  [the longest x3 442 us: pick_blocks(): pl.pallas_call(functools.partial(pick_kernel, widths), out_shape=[jax.Sha...]
    reduce_scatter x3 -> x0, waiting for transfers between devices: 283 us -> none  [the longest x1 142 us: body(): lax.psum_scatter(grad_down_weight, ('dp', 'fsdp'), scatter_dimension=0, t...]
    ppermute x0 -> x38, waiting for transfers between devices: none -> 127 us  [exchange(): return lax.ppermute(value, AXES, pairs)]
    unnamed x3 -> x0, blocking collectives: 124 us -> none
    unnamed x9 -> x0, waiting for transfers between devices: 106 us -> none
    all_gather x4 -> x0, waiting for transfers between devices: 76.7 us -> none  [the longest x1 39.2 us: body(): lax.all_gather(up_weight, ('dp', 'fsdp'), axis=0, tiled=True)]
    all_gather x1 -> x0, blocking collectives: 66.6 us -> none  [body(): lax.all_gather(query_emb, ('dp', 'fsdp'), axis=1, tiled=True)]
    ppermute x0 -> x38, starting transfers between devices: none -> 48.9 us  [exchange(): return lax.ppermute(value, AXES, pairs)]
  transfers between devices with their start and end apart: 8 -> 38, of which waited for: 5 -> 20; matrix products, arithmetic and copies ran while one was open for 15% -> 4% of each run, Pallas kernels for 0% -> 47%
where the time goes in v1:
time: 1250 us
  Pallas kernels  883 us (71%)
  waiting for transfers between devices  127 us (10%)
  matrix products  94.3 us (8%)
  starting transfers between devices  48.9 us (4%)
  other arithmetic  48.2 us (4%)
  local copies, waits for them, and re-layouts  39.9 us (3%)
    pallas_call x3, Pallas kernels, pick_blocks(): pl.pallas_call(functools.partial(pick_kernel, widths), out_shape=[jax.Sha...  442 us
    pallas_call x3, Pallas kernels, place_blocks(): pl.pallas_call(functools.partial(place_kernel, widths), out_shape=[jax.Sh...  442 us
    ppermute x38, waiting for transfers between devices, exchange(): return lax.ppermute(value, AXES, pairs)  127 us
    ppermute x38, starting transfers between devices, exchange(): return lax.ppermute(value, AXES, pairs)  48.9 us
  transfers between devices with their start and end apart: 38, of which 20 were waited for; matrix products, arithmetic and copies ran while one was open for 4% of the time, Pallas kernels for 47%

profile of v1, /device:TPU:0, one launch (start us, length us, event | category | flops | bytes accessed | tf_op | source)
XLA Modules:
  0.0 1246.0 jit_solution(10046262079352605241)
XLA Ops:
  18.2 10.5 collective-permute-done.12
  34.4 9.7 collective-permute-done.1
  48.2 12.8 %collective-permute-done.2 = bf16[4,24,3200]{2,1,0:T(8,128)(2,1)S(1)} collective-permute-done((bf16[4,24,3200]{2,1,0:T(8,128)(2,1)S(1)}, bf16[4,24,3200]{2,1,0:T(8,128)(2,1)S(1)}, u32[]{:S(2)}, u32[]{:S(2)}) %collective-permute-start.2) | collective-permute-done | bytes 614432 | tf_op jit(solution)/shard_map/ppermute | solution.py:149
  62.7 10.9 collective-permute-done.14
  76.3 7.2 collective-permute-done.3.refs_1_
  87.1 9.1 collective-permute-done.15.refs_1_
  100.0 145.0 %place_blocks.4 = bf16[32,24,3072]{2,1,0:T(8,128)(2,1)} custom-call(s32[32]{0:T(128)} %fusion.75.table_ref, bf16[8,24,3072]{2,1,0:T(8,128)(2,1)} %copy-done.7, bf16[8,24,3072]{2,1,0:T(8,128)(2,1)} %collective-permute-done.9.refs_1_, bf16[8,24,3072]{2,1,0:T(8,128)(2,1)} %copy-done.22, bf16[8,24,3072]{2,1,0:T(8,128)(2,1)} %collective-permute-done.11.refs_3_), custom_call_target="tpu_custom_call" | custom-call | tf_op jit(solution)/shard_map/place_blocks/pallas_call | solution.py:195
  245.1 145.0 %place_blocks.5 = bf16[32,96,768]{2,1,0:T(8,128)(2,1)} custom-call(s32[32]{0:T(128)} %fusion.75.table_ref, bf16[8,96,768]{2,1,0:T(8,128)(2,1)} %pad_maximum_fusion.3.refs_0_, bf16[8,96,768]{2,1,0:T(8,128)(2,1)} %collective-permute-done.15.refs_1_, bf16[8,96,768]{2,1,0:T(8,128)(2,1)} %collective-permute-done.16.refs_2_, ...), custom_call_target="tpu_custom_call" | custom-call | tf_op jit(solution)/shard_map/place_blocks/pallas_call | solution.py:195
  390.1 151.6 %place_blocks.3 = (bf16[32,24,2304]{2,1,0:T(8,128)(2,1)}, bf16[32,24,768]{2,1,0:T(8,128)(2,1)}, bf16[32,24,128]{2,1,0:T(8,128)(2,1)}) custom-call(s32[32]{0:T(128)} %fusion.75.table_ref, bf16[8,24,3200]{2,1,0:T(8,128)(2,1)} %copy-done.6, bf16[8,24,3200]{2,1,0:T(8,128)(2,1)} %copy-done.21, bf16[8,24,3200]{2,1,0:T(8,128)(2,1)} %collective-permute-done.4.refs_2_, ...), custom_call_target="tpu_custom_call" | custom-call | tf_op jit(solution)/shard_map/place_blocks/pallas_call | solution.py:195
  554.3 6.6 fusion.119
  574.0 16.8 %multiply_convert_fusion.1 = (bf16[2,288,3072]{2,1,0:T(8,128)(2,1)S(1)}, f32[2,288,3072]{2,1,0:T(8,128)S(1)}) fusion(f32[2,288,3072]{2,1,0:T(8,128)S(1)} %get-tuple-element.127, f32[3072]{0:T(1024)S(1)} %copy-done.34, u8[288,3072]{1,0:T(8,128)(4,1)S(1)} %get-tuple-element.83, u8[288,3072]{1,0:T(8,128)(4,1)S(1)} %get-tuple-element.82), kind=kLoop, calls=%fused_computation.17 | loop fusion | flops 125632512 | bytes 19476480 | tf_op jit(solution)/shard_map/convert_element_type | solution.py:99
  590.9 6.7 fusion.121
  619.3 9.8 fusion.123
  629.1 7.8 multiply_reduce_fusion.3
  644.5 8.0 bitcast_reduce_fusion
  652.5 6.6 multiply_reduce_fusion
  680.1 145.0 %pick_blocks.4 = (bf16[16,24,3072]{2,1,0:T(8,128)(2,1)}, bf16[16,24,3072]{2,1,0:T(8,128)(2,1)}) custom-call(s32[32]{0:T(128)} %fusion.75.table_ref, bf16[32,24,3072]{2,1,0:T(8,128)(2,1)} %bitcast.310), custom_call_target="tpu_custom_call" | custom-call | tf_op jit(solution)/shard_map/pick_blocks/pallas_call | solution.py:229
  833.9 145.1 %pick_blocks.5 = (bf16[16,96,768]{2,1,0:T(8,128)(2,1)}, bf16[16,96,768]{2,1,0:T(8,128)(2,1)}) custom-call(s32[32]{0:T(128)} %fusion.75.table_ref, bf16[32,96,768]{2,1,0:T(8,128)(2,1)} %bitcast.309), custom_call_target="tpu_custom_call" | custom-call | tf_op jit(solution)/shard_map/pick_blocks/pallas_call | solution.py:229
  981.2 6.3 bitcast_convert_fusion.2
  989.6 151.6 %pick_blocks.3 = (bf16[16,24,3200]{2,1,0:T(8,128)(2,1)}, bf16[16,24,3200]{2,1,0:T(8,128)(2,1)}) custom-call(s32[32]{0:T(128)} %fusion.75.table_ref, bf16[32,24,2304]{2,1,0:T(8,128)(2,1)} %bitcast.314, bf16[32,24,768]{2,1,0:T(8,128)(2,1)} %bitcast.327, bf16[32,24,128]{2,1,0:T(8,128)(2,1)} %bitcast.333), custom_call_target="tpu_custom_call" | custom-call | tf_op jit(solution)/shard_map/pick_blocks/pallas_call | solution.py:229
  1166.2 15.1 %collective-permute-done.34 = bf16[8,96,768]{2,1,0:T(8,128)(2,1)} collective-permute-done((bf16[8,96,768]{2,1,0:T(8,128)(2,1)}, bf16[8,96,768]{2,1,0:T(8,128)(2,1)}, u32[]{:S(2)}, u32[]{:S(2)}) %collective-permute-start.34) | collective-permute-done | bytes 1179680 | tf_op jit(solution)/shard_map/ppermute | solution.py:149
  1184.5 16.2 %collective-permute-done.24 = bf16[8,24,3200]{2,1,0:T(8,128)(2,1)S(1)} collective-permute-done((bf16[8,24,3200]{2,1,0:T(8,128)(2,1)}, bf16[8,24,3200]{2,1,0:T(8,128)(2,1)S(1)}, u32[]{:S(2)}, u32[]{:S(2)}) %collective-permute-start.24) | collective-permute-done | bytes 1228832 | tf_op jit(solution)/shard_map/ppermute | solution.py:149
  1215.7 8.2 collective-permute-done.36
  1231.6 6.8 collective-permute-done.37
  (392 shorter events, 183.3 us)
Async XLA Ops:
  0.7 14.9 %collective-permute-start.6 = (bf16[1,24,3072]{2,1,0:T(8,128)(2,1)}, bf16[1,24,3072]{2,1,0:T(8,128)(2,1)S(1)}, u32[]{:S(2)}, u32[]{:S(2)}) collective-permute-start(bf16[1,24,3072]{2,1,0:T(8,128)(2,1)} %bitcast.319), channel_id=1, source_target_pairs={{0,4},{1,5},{2,6},{3,7},{4,0},{5,1},{6,2},{7,3},{8,12},{9,13},{10,... | collective-permute-start | bytes 442376 | tf_op jit(solution)/shard_map/ppermute | solution.py:149
  12.6 17.1 %collective-permute-start = (bf16[1,24,3200]{2,1,0:T(8,128)(2,1)S(1)}, bf16[1,24,3200]{2,1,0:T(8,128)(2,1)S(1)}, u32[]{:S(2)}, u32[]{:S(2)}) collective-permute-start(bf16[1,24,3200]{2,1,0:T(8,128)(2,1)S(1)} %fusion.38), channel_id=1, source_target_pairs={{0,4},{1,5},{2,6},{3,7},{4,0},{5,1},{6,2},{7,3},{8,12},{9,13},{10,... | collective-permute-start | bytes 460808 | tf_op jit(solution)/shard_map/ppermute | solution.py:149
  12.7 16.0 %collective-permute-start.12 = (bf16[1,96,768]{2,1,0:T(8,128)(2,1)}, bf16[1,96,768]{2,1,0:T(8,128)(2,1)S(1)}, u32[]{:S(2)}, u32[]{:S(2)}) collective-permute-start(bf16[1,96,768]{2,1,0:T(8,128)(2,1)} %bitcast.323), channel_id=1, source_target_pairs={{0,4},{1,5},{2,6},{3,7},{4,0},{5,1},{6,2},{7,3},{8,12},{9,13},{10,... | collective-permute-start | bytes 442376 | tf_op jit(solution)/shard_map/ppermute | solution.py:149
  16.5 15.3 %collective-permute-start.7 = (bf16[2,24,3072]{2,1,0:T(8,128)(2,1)S(1)}, bf16[2,24,3072]{2,1,0:T(8,128)(2,1)S(1)}, u32[]{:S(2)}, u32[]{:S(2)}) collective-permute-start(bf16[2,24,3072]{2,1,0:T(8,128)(2,1)S(1)} %pad_maximum_fusion.10), channel_id=1, source_target_pairs={{0,2},{1,3},{2,0},{3,1},{4,6},{5,7},{6,4},{7,5},{8,10},{9,11},{10,... | collective-permute-start | bytes 884744 | tf_op jit(solution)/shard_map/ppermute | solution.py:149
  29.6 16.1 %collective-permute-start.13 = (bf16[2,96,768]{2,1,0:T(8,128)(2,1)S(1)}, bf16[2,96,768]{2,1,0:T(8,128)(2,1)S(1)}, u32[]{:S(2)}, u32[]{:S(2)}) collective-permute-start(bf16[2,96,768]{2,1,0:T(8,128)(2,1)S(1)} %pad_maximum_fusion.11), channel_id=1, source_target_pairs={{0,2},{1,3},{2,0},{3,1},{4,6},{5,7},{6,4},{7,5},{8,10},{9,11},{10,... | collective-permute-start | bytes 884744 | tf_op jit(solution)/shard_map/ppermute | solution.py:149
  44.2 16.8 %collective-permute-start.2 = (bf16[4,24,3200]{2,1,0:T(8,128)(2,1)S(1)}, bf16[4,24,3200]{2,1,0:T(8,128)(2,1)S(1)}, u32[]{:S(2)}, u32[]{:S(2)}) collective-permute-start(bf16[4,24,3200]{2,1,0:T(8,128)(2,1)S(1)} %pad_maximum_fusion.6), channel_id=1, source_target_pairs={{0,16},{1,17},{2,18},{3,19},{4,20},{5,21},{6,22},{7,23},{8,9},{9,8... | collective-permute-start | bytes 1843208 | tf_op jit(solution)/shard_map/ppermute | solution.py:149
  45.8 27.8 %collective-permute-start.14 = (bf16[4,96,768]{2,1,0:T(8,128)(2,1)S(1)}, bf16[4,96,768]{2,1,0:T(8,128)(2,1)S(1)}, u32[]{:S(2)}, u32[]{:S(2)}) collective-permute-start(bf16[4,96,768]{2,1,0:T(8,128)(2,1)S(1)} %pad_maximum_fusion.8), channel_id=1, source_target_pairs={{0,16},{1,17},{2,18},{3,19},{4,20},{5,21},{6,22},{7,23},{8,9},{9,8... | collective-permute-start | bytes 1769480 | tf_op jit(solution)/shard_map/ppermute | solution.py:149
  46.6 39.0 %collective-permute-start.9 = (bf16[8,24,3072]{2,1,0:T(8,128)(2,1)S(1)}, bf16[8,24,3072]{2,1,0:T(8,128)(2,1)}, u32[]{:S(2)}, u32[]{:S(2)}) collective-permute-start(bf16[8,24,3072]{2,1,0:T(8,128)(2,1)S(1)} %pad_maximum_fusion.2.refs_0_), channel_id=1, source_target_pairs={{0,1},{1,0},{2,3},{3,2},{4,5},{5,4},{6,7},{7,6},{8,24},{9,25},{10,... | collective-permute-start | bytes 3538952 | tf_op jit(solution)/shard_map/ppermute | solution.py:149
  48.2 37.5 %collective-permute-start.10 = (bf16[8,24,3072]{2,1,0:T(8,128)(2,1)S(1)}, bf16[8,24,3072]{2,1,0:T(8,128)(2,1)S(1)}, u32[]{:S(2)}, u32[]{:S(2)}) collective-permute-start(bf16[8,24,3072]{2,1,0:T(8,128)(2,1)S(1)} %pad_maximum_fusion.2.refs_0_), channel_id=1, source_target_pairs={{0,8},{1,9},{2,10},{3,11},{4,12},{5,13},{6,14},{7,15},{8,0},{9,1},... | collective-permute-start | bytes 3538952 | tf_op jit(solution)/shard_map/ppermute | solution.py:149
  61.1 22.3 %collective-permute-start.3 = (bf16[8,24,3200]{2,1,0:T(8,128)(2,1)S(1)}, bf16[8,24,3200]{2,1,0:T(8,128)(2,1)S(1)}, u32[]{:S(2)}, u32[]{:S(2)}) collective-permute-start(bf16[8,24,3200]{2,1,0:T(8,128)(2,1)S(1)} %pad_maximum_fusion.1.refs_0_), channel_id=1, source_target_pairs={{0,1},{1,0},{2,3},{3,2},{4,5},{5,4},{6,7},{7,6},{8,24},{9,25},{10,... | collective-permute-start | bytes 3686408 | tf_op jit(solution)/shard_map/ppermute | solution.py:149
  74.8 21.4 %collective-permute-start.15 = (bf16[8,96,768]{2,1,0:T(8,128)(2,1)}, bf16[8,96,768]{2,1,0:T(8,128)(2,1)}, u32[]{:S(2)}, u32[]{:S(2)}) collective-permute-start(bf16[8,96,768]{2,1,0:T(8,128)(2,1)} %pad_maximum_fusion.3.refs_0_), channel_id=1, source_target_pairs={{0,1},{1,0},{2,3},{3,2},{4,5},{5,4},{6,7},{7,6},{8,24},{9,25},{10,... | collective-permute-start | bytes 3538952 | tf_op jit(solution)/shard_map/ppermute | solution.py:149
  76.3 313.8 %collective-permute-start.4 = (bf16[8,24,3200]{2,1,0:T(8,128)(2,1)S(1)}, bf16[8,24,3200]{2,1,0:T(8,128)(2,1)}, u32[]{:S(2)}, u32[]{:S(2)}) collective-permute-start(bf16[8,24,3200]{2,1,0:T(8,128)(2,1)S(1)} %pad_maximum_fusion.1.refs_0_), channel_id=1, source_target_pairs={{0,8},{1,9},{2,10},{3,11},{4,12},{5,13},{6,14},{7,15},{8,0},{9,1},... | collective-permute-start | bytes 3686408 | tf_op jit(solution)/shard_map/ppermute | solution.py:149
  83.5 306.6 %collective-permute-start.5 = (bf16[8,24,3200]{2,1,0:T(8,128)(2,1)S(1)}, bf16[8,24,3200]{2,1,0:T(8,128)(2,1)}, u32[]{:S(2)}, u32[]{:S(2)}) collective-permute-start(bf16[8,24,3200]{2,1,0:T(8,128)(2,1)S(1)} %collective-permute-done.3.refs_1_), channel_id=1, source_target_pairs={{0,8},{1,9},{2,10},{3,11},{4,12},{5,13},{6,14},{7,15},{8,0},{9,1},... | collective-permute-start | bytes 3686408 | tf_op jit(solution)/shard_map/ppermute | solution.py:149
  86.7 158.4 %collective-permute-start.16 = (bf16[8,96,768]{2,1,0:T(8,128)(2,1)}, bf16[8,96,768]{2,1,0:T(8,128)(2,1)}, u32[]{:S(2)}, u32[]{:S(2)}) collective-permute-start(bf16[8,96,768]{2,1,0:T(8,128)(2,1)} %pad_maximum_fusion.3.refs_0_), channel_id=1, source_target_pairs={{0,8},{1,9},{2,10},{3,11},{4,12},{5,13},{6,14},{7,15},{8,0},{9,1},... | collective-permute-start | bytes 3538952 | tf_op jit(solution)/shard_map/ppermute | solution.py:149
  96.2 148.9 %collective-permute-start.17 = (bf16[8,96,768]{2,1,0:T(8,128)(2,1)}, bf16[8,96,768]{2,1,0:T(8,128)(2,1)}, u32[]{:S(2)}, u32[]{:S(2)}) collective-permute-start(bf16[8,96,768]{2,1,0:T(8,128)(2,1)} %collective-permute-done.15.refs_1_), channel_id=1, source_target_pairs={{0,8},{1,9},{2,10},{3,11},{4,12},{5,13},{6,14},{7,15},{8,0},{9,1},... | collective-permute-start | bytes 3538952 | tf_op jit(solution)/shard_map/ppermute | solution.py:149
  825.1 316.3 %collective-permute-start.28 = (bf16[16,24,3072]{2,1,0:T(8,128)(2,1)}, bf16[16,24,3072]{2,1,0:T(8,128)(2,1)}, u32[]{:S(2)}, u32[]{:S(2)}) collective-permute-start(bf16[16,24,3072]{2,1,0:T(8,128)(2,1)} %get-tuple-element.31), channel_id=1, source_target_pairs={{0,8},{1,9},{2,10},{3,11},{4,12},{5,13},{6,14},{7,15},{8,0},{9,1},... | collective-permute-start | bytes 7077896 | tf_op jit(solution)/shard_map/ppermute | solution.py:149
  979.0 168.3 %collective-permute-start.33 = (bf16[16,96,768]{2,1,0:T(8,128)(2,1)}, bf16[16,96,768]{2,1,0:T(8,128)(2,1)}, u32[]{:S(2)}, u32[]{:S(2)}) collective-permute-start(bf16[16,96,768]{2,1,0:T(8,128)(2,1)} %get-tuple-element.33), channel_id=1, source_target_pairs={{0,8},{1,9},{2,10},{3,11},{4,12},{5,13},{6,14},{7,15},{8,0},{9,1},... | collective-permute-start | bytes 7077896 | tf_op jit(solution)/shard_map/ppermute | solution.py:149
  1145.8 16.6 %collective-permute-start.29 = (bf16[8,24,3072]{2,1,0:T(8,128)(2,1)}, bf16[8,24,3072]{2,1,0:T(8,128)(2,1)}, u32[]{:S(2)}, u32[]{:S(2)}) collective-permute-start(bf16[8,24,3072]{2,1,0:T(8,128)(2,1)} %slice.291), channel_id=1, source_target_pairs={{0,1},{1,0},{2,3},{3,2},{4,5},{5,4},{6,7},{7,6},{8,24},{9,25},{10,... | collective-permute-start | bytes 3538952 | tf_op jit(solution)/shard_map/ppermute | solution.py:149
  1151.3 29.9 %collective-permute-start.34 = (bf16[8,96,768]{2,1,0:T(8,128)(2,1)}, bf16[8,96,768]{2,1,0:T(8,128)(2,1)}, u32[]{:S(2)}, u32[]{:S(2)}) collective-permute-start(bf16[8,96,768]{2,1,0:T(8,128)(2,1)} %slice.300), channel_id=1, source_target_pairs={{0,1},{1,0},{2,3},{3,2},{4,5},{5,4},{6,7},{7,6},{8,24},{9,25},{10,... | collective-permute-start | bytes 3538952 | tf_op jit(solution)/shard_map/ppermute | solution.py:149
  1156.1 44.6 %collective-permute-start.24 = (bf16[8,24,3200]{2,1,0:T(8,128)(2,1)}, bf16[8,24,3200]{2,1,0:T(8,128)(2,1)S(1)}, u32[]{:S(2)}, u32[]{:S(2)}) collective-permute-start(bf16[8,24,3200]{2,1,0:T(8,128)(2,1)} %slice.276), channel_id=1, source_target_pairs={{0,1},{1,0},{2,3},{3,2},{4,5},{5,4},{6,7},{7,6},{8,24},{9,25},{10,... | collective-permute-start | bytes 3686408 | tf_op jit(solution)/shard_map/ppermute | solution.py:149
  1164.7 38.0 %collective-permute-start.30 = (bf16[4,24,3072]{2,1,0:T(8,128)(2,1)S(1)}, bf16[4,24,3072]{2,1,0:T(8,128)(2,1)S(1)}, u32[]{:S(2)}, u32[]{:S(2)}) collective-permute-start(bf16[4,24,3072]{2,1,0:T(8,128)(2,1)S(1)} %slice.293), channel_id=1, source_target_pairs={{0,16},{1,17},{2,18},{3,19},{4,20},{5,21},{6,22},{7,23},{8,9},{9,8... | collective-permute-start | bytes 1769480 | tf_op jit(solution)/shard_map/ppermute | solution.py:149
  1182.9 21.1 %collective-permute-start.35 = (bf16[4,96,768]{2,1,0:T(8,128)(2,1)S(1)}, bf16[4,96,768]{2,1,0:T(8,128)(2,1)S(1)}, u32[]{:S(2)}, u32[]{:S(2)}) collective-permute-start(bf16[4,96,768]{2,1,0:T(8,128)(2,1)S(1)} %slice.302), channel_id=1, source_target_pairs={{0,16},{1,17},{2,18},{3,19},{4,20},{5,21},{6,22},{7,23},{8,9},{9,8... | collective-permute-start | bytes 1769480 | tf_op jit(solution)/shard_map/ppermute | solution.py:149
  1204.1 19.7 %collective-permute-start.36 = (bf16[2,96,768]{2,1,0:T(8,128)(2,1)S(1)}, bf16[2,96,768]{2,1,0:T(8,128)(2,1)S(1)}, u32[]{:S(2)}, u32[]{:S(2)}) collective-permute-start(bf16[2,96,768]{2,1,0:T(8,128)(2,1)S(1)} %slice.304), channel_id=1, source_target_pairs={{0,2},{1,3},{2,0},{3,1},{4,6},{5,7},{6,4},{7,5},{8,10},{9,11},{10,... | collective-permute-start | bytes 884744 | tf_op jit(solution)/shard_map/ppermute | solution.py:149
  1211.5 17.3 %collective-permute-start.26 = (bf16[2,24,3200]{2,1,0:T(8,128)(2,1)S(1)}, bf16[2,24,3200]{2,1,0:T(8,128)(2,1)S(1)}, u32[]{:S(2)}, u32[]{:S(2)}) collective-permute-start(bf16[2,24,3200]{2,1,0:T(8,128)(2,1)S(1)} %slice.280), channel_id=1, source_target_pairs={{0,2},{1,3},{2,0},{3,1},{4,6},{5,7},{6,4},{7,5},{8,10},{9,11},{10,... | collective-permute-start | bytes 921608 | tf_op jit(solution)/shard_map/ppermute | solution.py:149
  (103 other events, 1860.0 us)

commit v2 on v0

v2 whole, which is shorter than its diff:
```python
import functools
import math

import jax
import jax.numpy as jnp
import numpy as np
from jax import lax
from jax.experimental import pallas as pl
from jax.experimental.pallas import tpu as pltpu
from jax.sharding import PartitionSpec as P

HEAD = 64
PAIR = 2 * HEAD
LINE = 128
AXES = ("dp", "fsdp")
X_BIT, CORE_BIT, Z_FAR, Z_NEAR, Y_BIT = 16, 8, 4, 2, 1
BLOCKS = 32
HALF = BLOCKS // 2

eps_norm = 1e-12
loss_scale = 65536.0
neg_fill = -1e30
f32 = jnp.float32
bf16 = jnp.bfloat16
VMEM = pl.BlockSpec(memory_space=pltpu.VMEM)
SMEM = pl.BlockSpec(memory_space=pltpu.SMEM)
ANYWHERE = pl.BlockSpec(memory_space=pl.ANY)


def device_offsets(first, second):
    masks = (Z_FAR, Z_NEAR, first, second)
    return np.array(
        [sum(m for k, m in enumerate(masks) if p >> k & 1) for p in range(HALF)], np.int32
    )


def position_table(device_index):
    even = device_offsets(X_BIT, Y_BIT)
    odd = device_offsets(Y_BIT, X_BIT)
    table_even = jnp.asarray(np.concatenate([even, odd ^ CORE_BIT]))
    table_odd = jnp.asarray(np.concatenate([odd, even ^ CORE_BIT]))
    core = (device_index // CORE_BIT) % 2
    return jnp.where(core == 0, table_even, table_odd) ^ device_index


def exchange(value, even_mask, odd_mask):
    pairs = [(i, i ^ (odd_mask if i & CORE_BIT else even_mask)) for i in range(BLOCKS)]
    return lax.ppermute(value, AXES, pairs)


def gather_blocks(shard):
    held = shard[None]
    for even_mask, odd_mask in ((Z_FAR, Z_FAR), (Z_NEAR, Z_NEAR), (X_BIT, Y_BIT)):
        held = jnp.concatenate([held, exchange(held, even_mask, odd_mask)])
    last = exchange(held, Y_BIT, X_BIT)
    return (held, last, exchange(held, CORE_BIT, CORE_BIT), exchange(last, CORE_BIT, CORE_BIT))


def gather_plain(part):
    whole = lax.all_gather(part, AXES, axis=0, tiled=True)
    blocks = whole.reshape(BLOCKS, -1, whole.shape[1])
    return tuple(blocks[8 * k : 8 * k + 8] for k in range(4))


def add_low(first, second):
    return (first.astype(f32) + second.astype(f32)).astype(bf16)


def scatter_blocks(keep, send):
    held = add_low(keep, exchange(send, CORE_BIT, CORE_BIT))
    for even_mask, odd_mask in ((Y_BIT, X_BIT), (X_BIT, Y_BIT), (Z_NEAR, Z_NEAR), (Z_FAR, Z_FAR)):
        half = held.shape[0] // 2
        got = exchange(held[half:], even_mask, odd_mask)
        held = add_low(held[:half], got)
    return held[0].astype(f32)


def scatter_plain(keep, send):
    blocks = jnp.concatenate([keep, send])
    whole = blocks.reshape(-1, blocks.shape[2])
    return lax.psum_scatter(whole, AXES, scatter_dimension=0, tiled=True).astype(f32)


def merge_parts(first, second):
    peak = jnp.maximum(first[0], second[0])
    return (peak, first[1] * jnp.exp(first[0] - peak) + second[1] * jnp.exp(second[0] - peak))


def merge_all(pair, tuned):
    if tuned:
        for mask in (CORE_BIT, X_BIT, Y_BIT, Z_NEAR, Z_FAR):
            both = jnp.stack(pair)
            got = exchange(both, mask, mask)
            pair = merge_parts(pair, (got[0], got[1]))
        return pair
    peak = lax.pmax(pair[0], AXES)
    return (peak, lax.psum(pair[1] * jnp.exp(pair[0] - peak), AXES))


def call(kernel, name, outs, in_specs, out_specs, args, flops, moved, scratch=(), exps=0):
    return pl.pallas_call(
        kernel,
        out_shape=[jax.ShapeDtypeStruct(shape, dtype) for shape, dtype in outs],
        in_specs=in_specs,
        out_specs=out_specs,
        scratch_shapes=list(scratch),
        compiler_params=pltpu.CompilerParams(vmem_limit_bytes=44 * 2**20),
        cost_estimate=pl.CostEstimate(
            flops=int(flops), bytes_accessed=int(moved), transcendentals=int(exps)
        ),
        name=name,
    )(*args)


def mm(first, second):
    return jnp.dot(first, second, preferred_element_type=f32)


def mm_nt(first, second):
    return lax.dot_general(first, second, (((1,), (1,)), ((), ())), preferred_element_type=f32)


def mm_tn(first, second):
    return lax.dot_general(first, second, (((0,), (0,)), ((), ())), preferred_element_type=f32)


def row_mean(value):
    return jnp.mean(value, axis=-1, keepdims=True)


def block_copies(table_ref, pieces, start, width, target, sems):
    copies = [
        pltpu.make_async_copy(
            pieces[spot // 8].at[spot % 8, :, pl.ds(start, width)],
            target.at[table_ref[spot]],
            sems.at[spot],
        )
        for spot in range(BLOCKS)
    ]
    for copy in copies:
        copy.start()
    return copies


def wait_all(copies):
    for copy in copies:
        copy.wait()


def flat(value):
    return value.reshape(-1, value.shape[-1])


def small_kernel(start, table_ref, p0, p1, p2, p3, columns_ref, rows_ref, held_ref, sems):
    wait_all(block_copies(table_ref, (p0, p1, p2, p3), start, LINE, held_ref, sems))
    columns = flat(held_ref[...]).astype(f32)
    columns_ref[...] = columns
    rows_ref[...] = columns.T


def unpack_small(table, pieces, start):
    rows = pieces[0].shape[1]
    width = BLOCKS * rows
    return call(
        functools.partial(small_kernel, start),
        "unpack_small",
        [((width, LINE), f32), ((LINE, width), f32)],
        [SMEM] + [ANYWHERE] * 4,
        [VMEM, VMEM],
        (table, *pieces),
        0,
        width * LINE * 8,
        [pltpu.VMEM((BLOCKS, rows, LINE), bf16), pltpu.SemaphoreType.DMA((BLOCKS,))],
    )


def head_masks(shape):
    lane = lax.broadcasted_iota(jnp.int32, shape, 1)
    return lane < HEAD


def stacked(pair, low):
    zero = jnp.zeros_like(pair)
    return jnp.concatenate([jnp.where(low, pair, zero), jnp.where(low, zero, pair)])


def unstacked(value, low, length):
    return jnp.where(low, value[:length], value[length:])


def attention_kernel(
    buffers, table_ref, x_ref, bias_ref, p0, p1, p2, p3,
    qkv_ref, context_ref, lse_ref, wqkv_ref, wout_ref, sems, sems_out,
):
    pieces = (p0, p1, p2, p3)
    tokens, width = x_ref.shape
    length, pairs = tokens // buffers, width // PAIR
    copies = block_copies(table_ref, pieces, 0, 3 * width, wqkv_ref, sems)
    later = block_copies(table_ref, pieces, 3 * width, width, wout_ref, sems_out)
    wait_all(copies)
    x = x_ref[...]
    for part in range(3):
        span = slice(part * width, (part + 1) * width)
        weight = flat(wqkv_ref[:, :, span])
        qkv_ref[:, span] = (mm(x, weight) + bias_ref[:, span]).astype(bf16)
    scale = 1.0 / math.sqrt(HEAD)

    def step(index, carry):
        rows = pl.ds(pl.multiple_of(index // pairs * length, length), length)
        lane = pl.multiple_of(index % pairs * PAIR, PAIR)
        query = qkv_ref[rows, pl.ds(lane, PAIR)]
        key = qkv_ref[rows, pl.ds(lane + width, PAIR)]
        value = qkv_ref[rows, pl.ds(lane + 2 * width, PAIR)]
        low = head_masks(query.shape)
        scores = mm_nt(key, stacked(query, low)) * scale
        peak = jnp.max(scores, axis=0, keepdims=True)
        powers = jnp.exp(scores - peak)
        total = jnp.sum(powers, axis=0, keepdims=True)
        probs = (powers * (1.0 / total)).astype(bf16)
        mixed = mm_tn(value, probs).T
        context_ref[rows, pl.ds(lane, PAIR)] = unstacked(mixed, low, length).astype(bf16)
        lse_ref[index] = peak + jnp.log(total)
        return carry

    lax.fori_loop(0, buffers * pairs, step, 0)
    wait_all(later)


def attention_forward(table, x, buffers, bias, pieces):
    tokens, width = x.shape
    rows = pieces[0].shape[1]
    steps = buffers * (width // PAIR)
    length = tokens // buffers
    return call(
        functools.partial(attention_kernel, buffers),
        "attention_forward",
        [
            ((tokens, 3 * width), bf16),
            ((tokens, width), bf16),
            ((steps, 1, 2 * length), f32),
            ((BLOCKS, rows, 3 * width), bf16),
            ((BLOCKS, rows, width), bf16),
        ],
        [SMEM, VMEM, VMEM] + [ANYWHERE] * 4,
        [VMEM] * 5,
        (table, x, bias, *pieces),
        2 * tokens * width * (3 * width + 2 * length),
        20e6,
        [pltpu.SemaphoreType.DMA((BLOCKS,)), pltpu.SemaphoreType.DMA((BLOCKS,))],
        exps=tokens * length * width // HEAD,
    )


def normed_rows(residual):
    center = residual - row_mean(residual)
    inverse = lax.rsqrt(row_mean(center * center) + eps_norm)
    return center * inverse, inverse


def up_kernel(
    table_ref, x_ref, context_ref, wout_ref, vectors_ref, bias_ref, p0, p1, p2, p3,
    hidden_ref, normed_ref, inverse_ref, act_ref, slope_ref, wup_ref, sems,
):
    copies = block_copies(table_ref, (p0, p1, p2, p3), 0, wup_ref.shape[2], wup_ref, sems)
    out = mm(context_ref[...], flat(wout_ref[...])) + vectors_ref[0:1]
    normed, inverse = normed_rows(x_ref[...].astype(f32) + out)
    normed_ref[...] = normed
    inverse_ref[...] = inverse
    hidden = (normed * vectors_ref[1:2] + vectors_ref[2:3]).astype(bf16)
    hidden_ref[...] = hidden
    wait_all(copies)
    wide = 512

    def step(index, carry):
        span = pl.ds(pl.multiple_of(index * wide, wide), wide)
        up = mm(hidden_ref[...], flat(wup_ref[:, :, span])) + bias_ref[:, span]
        chance = 0.5 + 0.5 * lax.erf(up * math.sqrt(0.5))
        act_ref[:, span] = (up * chance).astype(bf16)
        density = jnp.exp(up * up * -0.5) * (1.0 / math.sqrt(2.0 * math.pi))
        slope_ref[:, span] = (chance + up * density).astype(bf16)
        return carry

    lax.fori_loop(0, wup_ref.shape[2] // wide, step, 0)


def up_forward(table, x, context, wout, vectors, bias, pieces):
    tokens, width = x.shape
    rows, hidden_units = pieces[0].shape[1:]
    return call(
        up_kernel,
        "up_forward",
        [
            ((tokens, width), bf16),
            ((tokens, width), f32),
            ((tokens, 1), f32),
            ((tokens, hidden_units), bf16),
            ((tokens, hidden_units), bf16),
            ((BLOCKS, rows, hidden_units), bf16),
        ],
        [SMEM] + [VMEM] * 5 + [ANYWHERE] * 4,
        [VMEM] * 6,
        (table, x, context, wout, vectors, bias, *pieces),
        2 * tokens * width * (width + hidden_units),
        20e6,
        [pltpu.SemaphoreType.DMA((BLOCKS,))],
        exps=2 * tokens * hidden_units,
    )


def down_kernel(
    buffers, table_ref, hidden_ref, act_ref, vectors_ref, chosen_ref, tags_ref, p0, p1, p2, p3,
    mixed_ref, like_ref, res_ref, low_ref, gain_ref, query_ref, bias_ref, wdown_ref, sems,
):
    tokens = hidden_ref.shape[0]
    length = tokens // buffers
    wait_all(block_copies(table_ref, (p0, p1, p2, p3), 0, wdown_ref.shape[2], wdown_ref, sems))
    weight = flat(wdown_ref[...])
    for buffer in range(buffers):
        rows = slice(buffer * length, (buffer + 1) * length)
        down = mm(act_ref[rows], weight) + vectors_ref[3:4]
        normed, inverse = normed_rows(hidden_ref[rows].astype(f32) + down)
        mixed = (normed * vectors_ref[4:5] + vectors_ref[5:6]).astype(bf16)
        mixed_ref[rows] = mixed
        mixed = mixed.astype(f32)
        chosen = chosen_ref[buffer : buffer + 1]
        logits = jnp.sum(mixed * chosen, axis=-1, keepdims=True)
        tags = tags_ref[rows].astype(f32)
        tail = jnp.log(1.0 + jnp.exp(-jnp.abs(logits)))
        log_yes = jnp.minimum(logits, 0.0) - tail
        log_no = jnp.minimum(-logits, 0.0) - tail
        like = jnp.sum(tags * log_yes + (1.0 - tags) * log_no, axis=0, keepdims=True) / length
        like_ref[buffer : buffer + 1] = jnp.broadcast_to(like, (1, LINE))
        pull = (tags - 1.0 / (1.0 + jnp.exp(-logits))) * (-loss_scale / length)
        gain_ref[buffer : buffer + 1] = jnp.sum(pull * normed, axis=0, keepdims=True) * chosen
        gain_ref[buffers + buffer : buffers + buffer + 1] = (
            jnp.sum(pull, axis=0, keepdims=True) * chosen
        )
        query_ref[buffer : buffer + 1] = jnp.sum(pull * mixed, axis=0, keepdims=True)
        slope = chosen * vectors_ref[4:5]
        grad = (inverse * pull) * (
            slope - row_mean(slope) - normed * row_mean(slope * normed)
        )
        res_ref[rows] = grad
        grad = grad.astype(bf16)
        low_ref[rows] = grad
        bias_ref[buffer : buffer + 1] = jnp.sum(grad.astype(f32), axis=0, keepdims=True)


def down_forward(table, hidden, act, vectors, chosen, tags, pieces, buffers):
    tokens, width = hidden.shape
    rows = pieces[0].shape[1]
    return call(
        functools.partial(down_kernel, buffers),
        "down_forward",
        [
            ((tokens, width), bf16),
            ((buffers, LINE), f32),
            ((tokens, width), f32),
            ((tokens, width), bf16),
            ((2 * buffers, width), f32),
            ((buffers, width), f32),
            ((buffers, width), f32),
            ((BLOCKS, rows, width), bf16),
        ],
        [SMEM] + [VMEM] * 5 + [ANYWHERE] * 4,
        [VMEM] * 8,
        (table, hidden, act, vectors, chosen, tags, *pieces),
        2 * tokens * width * BLOCKS * rows,
        20e6,
        [pltpu.SemaphoreType.DMA((BLOCKS,))],
    )


def up_back_kernel(buffers, low_ref, wdown_ref, slope_ref, grad_ref, bias_ref):
    tokens, units = slope_ref.shape
    length = tokens // buffers
    rows_of = wdown_ref.shape[1]
    part = 8

    def step(index, carry):
        blocks = pl.ds(index * part, part)
        wide = part * rows_of
        span = pl.ds(pl.multiple_of(index * wide, wide), wide)
        grad = mm_nt(low_ref[...], flat(wdown_ref[blocks])) * slope_ref[:, span].astype(f32)
        grad = grad.astype(bf16)
        grad_ref[:, span] = grad
        for buffer in range(buffers):
            piece = grad[buffer * length : (buffer + 1) * length].astype(f32)
            bias_ref[buffer : buffer + 1, span] = jnp.sum(piece, axis=0, keepdims=True)
        return carry

    lax.fori_loop(0, BLOCKS // part, step, 0)


def up_backward(low, wdown, slope, buffers):
    tokens, units = slope.shape
    return call(
        functools.partial(up_back_kernel, buffers),
        "up_backward",
        [((tokens, units), bf16), ((buffers, units), f32)],
        [VMEM] * 3,
        [VMEM] * 2,
        (low, wdown, slope),
        2 * tokens * units * low.shape[1],
        13e6,
    )


def hidden_back_kernel(
    buffers, res_ref, grad_up_ref, wup_ref, normed_ref, inverse_ref, vectors_ref, wout_ref,
    res_out_ref, low_ref, context_ref, gain_ref, bias_ref,
):
    tokens = res_ref.shape[0]
    length = tokens // buffers
    weight, weight_out = flat(wup_ref[...]), flat(wout_ref[...])
    for buffer in range(buffers):
        rows = slice(buffer * length, (buffer + 1) * length)
        normed = normed_ref[rows]
        grad = res_ref[rows] + mm_nt(grad_up_ref[rows], weight)
        gain_ref[buffer : buffer + 1] = jnp.sum(grad * normed, axis=0, keepdims=True)
        gain_ref[buffers + buffer : buffers + buffer + 1] = jnp.sum(grad, axis=0, keepdims=True)
        grad = grad * vectors_ref[1:2]
        grad = inverse_ref[rows] * (
            grad - row_mean(grad) - normed * row_mean(grad * normed)
        )
        res_out_ref[rows] = grad
        grad = grad.astype(bf16)
        low_ref[rows] = grad
        bias_ref[buffer : buffer + 1] = jnp.sum(grad.astype(f32), axis=0, keepdims=True)
        context_ref[rows] = mm_nt(grad, weight_out).astype(bf16)


def hidden_backward(res, grad_up, wup, normed, inverse, vectors, wout, buffers):
    tokens, width = res.shape
    return call(
        functools.partial(hidden_back_kernel, buffers),
        "hidden_backward",
        [
            ((tokens, width), f32),
            ((tokens, width), bf16),
            ((tokens, width), bf16),
            ((2 * buffers, width), f32),
            ((buffers, width), f32),
        ],
        [VMEM] * 7,
        [VMEM] * 5,
        (res, grad_up, wup, normed, inverse, vectors, wout),
        2 * tokens * width * (width + grad_up.shape[1]),
        18e6,
    )


def attention_back_kernel(buffers, qkv_ref, lse_ref, grad_ref, pre_ref, bias_ref):
    tokens, width = grad_ref.shape
    length, pairs = tokens // buffers, width // PAIR
    scale = 1.0 / math.sqrt(HEAD)

    def step(index, carry):
        rows = pl.ds(pl.multiple_of(index // pairs * length, length), length)
        lane = pl.multiple_of(index % pairs * PAIR, PAIR)
        query = qkv_ref[rows, pl.ds(lane, PAIR)]
        key = qkv_ref[rows, pl.ds(lane + width, PAIR)]
        value = qkv_ref[rows, pl.ds(lane + 2 * width, PAIR)]
        low = head_masks(query.shape)
        query = stacked(query, low)
        grad = stacked(grad_ref[rows, pl.ds(lane, PAIR)], low)
        probs = jnp.exp(mm_nt(key, query) * scale - lse_ref[index])
        grad_probs = mm_nt(value, grad)
        cross = jnp.sum(grad_probs * probs, axis=0, keepdims=True)
        grad_scores = (probs * (grad_probs - cross)).astype(bf16)
        grad_value = mm(probs.astype(bf16), grad)
        grad_key = mm(grad_scores, query) * scale
        grad_query = unstacked(mm_tn(key, grad_scores).T, low, length) * scale
        pre_ref[rows, pl.ds(lane, PAIR)] = grad_query.astype(bf16)
        pre_ref[rows, pl.ds(lane + width, PAIR)] = grad_key.astype(bf16)
        pre_ref[rows, pl.ds(lane + 2 * width, PAIR)] = grad_value.astype(bf16)
        return carry

    lax.fori_loop(0, buffers * pairs, step, 0)
    for buffer in range(buffers):
        rows = slice(buffer * length, (buffer + 1) * length)
        for start, source in ((0, 0), (width, 2 * width)):
            piece = pre_ref[rows, source : source + width].astype(f32)
            bias_ref[buffer : buffer + 1, start : start + width] = jnp.sum(
                piece, axis=0, keepdims=True
            )


def attention_backward(qkv, lse, grad, buffers):
    tokens, width = grad.shape
    length = tokens // buffers
    return call(
        functools.partial(attention_back_kernel, buffers),
        "attention_backward",
        [((tokens, 3 * width), bf16), ((buffers, 2 * width), f32)],
        [VMEM] * 3,
        [VMEM] * 2,
        (qkv, lse, grad),
        10 * tokens * length * width,
        7e6,
        exps=tokens * length * width // HEAD,
    )


def weight_kernel(buffers, tile, table_ref, scale_ref, left_ref, right_ref, *refs):
    extra, (keep_ref, send_ref, right_scaled, sums) = refs[:-4], refs[-4:]
    tokens, columns = right_ref.shape
    length = tokens // buffers
    rows = keep_ref.shape[1]
    for buffer in range(buffers):
        span = slice(buffer * length, (buffer + 1) * length)
        right_scaled[span] = (right_ref[span].astype(f32) * scale_ref[buffer]).astype(bf16)

    def place(value_of, start, count):
        for spot in range(BLOCKS):
            target = keep_ref if spot < HALF else send_ref
            target[spot % HALF, :, start : start + count] = value_of(table_ref[spot]).astype(bf16)

    def rows_at(block):
        return pl.ds(pl.multiple_of(block * rows, 8), rows)

    for start in range(0, columns, tile):
        sums[...] = mm_tn(left_ref[...], right_scaled[:, start : start + tile])
        place(lambda block: sums[rows_at(block)], start, tile)
    start = columns
    for ref in extra:
        place(lambda block, ref=ref: ref[rows_at(block)], start, ref.shape[1])
        start += ref.shape[1]


def weight_gradient(name, table, scale, left, right, buffers, tile, extra=()):
    tokens, height = left.shape
    columns = right.shape[1]
    rows = height // BLOCKS
    total = columns + sum(part.shape[1] for part in extra)
    return call(
        functools.partial(weight_kernel, buffers, tile),
        name,
        [((HALF, rows, total), bf16)] * 2,
        [SMEM, SMEM] + [VMEM] * (2 + len(extra)),
        [VMEM] * 2,
        (table, scale, left, right, *extra),
        2 * tokens * height * columns,
        10e6,
        [pltpu.VMEM((tokens, columns), bf16), pltpu.VMEM((height, tile), f32)],
    )


def out_weight_kernel(buffers, scale_ref, left_ref, right_ref, small_ref, out_ref, columns_ref):
    tokens = right_ref.shape[0]
    length = tokens // buffers
    scaled = jnp.concatenate(
        [
            (
                right_ref[buffer * length : (buffer + 1) * length].astype(f32)
                * scale_ref[buffer]
            ).astype(bf16)
            for buffer in range(buffers)
        ]
    )
    out_ref[...] = mm_tn(left_ref[...], scaled)
    columns_ref[...] = small_ref[...].T


def out_weight_gradient(scale, left, right, small, buffers):
    tokens, width = left.shape
    return call(
        functools.partial(out_weight_kernel, buffers),
        "out_weight_gradient",
        [((width, width), f32), ((width, LINE), f32)],
        [SMEM] + [VMEM] * 3,
        [VMEM] * 2,
        (scale, left, right, small),
        2 * tokens * width * width,
        6e6,
    )


def states_kernel(buffers, scale_ref, res_ref, pre_ref, weight_ref, out_ref):
    tokens = res_ref.shape[0]
    length = tokens // buffers
    weight = flat(weight_ref[...])
    for buffer in range(buffers):
        rows = slice(buffer * length, (buffer + 1) * length)
        grad = res_ref[rows] + mm_nt(pre_ref[rows], weight)
        out_ref[rows] = (grad * scale_ref[buffer]).astype(bf16)


def states_gradient(scale, res, pre, weight, buffers):
    tokens, width = res.shape
    return call(
        functools.partial(states_kernel, buffers),
        "states_gradient",
        [((tokens, width), bf16)],
        [SMEM] + [VMEM] * 3,
        [VMEM],
        (scale, res, pre, weight),
        6 * tokens * width * width,
        8e6,
    )[0]


def body(
    slot_states, answer_tags, slot_mask, retrieval, query_emb, qkv_weight, qkv_bias, out_weight,
    out_bias, attn_gain, attn_shift, up_weight, up_bias, down_weight, down_bias, ffn_gain, ffn_shift,
):
    group_count = lax.axis_size(AXES)
    device_index = lax.axis_index(AXES)
    tuned = group_count == BLOCKS
    buffers, length, width = slot_states.shape
    query_count, slot_count = slot_mask.shape
    tokens = buffers * length
    x = slot_states.reshape(tokens, width)

    running = jnp.cumsum(slot_mask.reshape(-1), dtype=jnp.int32)
    slot_ranks = jnp.arange(buffers, dtype=jnp.int32) * group_count + device_index
    places = jnp.sum(
        (running[None, :] <= slot_ranks[:, None]).astype(jnp.int32), axis=1, dtype=jnp.int32
    )
    slot_pick = places[:, None] == jnp.arange(query_count * slot_count, dtype=jnp.int32)[None, :]
    owner_mask = (places // slot_count)[:, None] == jnp.arange(query_count, dtype=jnp.int32)[None]
    prior_score = jnp.sum(jnp.where(slot_pick, retrieval.reshape(-1)[None, :], 0.0), axis=1)
    tags = answer_tags.reshape(tokens, 1)

    if tuned:
        table = position_table(device_index)
        rows = qkv_weight.shape[0]
        small = jnp.concatenate(
            [
                jnp.stack([out_bias, attn_gain, attn_shift, down_bias, ffn_gain, ffn_shift], axis=1),
                qkv_bias.reshape(rows, 2),
                up_bias.reshape(rows, 4),
                query_emb.T,
            ],
            axis=1,
        )
        small = jnp.pad(small, ((0, 0), (0, LINE - small.shape[1])))
        first = gather_blocks(jnp.concatenate([qkv_weight, out_weight, small], axis=1))
        second = gather_blocks(up_weight)
        third = gather_blocks(down_weight)
        columns, small_rows = unpack_small(table, first, 4 * width)
        vectors = small_rows[:6]
        qkv_bias_all = columns[:, 6:8].reshape(-1)
        up_bias_all = columns[:, 8:12].reshape(1, -1)
        query_table = small_rows[12 : 12 + query_count]
    else:
        table = jnp.arange(BLOCKS, dtype=jnp.int32)
        everything = lambda part: lax.all_gather(part, AXES, axis=0, tiled=True).astype(f32)
        first = gather_plain(jnp.concatenate([qkv_weight, out_weight], axis=1))
        second = gather_plain(up_weight)
        third = gather_plain(down_weight)
        vectors = jnp.stack(
            [
                everything(part)
                for part in (out_bias, attn_gain, attn_shift, down_bias, ffn_gain, ffn_shift)
            ]
        )
        qkv_bias_all = everything(qkv_bias)
        up_bias_all = everything(up_bias).reshape(1, -1)
        query_table = lax.all_gather(query_emb, AXES, axis=1, tiled=True).astype(f32)
    bias = jnp.concatenate(
        [qkv_bias_all[:width], jnp.zeros((width,), f32), qkv_bias_all[width:]]
    ).reshape(1, -1)
    chosen = jnp.sum(jnp.where(owner_mask[:, :, None], query_table[None], 0.0), axis=1)

    qkv, context, lse, wqkv, wout = attention_forward(table, x, buffers, bias, first)
    hidden, normed, inverse, act, slope, wup = up_forward(
        table, x, context, wout, vectors, up_bias_all, second
    )
    mixed, like, grad_res, grad_low, gain_sums, query_sums, down_sums, wdown = down_forward(
        table, hidden, act, vectors, chosen, tags, third, buffers
    )

    scores = like[:, 0] + prior_score
    masked = jnp.where(owner_mask, scores[:, None], neg_fill)
    local_peak = jnp.max(masked, axis=0)
    local_total = jnp.sum(jnp.where(owner_mask, jnp.exp(masked - local_peak[None, :]), 0.0), axis=0)
    merged = merge_all((local_peak, local_total), tuned)
    totals = merged[0] + jnp.log(merged[1])
    loss = -jnp.sum(totals)
    scale = jnp.sum(
        jnp.where(owner_mask, jnp.exp(scores[:, None] - totals[None, :]), 0.0), axis=1
    )

    grad_up, up_sums = up_backward(grad_low, wdown, slope, buffers)
    grad_hidden, grad_attn, grad_context, attn_sums, out_sums = hidden_backward(
        grad_res, grad_up, wup, normed, inverse, vectors, wout, buffers
    )
    grad_pre, pre_sums = attention_backward(qkv, lse, grad_context, buffers)

    scatter = scatter_blocks if tuned else scatter_plain
    down_part = scatter(
        *weight_gradient("down_gradient", table, scale, act, grad_low, buffers, width)
    )
    up_part = scatter(
        *weight_gradient("up_gradient", table, scale, hidden, grad_up, buffers, width)
    )
    weigh = lambda sums: jnp.sum(scale[:, None] * sums, axis=0)
    six = [
        weigh(out_sums),
        weigh(attn_sums[:buffers]),
        weigh(attn_sums[buffers:]),
        weigh(down_sums),
        weigh(gain_sums[:buffers]),
        weigh(gain_sums[buffers:]),
    ]
    qkv_bias_sum = weigh(pre_sums)
    up_bias_sum = weigh(up_sums)
    weighed = jnp.where(owner_mask, scale[:, None], 0.0)
    query_sum = jnp.sum(weighed[:, :, None] * query_sums[:, None, :], axis=0)
    if tuned:
        small = jnp.concatenate(
            [
                jnp.stack(six),
                qkv_bias_sum.reshape(width, 2).T,
                up_bias_sum.reshape(width, 4).T,
                query_sum,
            ]
        )
        small = jnp.pad(small, ((0, LINE - small.shape[0]), (0, 0)))
    else:
        small = jnp.zeros((LINE, width), f32)
    grad_out, small = out_weight_gradient(scale, context, grad_attn, small, buffers)
    first = scatter(
        *weight_gradient(
            "qkv_gradient", table, scale, x, grad_pre, buffers, width, (grad_out, small)
        )
    )
    states = states_gradient(scale, grad_hidden, grad_pre, wqkv, buffers)
    if tuned:
        small = first[:, 4 * width :]
        six = [small[:, k] for k in range(6)]
        qkv_bias_sum = small[:, 6:8].reshape(-1)
        up_bias_sum = small[:, 8:12].reshape(-1)
        query_sum = small[:, 12 : 12 + query_count].T
    else:
        mine = lambda part: lax.psum_scatter(part, AXES, scatter_dimension=0, tiled=True)
        six = [mine(part) for part in six]
        qkv_bias_sum = mine(qkv_bias_sum)
        up_bias_sum = mine(up_bias_sum)
        query_sum = lax.psum_scatter(query_sum, AXES, scatter_dimension=1, tiled=True)
    return (
        mixed.reshape(slot_states.shape),
        loss,
        states.reshape(slot_states.shape),
        query_sum,
        first[:, : 3 * width],
        qkv_bias_sum,
        first[:, 3 * width : 4 * width],
        six[0],
        six[1],
        six[2],
        up_part,
        up_bias_sum,
        down_part,
        six[3],
        six[4],
        six[5],
    )


def solution(mesh):
    split = P(AXES)
    in_specs = (split, split, P(), P(), P(None, AXES)) + (split,) * 12
    out_specs = (split, P(), split, P(None, AXES)) + (split,) * 12
    return jax.shard_map(body, mesh=mesh, in_specs=in_specs, out_specs=out_specs, check_vma=False)
```

time: 928 us -> 329 us (0.35)
  waiting for transfers between devices: 466 us -> 136 us
  blocking collectives: 191 us -> 0 us
  matrix products: 115 us -> 0 us
  Pallas kernels: 0 us -> 95.1 us
  other arithmetic: 78.2 us -> 20.9 us
  starting transfers between devices: 0.72 us -> 40.6 us
  local copies, waits for them, and re-layouts: 53.6 us -> 27.9 us
  between operations: 16.8 us -> 3.71 us
    reduce_scatter x3 -> x0, waiting for transfers between devices: 283 us -> none  [the longest x1 142 us: body(): lax.psum_scatter(grad_down_weight, ('dp', 'fsdp'), scatter_dimension=0, t...]
    ppermute x0 -> x38, waiting for transfers between devices: none -> 136 us  [exchange(): return lax.ppermute(value, AXES, pairs)]
    unnamed x3 -> x0, blocking collectives: 124 us -> none
    dot_general x22 -> x0, matrix products: 109 us -> none  [the longest x1 10.3 us: body(): jnp.einsum('bld,fd->blf', grad_down_low, down_full, preferred_element_typ...]
    unnamed x9 -> x0, waiting for transfers between devices: 106 us -> none
    pallas_call x0 -> x12, Pallas kernels: none -> 95.1 us  [call(): pl.pallas_call(kernel, out_shape=[jax.ShapeDtypeStruct(shape, dtype) for...]
    all_gather x4 -> x0, waiting for transfers between devices: 76.7 us -> none  [the longest x1 39.2 us: body(): lax.all_gather(up_weight, ('dp', 'fsdp'), axis=0, tiled=True)]
    all_gather x1 -> x0, blocking collectives: 66.6 us -> none  [body(): lax.all_gather(query_emb, ('dp', 'fsdp'), axis=1, tiled=True)]
  transfers between devices with their start and end apart: 8 -> 38, of which waited for: 5 -> 20; matrix products, arithmetic and copies ran while one was open for 15% -> 8% of each run, Pallas kernels for 0% -> 24%
where the time goes in v2:
time: 329 us; the launch traced here: 325 us
  waiting for transfers between devices  136 us (41%)
  Pallas kernels  95.1 us (29%)
  starting transfers between devices  40.6 us (12%)
  local copies, waits for them, and re-layouts  27.9 us (8%)
  other arithmetic  20.9 us (6%)
  between operations  3.71 us (1%)
    ppermute x38, waiting for transfers between devices, exchange(): return lax.ppermute(value, AXES, pairs)  136 us
    pallas_call x12, Pallas kernels, call(): pl.pallas_call(kernel, out_shape=[jax.ShapeDtypeStruct(shape, dtype) for...  95.1 us
    ppermute x38, starting transfers between devices, exchange(): return lax.ppermute(value, AXES, pairs)  40.6 us
    convert_element_type x12, other arithmetic, add_low(): return (first.astype(f32) + second.astype(f32)).astype(bf16)  12.2 us
    unnamed x58, local copies, waits for them, and re-layouts  11.1 us
  transfers between devices with their start and end apart: 38, of which 20 were waited for; matrix products, arithmetic and copies ran while one was open for 8% of the time, Pallas kernels for 24%

profile of v2, /device:TPU:0, one launch (start us, length us, event | category | flops | bytes accessed | tf_op | source)
XLA Modules:
  0.0 324.7 jit_solution(17168053234920589718)
XLA Ops:
  8.5 4.1 %collective-permute-start = (bf16[1,24,3200]{2,1,0:T(8,128)(2,1)S(1)}, bf16[1,24,3200]{2,1,0:T(8,128)(2,1)S(1)}, u32[]{:S(2)}, u32[]{:S(2)}) collective-permute-start(bf16[1,24,3200]{2,1,0:T(8,128)(2,1)S(1)} %fusion.2), channel_id=1, source_target_pairs={{0,4},{1,5},{2,6},{3,7},{4,0},{5,1},{6,2},{7,3},{8,12},{9,13},{10,... | collective-permute-start | bytes 460808 | tf_op jit(solution)/shard_map/ppermute | solution.py:48
  15.5 11.5 %collective-permute-done = bf16[1,24,3200]{2,1,0:T(8,128)(2,1)S(1)} collective-permute-done((bf16[1,24,3200]{2,1,0:T(8,128)(2,1)S(1)}, bf16[1,24,3200]{2,1,0:T(8,128)(2,1)S(1)}, u32[]{:S(2)}, u32[]{:S(2)}) %collective-permute-start) | collective-permute-done | bytes 153632 | tf_op jit(solution)/shard_map/ppermute | solution.py:48
  31.3 7.9 %collective-permute-done.1 = bf16[2,24,3200]{2,1,0:T(8,128)(2,1)S(1)} collective-permute-done((bf16[2,24,3200]{2,1,0:T(8,128)(2,1)S(1)}, bf16[2,24,3200]{2,1,0:T(8,128)(2,1)S(1)}, u32[]{:S(2)}, u32[]{:S(2)}) %collective-permute-start.1) | collective-permute-done | bytes 307232 | tf_op jit(solution)/shard_map/ppermute | solution.py:48
  41.0 4.5 %collective-permute-done.7 = bf16[2,24,3072]{2,1,0:T(8,128)(2,1)S(1)} collective-permute-done((bf16[2,24,3072]{2,1,0:T(8,128)(2,1)S(1)}, bf16[2,24,3072]{2,1,0:T(8,128)(2,1)S(1)}, u32[]{:S(2)}, u32[]{:S(2)}) %collective-permute-start.7) | collective-permute-done | bytes 294944 | tf_op jit(solution)/shard_map/ppermute | solution.py:48
  53.4 6.8 %collective-permute-done.8 = bf16[4,24,3072]{2,1,0:T(8,128)(2,1)S(1)} collective-permute-done((bf16[4,24,3072]{2,1,0:T(8,128)(2,1)S(1)}, bf16[4,24,3072]{2,1,0:T(8,128)(2,1)S(1)}, u32[]{:S(2)}, u32[]{:S(2)}) %collective-permute-start.8) | collective-permute-done | bytes 589856 | tf_op jit(solution)/shard_map/ppermute | solution.py:48
  63.0 9.8 %collective-permute-done.14 = bf16[4,96,768]{2,1,0:T(8,128)(2,1)S(1)} collective-permute-done((bf16[4,96,768]{2,1,0:T(8,128)(2,1)S(1)}, bf16[4,96,768]{2,1,0:T(8,128)(2,1)S(1)}, u32[]{:S(2)}, u32[]{:S(2)}) %collective-permute-start.14) | collective-permute-done | bytes 589856 | tf_op jit(solution)/shard_map/ppermute | solution.py:48
  76.8 10.2 %collective-permute-done.9.p1 = bf16[8,24,3072]{2,1,0:T(8,128)(2,1)} collective-permute-done((bf16[8,24,3072]{2,1,0:T(8,128)(2,1)}, bf16[8,24,3072]{2,1,0:T(8,128)(2,1)}, u32[]{:S(2)}, u32[]{:S(2)}) %collective-permute-start.9) | collective-permute-done | bytes 1179680 | tf_op jit(solution)/shard_map/ppermute | solution.py:48
  88.7 10.9 %collective-permute-done.15.p1 = bf16[8,96,768]{2,1,0:T(8,128)(2,1)} collective-permute-done((bf16[8,96,768]{2,1,0:T(8,128)(2,1)}, bf16[8,96,768]{2,1,0:T(8,128)(2,1)}, u32[]{:S(2)}, u32[]{:S(2)}) %collective-permute-start.15) | collective-permute-done | bytes 1179680 | tf_op jit(solution)/shard_map/ppermute | solution.py:48
  106.2 17.6 %attention_forward.1 = (bf16[576,2304]{1,0:T(8,128)(2,1)}, bf16[576,768]{1,0:T(8,128)(2,1)S(1)}, f32[12,1,576]{2,1,0:T(1,128)S(1)}, bf16[32,24,2304]{2,1,0:T(8,128)(2,1)}, bf16[32,24,768]{2,1,0:T(8,128)(2,1)S(1)}) custom-call(s32[32]{0:T(128)S(1)} %fusion.14.table_ref, bf16[576,768]{1,0:T(8,128)(2,1)S(1)} %bitcast.179, f32[1,2304]{1,0:T(1,128)S(1)} %reshape.201.bias_ref, ...), custom_call_target="tpu_custom_call" | custom-call | flops 2548039680 | bytes 20000000 | tf_op jit(solution)/shard_map/attention_forward/pallas_call | solution.py:101
  123.9 14.7 %up_forward.1 = (bf16[576,768]{1,0:T(8,128)(2,1)S(1)}, f32[576,768]{1,0:T(8,128)}, f32[576,1]{1,0:T(8,128)S(1)}, bf16[576,3072]{1,0:T(8,128)(2,1)}, bf16[576,307...) custom-call(s32[32]{0:T(128)S(1)} %fusion.14.table_ref, bf16[576,768]{1,0:T(8,128)(2,1)S(1)} %bitcast.180, ...), custom_call_target="tpu_custom_call" | custom-call | flops 3397386240 | bytes 20000000 | tf_op jit(solution)/shard_map/up_forward/pallas_call | solution.py:101
  138.6 10.5 %down_forward.1 = (bf16[576,768]{1,0:T(8,128)(2,1)}, f32[2,128]{1,0:T(2,128)S(1)}, f32[576,768]{1,0:T(8,128)S(1)}, bf16[576,768]{1,0:T(8,128)(2,1)S(1)}, f32[4,7...) custom-call(s32[32]{0:T(128)S(1)} %fusion.14.table_ref, ...), custom_call_target="tpu_custom_call" | custom-call | flops 2717908992 | bytes 20000000 | tf_op jit(solution)/shard_map/down_forward/pallas_call | solution.py:101
  156.1 6.5 %up_backward.1 = (bf16[576,3072]{1,0:T(8,128)(2,1)S(1)}, f32[2,3072]{1,0:T(2,128)S(1)}) custom-call(bf16[576,768]{1,0:T(8,128)(2,1)S(1)} %get-tuple-element.63.low_ref.right_ref, bf16[32,96,768]{2,1,0:T(8,128)(2,1)} %get-tuple-element.64.wdown_ref, bf16[576,3072]{1,0:T(8,128)(2,1)S(1)} %copy-done.17), custom_call_target="tpu_custom_call" | custom-call | flops 2717908992 | bytes 13000000 | tf_op jit(solution)/shard_map/up_backward/pallas_call | solution.py:101
  164.5 9.2 %hidden_backward.1 = (f32[576,768]{1,0:T(8,128)S(1)}, bf16[576,768]{1,0:T(8,128)(2,1)S(1)}, bf16[576,768]{1,0:T(8,128)(2,1)S(1)}, f32[4,768]{1,0:T(4,128)S(1)}, f32[2,768]{1,0:T(2,128)S(1)}) custom-call(f32[576,768]{1,0:T(8,128)S(1)} %get-tuple-element.62.res_ref, bf16[576,3072]{1,0:T(8,128)(2,1)} %copy-done.1, ...), custom_call_target="tpu_custom_call" | custom-call | flops 3397386240 | bytes 18000000 | tf_op jit(solution)/shard_map/hidden_backward/pallas_call | solution.py:101
  175.0 4.1 %collective-permute-start.22 = (f32[2,8]{1,0:T(2,128)S(1)}, f32[2,8]{1,0:T(2,128)S(1)}, u32[]{:S(2)}, u32[]{:S(2)}) collective-permute-start(f32[2,8]{1,0:T(2,128)S(1)} %pad_maximum_fusion.14), channel_id=1, source_target_pairs={{0,4},{1,5},{2,6},{3,7},{4,0},{5,1},{6,2},{7,3},{8,12},{9,13},{10,... | collective-permute-start | bytes 200 | tf_op jit(solution)/shard_map/ppermute | solution.py:48
  179.1 10.2 %attention_backward.1 = (bf16[576,2304]{1,0:T(8,128)(2,1)S(1)}, f32[2,1536]{1,0:T(2,128)S(1)}) custom-call(bf16[576,2304]{1,0:T(8,128)(2,1)S(1)} %copy-done.20, f32[12,1,576]{2,1,0:T(1,128)S(1)} %get-tuple-element.72.lse_ref, bf16[576,768]{1,0:T(8,128)(2,1)S(1)} %get-tuple-element.73.grad_ref), custom_call_target="tpu_custom_call" | custom-call | flops 1274019840 | bytes 7000000 | tf_op jit(solution)/shard_map/attention_backward/pallas_call | solution.py:101
  191.1 6.4 %down_gradient.1 = (bf16[16,96,768]{2,1,0:T(8,128)(2,1)S(1)}, bf16[16,96,768]{2,1,0:T(8,128)(2,1)}) custom-call(s32[32]{0:T(128)S(1)} %fusion.14.table_ref, f32[2]{0:T(128)S(1)} %select_reduce_fusion.2.scale_ref, bf16[576,3072]{1,0:T(8,128)(2,1)S(1)} %copy-done.14, bf16[576,768]{1,0:T(8,128)(2,1)S(1)} %copy-done.19), custom_call_target="tpu_custom_call" | custom-call | flops 2717908992 | bytes 10000000 | tf_op jit(solution)/shard_map/down_gradient/pallas_call | solution.py:101
  199.1 6.1 %up_gradient.1 = (bf16[16,24,3072]{2,1,0:T(8,128)(2,1)S(1)}, bf16[16,24,3072]{2,1,0:T(8,128)(2,1)}) custom-call(s32[32]{0:T(128)S(1)} %fusion.14.table_ref, f32[2]{0:T(128)S(1)} %select_reduce_fusion.2.scale_ref, bf16[576,768]{1,0:T(8,128)(2,1)S(1)} %get-tuple-element.58.hidden_ref.left_ref, bf16[576,3072]{1,0:T(8,128)(2,1)S(1)} %copy-done.2), custom_call_target="tpu_custom_call" | custom-call | flops 2717908992 | bytes 10000000 | tf_op jit(solution)/shard_map/up_gradient/pallas_call | solution.py:101
  210.9 6.6 %qkv_gradient.1 = (bf16[16,24,3200]{2,1,0:T(8,128)(2,1)S(1)}, bf16[16,24,3200]{2,1,0:T(8,128)(2,1)}) custom-call(s32[32]{0:T(128)S(1)} %fusion.14.table_ref, f32[2]{0:T(128)S(1)} %select_reduce_fusion.2.scale_ref, bf16[576,768]{1,0:T(8,128)(2,1)S(1)} %bitcast.181, bf16[576,2304]{1,0:T(8,128)(2,1)} %copy-done.3, f32[768,768]{1,0:T(8,128)S(1)} %get-tuple-element.84.refs_0_, ...), custom_call_target="tpu_custom_call" | custom-call | flops 2038431744 | bytes 10000000 | tf_op jit(solution)/shard_map/qkv_gradient/pallas_call | solution.py:101
  242.7 15.8 %collective-permute-done.29 = bf16[8,24,3072]{2,1,0:T(8,128)(2,1)} collective-permute-done((bf16[8,24,3072]{2,1,0:T(8,128)(2,1)}, bf16[8,24,3072]{2,1,0:T(8,128)(2,1)}, u32[]{:S(2)}, u32[]{:S(2)}) %collective-permute-start.29) | collective-permute-done | bytes 1179680 | tf_op jit(solution)/shard_map/ppermute | solution.py:48
  261.8 16.1 %collective-permute-done.24 = bf16[8,24,3200]{2,1,0:T(8,128)(2,1)S(1)} collective-permute-done((bf16[8,24,3200]{2,1,0:T(8,128)(2,1)S(1)}, bf16[8,24,3200]{2,1,0:T(8,128)(2,1)S(1)}, u32[]{:S(2)}, u32[]{:S(2)}) %collective-permute-start.24) | collective-permute-done | bytes 1228832 | tf_op jit(solution)/shard_map/ppermute | solution.py:48
  282.3 6.1 %collective-permute-done.25 = bf16[4,24,3200]{2,1,0:T(8,128)(2,1)S(1)} collective-permute-done((bf16[4,24,3200]{2,1,0:T(8,128)(2,1)S(1)}, bf16[4,24,3200]{2,1,0:T(8,128)(2,1)S(1)}, u32[]{:S(2)}, u32[]{:S(2)}) %collective-permute-start.25) | collective-permute-done | bytes 614432 | tf_op jit(solution)/shard_map/ppermute | solution.py:48
  288.7 10.7 %collective-permute-done.31 = bf16[2,24,3072]{2,1,0:T(8,128)(2,1)S(1)} collective-permute-done((bf16[2,24,3072]{2,1,0:T(8,128)(2,1)S(1)}, bf16[2,24,3072]{2,1,0:T(8,128)(2,1)S(1)}, u32[]{:S(2)}, u32[]{:S(2)}) %collective-permute-start.31) | collective-permute-done | bytes 294944 | tf_op jit(solution)/shard_map/ppermute | solution.py:48
  302.7 8.1 %collective-permute-done.32 = bf16[1,24,3072]{2,1,0:T(8,128)(2,1)S(1)} collective-permute-done((bf16[1,24,3072]{2,1,0:T(8,128)(2,1)S(1)}, bf16[1,24,3072]{2,1,0:T(8,128)(2,1)S(1)}, u32[]{:S(2)}, u32[]{:S(2)}) %collective-permute-start.32) | collective-permute-done | bytes 147488 | tf_op jit(solution)/shard_map/ppermute | solution.py:48
  313.2 5.7 %collective-permute-done.27 = bf16[1,24,3200]{2,1,0:T(8,128)(2,1)S(1)} collective-permute-done((bf16[1,24,3200]{2,1,0:T(8,128)(2,1)S(1)}, bf16[1,24,3200]{2,1,0:T(8,128)(2,1)S(1)}, u32[]{:S(2)}, u32[]{:S(2)}) %collective-permute-start.27) | collective-permute-done | bytes 153632 | tf_op jit(solution)/shard_map/ppermute | solution.py:48
  (231 shorter events, 100.8 us)
Async XLA Ops:
  8.5 18.5 %collective-permute-start = (bf16[1,24,3200]{2,1,0:T(8,128)(2,1)S(1)}, bf16[1,24,3200]{2,1,0:T(8,128)(2,1)S(1)}, u32[]{:S(2)}, u32[]{:S(2)}) collective-permute-start(bf16[1,24,3200]{2,1,0:T(8,128)(2,1)S(1)} %fusion.2), channel_id=1, source_target_pairs={{0,4},{1,5},{2,6},{3,7},{4,0},{5,1},{6,2},{7,3},{8,12},{9,13},{10,... | collective-permute-start | bytes 460808 | tf_op jit(solution)/shard_map/ppermute | solution.py:48
  12.6 17.7 %collective-permute-start.6 = (bf16[1,24,3072]{2,1,0:T(8,128)(2,1)}, bf16[1,24,3072]{2,1,0:T(8,128)(2,1)S(1)}, u32[]{:S(2)}, u32[]{:S(2)}) collective-permute-start(bf16[1,24,3072]{2,1,0:T(8,128)(2,1)} %bitcast.182), channel_id=1, source_target_pairs={{0,4},{1,5},{2,6},{3,7},{4,0},{5,1},{6,2},{7,3},{8,12},{9,13},{10,... | collective-permute-start | bytes 442376 | tf_op jit(solution)/shard_map/ppermute | solution.py:48
  12.7 28.2 %collective-permute-start.12 = (bf16[1,96,768]{2,1,0:T(8,128)(2,1)}, bf16[1,96,768]{2,1,0:T(8,128)(2,1)S(1)}, u32[]{:S(2)}, u32[]{:S(2)}) collective-permute-start(bf16[1,96,768]{2,1,0:T(8,128)(2,1)} %bitcast.186), channel_id=1, source_target_pairs={{0,4},{1,5},{2,6},{3,7},{4,0},{5,1},{6,2},{7,3},{8,12},{9,13},{10,... | collective-permute-start | bytes 442376 | tf_op jit(solution)/shard_map/ppermute | solution.py:48
  49.6 26.0 %collective-permute-start.3 = (bf16[8,24,3200]{2,1,0:T(8,128)(2,1)S(1)}, bf16[8,24,3200]{2,1,0:T(8,128)(2,1)S(1)}, u32[]{:S(2)}, u32[]{:S(2)}) collective-permute-start(bf16[8,24,3200]{2,1,0:T(8,128)(2,1)S(1)} %pad_maximum_fusion.p0), channel_id=1, source_target_pairs={{0,1},{1,0},{2,3},{3,2},{4,5},{5,4},{6,7},{7,6},{8,24},{9,25},{10,... | collective-permute-start | bytes 3686408 | tf_op jit(solution)/shard_map/ppermute | solution.py:48
  51.8 21.0 %collective-permute-start.14 = (bf16[4,96,768]{2,1,0:T(8,128)(2,1)S(1)}, bf16[4,96,768]{2,1,0:T(8,128)(2,1)S(1)}, u32[]{:S(2)}, u32[]{:S(2)}) collective-permute-start(bf16[4,96,768]{2,1,0:T(8,128)(2,1)S(1)} %pad_maximum_fusion.5), channel_id=1, source_target_pairs={{0,16},{1,17},{2,18},{3,19},{4,20},{5,21},{6,22},{7,23},{8,9},{9,8... | collective-permute-start | bytes 1769480 | tf_op jit(solution)/shard_map/ppermute | solution.py:48
  61.4 25.6 %collective-permute-start.9 = (bf16[8,24,3072]{2,1,0:T(8,128)(2,1)}, bf16[8,24,3072]{2,1,0:T(8,128)(2,1)}, u32[]{:S(2)}, u32[]{:S(2)}) collective-permute-start(bf16[8,24,3072]{2,1,0:T(8,128)(2,1)} %pad_maximum_fusion.1.p0), channel_id=1, source_target_pairs={{0,1},{1,0},{2,3},{3,2},{4,5},{5,4},{6,7},{7,6},{8,24},{9,25},{10,... | collective-permute-start | bytes 3538952 | tf_op jit(solution)/shard_map/ppermute | solution.py:48
  63.0 37.5 %collective-permute-start.4 = (bf16[8,24,3200]{2,1,0:T(8,128)(2,1)S(1)}, bf16[8,24,3200]{2,1,0:T(8,128)(2,1)}, u32[]{:S(2)}, u32[]{:S(2)}) collective-permute-start(bf16[8,24,3200]{2,1,0:T(8,128)(2,1)S(1)} %pad_maximum_fusion.p0), channel_id=1, source_target_pairs={{0,8},{1,9},{2,10},{3,11},{4,12},{5,13},{6,14},{7,15},{8,0},{9,1},... | collective-permute-start | bytes 3686408 | tf_op jit(solution)/shard_map/ppermute | solution.py:48
  74.0 25.6 %collective-permute-start.15 = (bf16[8,96,768]{2,1,0:T(8,128)(2,1)}, bf16[8,96,768]{2,1,0:T(8,128)(2,1)}, u32[]{:S(2)}, u32[]{:S(2)}) collective-permute-start(bf16[8,96,768]{2,1,0:T(8,128)(2,1)} %pad_maximum_fusion.2.p0), channel_id=1, source_target_pairs={{0,1},{1,0},{2,3},{3,2},{4,5},{5,4},{6,7},{7,6},{8,24},{9,25},{10,... | collective-permute-start | bytes 3538952 | tf_op jit(solution)/shard_map/ppermute | solution.py:48
  75.6 25.0 %collective-permute-start.5 = (bf16[8,24,3200]{2,1,0:T(8,128)(2,1)S(1)}, bf16[8,24,3200]{2,1,0:T(8,128)(2,1)}, u32[]{:S(2)}, u32[]{:S(2)}) collective-permute-start(bf16[8,24,3200]{2,1,0:T(8,128)(2,1)S(1)} %collective-permute-done.3.p1), channel_id=1, source_target_pairs={{0,8},{1,9},{2,10},{3,11},{4,12},{5,13},{6,14},{7,15},{8,0},{9,1},... | collective-permute-start | bytes 3686408 | tf_op jit(solution)/shard_map/ppermute | solution.py:48
  76.2 47.6 %collective-permute-start.10 = (bf16[8,24,3072]{2,1,0:T(8,128)(2,1)}, bf16[8,24,3072]{2,1,0:T(8,128)(2,1)}, u32[]{:S(2)}, u32[]{:S(2)}) collective-permute-start(bf16[8,24,3072]{2,1,0:T(8,128)(2,1)} %pad_maximum_fusion.1.p0), channel_id=1, source_target_pairs={{0,8},{1,9},{2,10},{3,11},{4,12},{5,13},{6,14},{7,15},{8,0},{9,1},... | collective-permute-start | bytes 3538952 | tf_op jit(solution)/shard_map/ppermute | solution.py:48
  87.0 36.9 %collective-permute-start.11 = (bf16[8,24,3072]{2,1,0:T(8,128)(2,1)}, bf16[8,24,3072]{2,1,0:T(8,128)(2,1)}, u32[]{:S(2)}, u32[]{:S(2)}) collective-permute-start(bf16[8,24,3072]{2,1,0:T(8,128)(2,1)} %collective-permute-done.9.p1), channel_id=1, source_target_pairs={{0,8},{1,9},{2,10},{3,11},{4,12},{5,13},{6,14},{7,15},{8,0},{9,1},... | collective-permute-start | bytes 3538952 | tf_op jit(solution)/shard_map/ppermute | solution.py:48
  99.6 38.9 %collective-permute-start.16 = (bf16[8,96,768]{2,1,0:T(8,128)(2,1)}, bf16[8,96,768]{2,1,0:T(8,128)(2,1)}, u32[]{:S(2)}, u32[]{:S(2)}) collective-permute-start(bf16[8,96,768]{2,1,0:T(8,128)(2,1)} %pad_maximum_fusion.2.p0), channel_id=1, source_target_pairs={{0,8},{1,9},{2,10},{3,11},{4,12},{5,13},{6,14},{7,15},{8,0},{9,1},... | collective-permute-start | bytes 3538952 | tf_op jit(solution)/shard_map/ppermute | solution.py:48
  100.5 38.1 %collective-permute-start.17 = (bf16[8,96,768]{2,1,0:T(8,128)(2,1)}, bf16[8,96,768]{2,1,0:T(8,128)(2,1)}, u32[]{:S(2)}, u32[]{:S(2)}) collective-permute-start(bf16[8,96,768]{2,1,0:T(8,128)(2,1)} %collective-permute-done.15.p1), channel_id=1, source_target_pairs={{0,8},{1,9},{2,10},{3,11},{4,12},{5,13},{6,14},{7,15},{8,0},{9,1},... | collective-permute-start | bytes 3538952 | tf_op jit(solution)/shard_map/ppermute | solution.py:48
  175.0 15.9 %collective-permute-start.22 = (f32[2,8]{1,0:T(2,128)S(1)}, f32[2,8]{1,0:T(2,128)S(1)}, u32[]{:S(2)}, u32[]{:S(2)}) collective-permute-start(f32[2,8]{1,0:T(2,128)S(1)} %pad_maximum_fusion.14), channel_id=1, source_target_pairs={{0,4},{1,5},{2,6},{3,7},{4,0},{5,1},{6,2},{7,3},{8,12},{9,13},{10,... | collective-permute-start | bytes 200 | tf_op jit(solution)/shard_map/ppermute | solution.py:48
  199.1 19.7 %collective-permute-start.33 = (bf16[16,96,768]{2,1,0:T(8,128)(2,1)}, bf16[16,96,768]{2,1,0:T(8,128)(2,1)}, u32[]{:S(2)}, u32[]{:S(2)}) collective-permute-start(bf16[16,96,768]{2,1,0:T(8,128)(2,1)} %get-tuple-element.91), channel_id=1, source_target_pairs={{0,8},{1,9},{2,10},{3,11},{4,12},{5,13},{6,14},{7,15},{8,0},{9,1},... | collective-permute-start | bytes 7077896 | tf_op jit(solution)/shard_map/ppermute | solution.py:48
  206.6 16.9 %collective-permute-start.28 = (bf16[16,24,3072]{2,1,0:T(8,128)(2,1)}, bf16[16,24,3072]{2,1,0:T(8,128)(2,1)}, u32[]{:S(2)}, u32[]{:S(2)}) collective-permute-start(bf16[16,24,3072]{2,1,0:T(8,128)(2,1)} %get-tuple-element.89), channel_id=1, source_target_pairs={{0,8},{1,9},{2,10},{3,11},{4,12},{5,13},{6,14},{7,15},{8,0},{9,1},... | collective-permute-start | bytes 7077896 | tf_op jit(solution)/shard_map/ppermute | solution.py:48
  223.0 16.5 %collective-permute-start.34 = (bf16[8,96,768]{2,1,0:T(8,128)(2,1)}, bf16[8,96,768]{2,1,0:T(8,128)(2,1)}, u32[]{:S(2)}, u32[]{:S(2)}) collective-permute-start(bf16[8,96,768]{2,1,0:T(8,128)(2,1)} %slice.266), channel_id=1, source_target_pairs={{0,1},{1,0},{2,3},{3,2},{4,5},{5,4},{6,7},{7,6},{8,24},{9,25},{10,... | collective-permute-start | bytes 3538952 | tf_op jit(solution)/shard_map/ppermute | solution.py:48
  227.6 30.9 %collective-permute-start.29 = (bf16[8,24,3072]{2,1,0:T(8,128)(2,1)}, bf16[8,24,3072]{2,1,0:T(8,128)(2,1)}, u32[]{:S(2)}, u32[]{:S(2)}) collective-permute-start(bf16[8,24,3072]{2,1,0:T(8,128)(2,1)} %slice.257), channel_id=1, source_target_pairs={{0,1},{1,0},{2,3},{3,2},{4,5},{5,4},{6,7},{7,6},{8,24},{9,25},{10,... | collective-permute-start | bytes 3538952 | tf_op jit(solution)/shard_map/ppermute | solution.py:48
  231.3 46.5 %collective-permute-start.24 = (bf16[8,24,3200]{2,1,0:T(8,128)(2,1)S(1)}, bf16[8,24,3200]{2,1,0:T(8,128)(2,1)S(1)}, u32[]{:S(2)}, u32[]{:S(2)}) collective-permute-start(bf16[8,24,3200]{2,1,0:T(8,128)(2,1)S(1)} %slice.242), channel_id=1, source_target_pairs={{0,1},{1,0},{2,3},{3,2},{4,5},{5,4},{6,7},{7,6},{8,24},{9,25},{10,... | collective-permute-start | bytes 3686408 | tf_op jit(solution)/shard_map/ppermute | solution.py:48
  241.1 38.6 %collective-permute-start.35 = (bf16[4,96,768]{2,1,0:T(8,128)(2,1)S(1)}, bf16[4,96,768]{2,1,0:T(8,128)(2,1)S(1)}, u32[]{:S(2)}, u32[]{:S(2)}) collective-permute-start(bf16[4,96,768]{2,1,0:T(8,128)(2,1)S(1)} %slice.268), channel_id=1, source_target_pairs={{0,16},{1,17},{2,18},{3,19},{4,20},{5,21},{6,22},{7,23},{8,9},{9,8... | collective-permute-start | bytes 1769480 | tf_op jit(solution)/shard_map/ppermute | solution.py:48
  260.2 19.8 %collective-permute-start.30 = (bf16[4,24,3072]{2,1,0:T(8,128)(2,1)S(1)}, bf16[4,24,3072]{2,1,0:T(8,128)(2,1)S(1)}, u32[]{:S(2)}, u32[]{:S(2)}) collective-permute-start(bf16[4,24,3072]{2,1,0:T(8,128)(2,1)S(1)} %slice.259), channel_id=1, source_target_pairs={{0,16},{1,17},{2,18},{3,19},{4,20},{5,21},{6,22},{7,23},{8,9},{9,8... | collective-permute-start | bytes 1769480 | tf_op jit(solution)/shard_map/ppermute | solution.py:48
  279.9 19.7 %collective-permute-start.36 = (bf16[2,96,768]{2,1,0:T(8,128)(2,1)S(1)}, bf16[2,96,768]{2,1,0:T(8,128)(2,1)S(1)}, u32[]{:S(2)}, u32[]{:S(2)}) collective-permute-start(bf16[2,96,768]{2,1,0:T(8,128)(2,1)S(1)} %slice.270), channel_id=1, source_target_pairs={{0,2},{1,3},{2,0},{3,1},{4,6},{5,7},{6,4},{7,5},{8,10},{9,11},{10,... | collective-permute-start | bytes 884744 | tf_op jit(solution)/shard_map/ppermute | solution.py:48
  280.2 19.2 %collective-permute-start.31 = (bf16[2,24,3072]{2,1,0:T(8,128)(2,1)S(1)}, bf16[2,24,3072]{2,1,0:T(8,128)(2,1)S(1)}, u32[]{:S(2)}, u32[]{:S(2)}) collective-permute-start(bf16[2,24,3072]{2,1,0:T(8,128)(2,1)S(1)} %slice.261), channel_id=1, source_target_pairs={{0,2},{1,3},{2,0},{3,1},{4,6},{5,7},{6,4},{7,5},{8,10},{9,11},{10,... | collective-permute-start | bytes 884744 | tf_op jit(solution)/shard_map/ppermute | solution.py:48
  288.6 23.0 %collective-permute-start.26 = (bf16[2,24,3200]{2,1,0:T(8,128)(2,1)S(1)}, bf16[2,24,3200]{2,1,0:T(8,128)(2,1)S(1)}, u32[]{:S(2)}, u32[]{:S(2)}) collective-permute-start(bf16[2,24,3200]{2,1,0:T(8,128)(2,1)S(1)} %slice.246), channel_id=1, source_target_pairs={{0,2},{1,3},{2,0},{3,1},{4,6},{5,7},{6,4},{7,5},{8,10},{9,11},{10,... | collective-permute-start | bytes 921608 | tf_op jit(solution)/shard_map/ppermute | solution.py:48
  (42 other events, 443.8 us)

commit v3 on v2

v3 whole, which is shorter than its diff:
```python
import functools
import math

import jax
import jax.numpy as jnp
import numpy as np
from jax import lax
from jax.experimental import pallas as pl
from jax.experimental.pallas import tpu as pltpu
from jax.sharding import PartitionSpec as P

HEAD = 64
PAIR = 2 * HEAD
LINE = 128
AXES = ("dp", "fsdp")
X_BIT, CORE_BIT, Z_FAR, Z_NEAR, Y_BIT = 16, 8, 4, 2, 1
BLOCKS = 32
HALF = BLOCKS // 2
SHARE = 0.02
LIMIT = 12

eps_norm = 1e-12
loss_scale = 65536.0
neg_fill = -1e30
f32 = jnp.float32
bf16 = jnp.bfloat16
VMEM = pl.BlockSpec(memory_space=pltpu.VMEM)
SMEM = pl.BlockSpec(memory_space=pltpu.SMEM)
HBM = pl.BlockSpec(memory_space=pltpu.HBM)


def device_offsets(first, second):
    masks = (Z_FAR, Z_NEAR, first, second)
    return np.array(
        [sum(m for k, m in enumerate(masks) if p >> k & 1) for p in range(HALF)], np.int32
    )


def position_table(device_index):
    even = device_offsets(X_BIT, Y_BIT)
    odd = device_offsets(Y_BIT, X_BIT)
    table_even = jnp.asarray(np.concatenate([even, odd ^ CORE_BIT]))
    table_odd = jnp.asarray(np.concatenate([odd, even ^ CORE_BIT]))
    core = (device_index // CORE_BIT) % 2
    return jnp.where(core == 0, table_even, table_odd) ^ device_index


def exchange(value, even_mask, odd_mask):
    pairs = [(i, i ^ (odd_mask if i & CORE_BIT else even_mask)) for i in range(BLOCKS)]
    return lax.ppermute(value, AXES, pairs)


def after(value, *earlier):
    return lax.optimization_barrier((value, *earlier))[0]


SIDE, OTHER, CORES = (X_BIT, Y_BIT), (Y_BIT, X_BIT), (CORE_BIT, CORE_BIT)
LINE_MASKS = (Z_FAR, Z_NEAR, Z_FAR | Z_NEAR)


class Order:
    def __init__(self, tuned):
        self.tuned, self.last = tuned, None

    def place(self, value):
        if self.tuned and self.last is not None:
            return after(value, self.last)
        return value

    def mark(self, value):
        self.last = value


class Gather:
    def __init__(self, order, held):
        self.order, self.held = order, held

    def start_line(self, *earlier):
        own = after(self.held, *earlier) if earlier else self.held
        self.got = [exchange(own, mask, mask) for mask in LINE_MASKS]

    def start(self, masks, *earlier):
        self.got = [exchange(after(self.held, *earlier) if earlier else self.held, *masks)]

    def join(self):
        got = [self.order.place(part) for part in self.got]
        self.held = jnp.concatenate([self.held, *got])
        self.order.mark(self.held)

    def start_cores(self):
        self.last = self.order.place(self.got[0])
        self.order.mark(self.last)
        self.far = exchange(self.held, *CORES), exchange(self.last, *CORES)

    def pieces(self):
        far = [self.order.place(part) for part in self.far]
        self.order.mark(far[1])
        return (self.held, self.last, *far)


def gather_plain(part):
    whole = lax.all_gather(part, AXES, axis=0, tiled=True)
    blocks = whole.reshape(BLOCKS, -1, whole.shape[1])
    return tuple(blocks[8 * k : 8 * k + 8] for k in range(4))


def add_low(first, second):
    return (first.astype(f32) + second.astype(f32)).astype(bf16)


class Scatter:
    def __init__(self, order, keep, send):
        self.order, self.keep, self.send = order, keep, send

    def start(self, masks, *earlier):
        self.got = exchange(after(self.send, *earlier) if earlier else self.send, *masks)

    def join(self):
        half = self.keep.shape[0] // 2
        got = self.order.place(self.got)
        self.send = add_low(self.keep[half:], got[half:])
        self.keep = add_low(self.keep[:half], got[:half])
        self.order.mark(self.send)

    def start_line(self):
        got = self.order.place(self.got)
        sends = [add_low(self.keep[p : p + 1], got[p : p + 1]) for p in (1, 2, 3)]
        self.got = [exchange(part, mask, mask) for part, mask in zip(sends, LINE_MASKS)]
        self.keep = self.keep[0].astype(f32) + got[0].astype(f32)
        self.order.mark(sends[-1])

    def finish(self, start=0, width=None):
        end = self.keep.shape[1] if width is None else start + width
        cut = lambda part: part[..., start:end]
        got = [cut(self.order.place(part)[0]).astype(f32) for part in self.got]
        return cut(self.keep) + (got[0] + got[1] + got[2])


def scatter_plain(keep, send):
    blocks = jnp.concatenate([keep, send])
    whole = blocks.reshape(-1, blocks.shape[2])
    return lax.psum_scatter(whole, AXES, scatter_dimension=0, tiled=True).astype(f32)


def merge_parts(first, second):
    peak = jnp.maximum(first[0], second[0])
    return (peak, first[1] * jnp.exp(first[0] - peak) + second[1] * jnp.exp(second[0] - peak))


def merge_start(pair, mask):
    return exchange(jnp.stack(pair), mask, mask)


def merge_join(order, pair, got):
    got = order.place(got)
    pair = merge_parts(pair, (got[0], got[1]))
    order.mark(pair[0])
    return pair


def merge_plain(pair):
    peak = lax.pmax(pair[0], AXES)
    return (peak, lax.psum(pair[1] * jnp.exp(pair[0] - peak), AXES))


def call(
    kernel, name, outs, in_specs, out_specs, args, flops, moved, scratch=(), exps=0, limit=None
):
    args = [
        pltpu.with_memory_space_constraint(arg, pltpu.HBM) if spec is HBM else arg
        for arg, spec in zip(args, in_specs)
    ]
    return pl.pallas_call(
        kernel,
        out_shape=[
            pltpu.HBM(shape, dtype) if spec is HBM else jax.ShapeDtypeStruct(shape, dtype)
            for (shape, dtype), spec in zip(outs, out_specs)
        ],
        in_specs=in_specs,
        out_specs=out_specs,
        scratch_shapes=list(scratch),
        compiler_params=pltpu.CompilerParams(vmem_limit_bytes=(limit or LIMIT) * 2**20),
        cost_estimate=pl.CostEstimate(
            flops=int(flops * SHARE), bytes_accessed=int(moved * SHARE), transcendentals=int(exps * SHARE)
        ),
        name=name,
    )(*args)


def mm(first, second):
    return jnp.dot(first, second, preferred_element_type=f32)


def mm_nt(first, second):
    return lax.dot_general(first, second, (((1,), (1,)), ((), ())), preferred_element_type=f32)


def mm_tn(first, second):
    return lax.dot_general(first, second, (((0,), (0,)), ((), ())), preferred_element_type=f32)


def row_mean(value):
    return jnp.mean(value, axis=-1, keepdims=True)


def block_copies(table_ref, pieces, start, width, target, sems):
    copies = [
        pltpu.make_async_copy(
            pieces[spot // 8].at[spot % 8, :, pl.ds(start, width)],
            target.at[table_ref[spot]],
            sems.at[spot],
        )
        for spot in range(BLOCKS)
    ]
    for copy in copies:
        copy.start()
    return copies


def fetch(pairs, sems, first=0):
    copies = [
        pltpu.make_async_copy(source, target, sems.at[first + k])
        for k, (source, target) in enumerate(pairs)
    ]
    for copy in copies:
        copy.start()
    return copies


def wait_all(copies):
    for copy in copies:
        copy.wait()


def flat(value):
    return value.reshape(-1, value.shape[-1])


SIX, QKV_AT, UP_AT, QUERY_AT = 6, 6, 8, 12
VECTORS = 8


def pack_kernel(weight_hbm, *refs):
    sources, out_ref, parts, held_ref, sems = refs[: SIX + 3], refs[SIX + 3], refs[SIX + 4 : -2], *refs[-2:]
    rows, width = out_ref.shape[1], out_ref.shape[2] - LINE
    copies = fetch(zip(sources, parts), sems)
    copies += fetch([(weight_hbm, out_ref.at[0, :, pl.ds(0, width)])], sems, len(parts))
    vectors, (qkv_ref, up_ref, query_ref) = parts[:SIX], parts[SIX:]
    held_ref[...] = jnp.zeros_like(held_ref)
    wait_all(copies)
    for k, ref in enumerate(vectors):
        held_ref[k : k + 1, :rows] = ref[...].astype(f32)
    for at, ref, count in ((QKV_AT, qkv_ref, 2), (UP_AT, up_ref, 4)):
        value = ref[...].astype(f32)
        for c in range(count):
            held_ref[at + c : at + c + 1, :rows] = value[:, c * rows : (c + 1) * rows]
    count = query_ref.shape[0]
    held_ref[QUERY_AT : QUERY_AT + count, :rows] = query_ref[...].astype(f32)
    out_ref[0, :, width:] = held_ref[...].T[:rows].astype(bf16)


def pack_first(weight, vectors, qkv_bias, up_bias, query_emb):
    rows, width = weight.shape
    parts = [part.reshape(1, -1) for part in (*vectors, qkv_bias, up_bias)] + [query_emb]
    return call(
        pack_kernel,
        "pack_first",
        [((1, rows, width + LINE), bf16)],
        [HBM] * (1 + len(parts)),
        [VMEM],
        [weight, *parts],
        0,
        1e5,
        [pltpu.VMEM(part.shape, part.dtype) for part in parts]
        + [pltpu.VMEM((LINE, LINE), f32), pltpu.SemaphoreType.DMA((len(parts) + 1,))],
    )[0]


def unpack_kernel(
    start, count, table_ref, p0, p1, p2, p3, consts_ref, qkv_ref, up_ref,
    held_ref, qkv_wide, up_wide, sems,
):
    wait_all(block_copies(table_ref, (p0, p1, p2, p3), start, LINE, held_ref, sems))
    rows = held_ref.shape[1]
    every = flat(held_ref[...]).astype(f32)
    for block in range(BLOCKS):
        value = every[block * rows : (block + 1) * rows]
        for c in range(2):
            qkv_wide[(2 * block + c) * rows : (2 * block + c + 1) * rows] = value
        for c in range(4):
            up_wide[(4 * block + c) * rows : (4 * block + c + 1) * rows] = value
    turned = every.T
    consts_ref[:VECTORS] = turned[:VECTORS]
    consts_ref[VECTORS:] = turned[QUERY_AT : QUERY_AT + count]

    def line(wide, at, count):
        picks = lax.broadcasted_iota(jnp.int32, (8, LINE), 1) == at + lax.broadcasted_iota(
            jnp.int32, (8, LINE), 0
        )
        found = mm_nt(picks.astype(bf16), wide[...].astype(bf16))
        part = lax.broadcasted_iota(jnp.int32, found.shape, 1) // rows % count
        mine = part == lax.broadcasted_iota(jnp.int32, found.shape, 0)
        return jnp.sum(jnp.where(mine, found, 0.0), axis=0, keepdims=True)

    up_ref[...] = line(up_wide, UP_AT, 4)
    width = held_ref.shape[0] * rows
    bias = line(qkv_wide, QKV_AT, 2)
    qkv_ref[:, :width] = bias[:, :width]
    qkv_ref[:, width : 2 * width] = jnp.zeros((1, width), f32)
    qkv_ref[:, 2 * width :] = bias[:, width:]


def unpack_small(table, pieces, start, query_count):
    rows = pieces[0].shape[1]
    width = BLOCKS * rows
    return call(
        functools.partial(unpack_kernel, start, query_count),
        "unpack_small",
        [((VECTORS + query_count, width), f32), ((1, 3 * width), f32), ((1, 4 * width), f32)],
        [SMEM] + [HBM] * 4,
        [VMEM] * 3,
        (table, *pieces),
        0,
        1e6,
        [
            pltpu.VMEM((BLOCKS, rows, LINE), bf16),
            pltpu.VMEM((2 * width, LINE), f32),
            pltpu.VMEM((4 * width, LINE), f32),
            pltpu.SemaphoreType.DMA((BLOCKS,)),
        ],
    )


def split_kernel(small_ref, *refs):
    vectors, (qkv_ref, up_ref, query_ref, held_ref) = refs[:SIX], refs[SIX:]
    rows = small_ref.shape[0]
    held_ref[...] = jnp.zeros_like(held_ref)
    held_ref[:rows] = small_ref[...]
    turned = held_ref[...].T
    for k, ref in enumerate(vectors):
        ref[...] = turned[k : k + 1, :rows]
    for c in range(2):
        qkv_ref[:, c * rows : (c + 1) * rows] = turned[QKV_AT + c : QKV_AT + c + 1, :rows]
    for c in range(4):
        up_ref[:, c * rows : (c + 1) * rows] = turned[UP_AT + c : UP_AT + c + 1, :rows]
    query_ref[...] = turned[QUERY_AT : QUERY_AT + query_ref.shape[0], :rows]


def split_small(small, query_count):
    rows = small.shape[0]
    outs = call(
        split_kernel,
        "split_small",
        [((1, rows), f32)] * SIX + [((1, 2 * rows), f32), ((1, 4 * rows), f32), ((query_count, rows), f32)],
        [VMEM],
        [VMEM] * (SIX + 3),
        (small,),
        0,
        1e5,
        [pltpu.VMEM((LINE, LINE), f32)],
    )
    return [part.reshape(-1) for part in outs[:-1]] + [outs[-1]]


def block_scratch(rows, width):
    return [pltpu.VMEM((BLOCKS, rows, width), bf16), pltpu.SemaphoreType.DMA((BLOCKS,))]


def head_masks(shape):
    lane = lax.broadcasted_iota(jnp.int32, shape, 1)
    return lane < HEAD


def stacked(pair, low):
    zero = jnp.zeros_like(pair)
    return jnp.concatenate([jnp.where(low, pair, zero), jnp.where(low, zero, pair)])


def unstacked(value, low, length):
    return jnp.where(low, value[:length], value[length:])


def rows_of(buffer, length):
    return slice(buffer * length, (buffer + 1) * length)


def rows_of(buffer, length):
    return slice(buffer * length, (buffer + 1) * length)


def qkv_kernel(table_ref, x_ref, bias_ref, p0, p1, p2, p3, qkv_ref, weight_ref, sems):
    width = x_ref.shape[1]
    wait_all(block_copies(table_ref, (p0, p1, p2, p3), 0, 3 * width, weight_ref, sems))
    x = x_ref[...]
    for part in range(3):
        span = slice(part * width, (part + 1) * width)
        weight = flat(weight_ref[:, :, span])
        qkv_ref[:, span] = (mm(x, weight) + bias_ref[:, span]).astype(bf16)


def qkv_forward(table, x, bias, pieces):
    tokens, width = x.shape
    rows = pieces[0].shape[1]
    return call(
        qkv_kernel,
        "qkv_forward",
        [((tokens, 3 * width), bf16), ((BLOCKS, rows, 3 * width), bf16)],
        [SMEM, VMEM, VMEM] + [HBM] * 4,
        [VMEM] * 2,
        (table, x, bias, *pieces),
        6 * tokens * width * width,
        10e6,
        [pltpu.SemaphoreType.DMA((BLOCKS,))],
    )


def attention_kernel(buffers, qkv_ref, context_ref, lse_ref):
    tokens, width = context_ref.shape
    length, pairs = tokens // buffers, width // PAIR
    scale = 1.0 / math.sqrt(HEAD)

    def step(index, carry):
        rows = pl.ds(pl.multiple_of(index // pairs * length, length), length)
        lane = pl.multiple_of(index % pairs * PAIR, PAIR)
        query = qkv_ref[rows, pl.ds(lane, PAIR)]
        key = qkv_ref[rows, pl.ds(lane + width, PAIR)]
        value = qkv_ref[rows, pl.ds(lane + 2 * width, PAIR)]
        low = head_masks(query.shape)
        scores = mm_nt(key, stacked(query, low)) * scale
        peak = jnp.max(scores, axis=0, keepdims=True)
        powers = jnp.exp(scores - peak)
        total = jnp.sum(powers, axis=0, keepdims=True)
        probs = (powers * (1.0 / total)).astype(bf16)
        mixed = mm_tn(value, probs).T
        context_ref[rows, pl.ds(lane, PAIR)] = unstacked(mixed, low, length).astype(bf16)
        lse_ref[index] = peak + jnp.log(total)
        return carry

    lax.fori_loop(0, buffers * pairs, step, 0)


def attention_forward(qkv, buffers):
    tokens, width = qkv.shape[0], qkv.shape[1] // 3
    length = tokens // buffers
    lse = (buffers * (width // PAIR), 1, 2 * length)
    return call(
        functools.partial(attention_kernel, buffers),
        "attention_forward",
        [((tokens, width), bf16), (lse, f32)],
        [VMEM],
        [VMEM] * 2,
        (qkv,),
        4 * tokens * width * length,
        4e6,
        exps=tokens * length * width // HEAD,
    )


def normed_rows(residual):
    center = residual - row_mean(residual)
    inverse = lax.rsqrt(row_mean(center * center) + eps_norm)
    return center * inverse, inverse


def up_kernel(
    table_ref, x_ref, context_ref, vectors_ref, bias_ref, p0, p1, p2, p3,
    hidden_ref, act_ref, hidden_hbm, act_hbm, slope_hbm, normed_hbm, inverse_hbm, wout_hbm, wup_hbm,
    slope_ref, normed_ref, inverse_ref, wout_ref, wup_ref, sems_out, sems_up, sems,
):
    pieces = (p0, p1, p2, p3)
    width, units = x_ref.shape[1], wup_ref.shape[2]
    first = block_copies(table_ref, pieces, 0, width, wout_ref, sems_out)
    copies = block_copies(table_ref, pieces, width, units, wup_ref, sems_up)
    wait_all(first)
    out = mm(context_ref[...], flat(wout_ref[...])) + vectors_ref[0:1]
    normed, inverse = normed_rows(x_ref[...].astype(f32) + out)
    normed_ref[...] = normed
    inverse_ref[...] = jnp.broadcast_to(inverse, inverse_ref.shape)
    hidden_ref[...] = (normed * vectors_ref[1:2] + vectors_ref[2:3]).astype(bf16)
    wait_all(copies)
    pairs = [
        (wup_ref, wup_hbm),
        (wout_ref, wout_hbm),
        (normed_ref, normed_hbm),
        (inverse_ref, inverse_hbm),
        (hidden_ref, hidden_hbm),
    ]
    stores = fetch(pairs, sems)
    wide = 512
    for part in range(units // wide):
        span = pl.ds(part * wide, wide)
        up = mm(hidden_ref[...], flat(wup_ref[:, :, span])) + bias_ref[:, span]
        chance = 0.5 + 0.5 * lax.erf(up * math.sqrt(0.5))
        act_ref[:, span] = (up * chance).astype(bf16)
        density = jnp.exp(up * up * -0.5) * (1.0 / math.sqrt(2.0 * math.pi))
        slope_ref[:, span] = (chance + up * density).astype(bf16)
        pairs = [
            (act_ref.at[:, span], act_hbm.at[:, span]),
            (slope_ref.at[:, span], slope_hbm.at[:, span]),
        ]
        stores += fetch(pairs, sems, 5 + 2 * part)
    wait_all(stores)


def up_forward(table, x, context, vectors, bias, pieces):
    tokens, width = x.shape
    rows, units = pieces[0].shape[1], pieces[0].shape[2] - width
    now = [((tokens, width), bf16), ((tokens, units), bf16)]
    later = [
        ((tokens, units), bf16),
        ((tokens, width), f32),
        ((tokens, LINE), f32),
        ((BLOCKS, rows, width), bf16),
        ((BLOCKS, rows, units), bf16),
    ]
    return call(
        up_kernel,
        "up_forward",
        now + now + later,
        [SMEM] + [VMEM] * 4 + [HBM] * 4,
        [VMEM] * 2 + [HBM] * 7,
        (table, x, context, vectors, bias, *pieces),
        2 * tokens * width * (width + units),
        20e6,
        [pltpu.VMEM(*out) for out in later]
        + [pltpu.SemaphoreType.DMA((BLOCKS,)), pltpu.SemaphoreType.DMA((BLOCKS,))]
        + [pltpu.SemaphoreType.DMA((5 + 2 * (units // 512),))],
        exps=2 * tokens * units,
        limit=24,
    )


def chosen_row(owner_ref, vectors_ref, buffer):
    queries = vectors_ref[VECTORS:]
    query = lax.broadcasted_iota(jnp.int32, queries.shape, 0)
    return jnp.sum(jnp.where(query == owner_ref[buffer], queries, 0.0), axis=0, keepdims=True)


def down_kernel(
    buffers, table_ref, owner_ref, hidden_ref, act_ref, vectors_ref, tags_ref, p0, p1, p2, p3,
    mixed_ref, like_ref, normed_ref, sides_ref, wdown_ref, mixed_hbm, sems, sems_mixed,
):
    tokens = hidden_ref.shape[0]
    length = tokens // buffers
    wait_all(block_copies(table_ref, (p0, p1, p2, p3), 0, wdown_ref.shape[2], wdown_ref, sems))
    weight = flat(wdown_ref[...])
    stores = []
    for buffer in range(buffers):
        rows = rows_of(buffer, length)
        down = mm(act_ref[rows], weight) + vectors_ref[3:4]
        normed, inverse = normed_rows(hidden_ref[rows].astype(f32) + down)
        normed_ref[rows] = normed
        mixed = (normed * vectors_ref[4:5] + vectors_ref[5:6]).astype(bf16)
        mixed_ref[rows] = mixed
        span = pl.ds(buffer * length, length)
        stores += fetch([(mixed_ref.at[span], mixed_hbm.at[span])], sems_mixed, buffer)
        chosen = chosen_row(owner_ref, vectors_ref, buffer).astype(bf16)
        logits = mm_nt(jnp.broadcast_to(chosen, (8, chosen.shape[1])), mixed)[0:1]
        tags = tags_ref[buffer : buffer + 1].astype(f32)
        tail = jnp.log(1.0 + jnp.exp(-jnp.abs(logits)))
        log_yes = jnp.minimum(logits, 0.0) - tail
        log_no = jnp.minimum(-logits, 0.0) - tail
        like = jnp.sum(tags * log_yes + (1.0 - tags) * log_no, axis=1, keepdims=True) / length
        like_ref[buffer : buffer + 1] = jnp.broadcast_to(like, (1, LINE))
        pull = (tags - 1.0 / (1.0 + jnp.exp(-logits))) * (-loss_scale / length)
        pull = jnp.broadcast_to(pull, (LINE, length)).T
        lane = lax.broadcasted_iota(jnp.int32, (length, LINE), 1)
        sides_ref[rows] = jnp.where(lane < HEAD, inverse, pull)
    wait_all(stores)


def down_forward(table, owner, hidden, act, vectors, tags, pieces, buffers):
    tokens, width = hidden.shape
    rows, units = pieces[0].shape[1], act.shape[1]
    return call(
        functools.partial(down_kernel, buffers),
        "down_forward",
        [
            ((tokens, width), bf16),
            ((buffers, LINE), f32),
            ((tokens, width), f32),
            ((tokens, LINE), f32),
            ((BLOCKS, rows, width), bf16),
            ((tokens, width), bf16),
        ],
        [SMEM, SMEM] + [VMEM] * 4 + [HBM] * 4,
        [VMEM] * 5 + [HBM],
        (table, owner, hidden, act, vectors, tags, *pieces),
        2 * tokens * width * units,
        20e6,
        [pltpu.SemaphoreType.DMA((BLOCKS,)), pltpu.SemaphoreType.DMA((buffers,))],
    )


UP_SUM, GAIN_SUM, SHIFT_SUM, QUERY_SUM, DOWN_SUM = range(5)
ATTN_GAIN_SUM, ATTN_SHIFT_SUM, OUT_SUM = range(3)


def adder(sums_ref, buffers):
    def add_up(kind, buffer, value, start=0):
        row = kind * buffers + buffer
        sums_ref[row : row + 1, start : start + value.shape[1]] = jnp.sum(
            value, axis=0, keepdims=True
        )

    return add_up


def up_back_kernel(
    buffers, owner_ref, mixed_ref, normed_ref, sides_ref, slope_ref, vectors_ref, wdown_ref,
    low_ref, up_ref, res_ref, sums_ref,
):
    tokens, width = mixed_ref.shape
    units = slope_ref.shape[1]
    length = tokens // buffers
    sums_ref[...] = jnp.zeros_like(sums_ref)
    add_up = adder(sums_ref, buffers)
    for buffer in range(buffers):
        rows = rows_of(buffer, length)
        normed = normed_ref[rows]
        inverse, pull = sides_ref[rows, 0:1], sides_ref[rows, HEAD : HEAD + 1]
        chosen = chosen_row(owner_ref, vectors_ref, buffer)
        add_up(GAIN_SUM, buffer, pull * normed * chosen)
        add_up(SHIFT_SUM, buffer, pull * chosen)
        add_up(QUERY_SUM, buffer, pull * mixed_ref[rows].astype(f32))
        slope = chosen * vectors_ref[4:5]
        grad = (inverse * pull) * (slope - row_mean(slope) - normed * row_mean(slope * normed))
        res_ref[rows] = grad
        grad = grad.astype(bf16)
        low_ref[rows] = grad
        add_up(DOWN_SUM, buffer, grad.astype(f32))
    part = BLOCKS // 4
    wide = units // 4
    for k in range(4):
        span = slice(k * wide, (k + 1) * wide)
        grad = mm_nt(low_ref[...], flat(wdown_ref[k * part : (k + 1) * part]))
        grad = (grad * slope_ref[:, span].astype(f32)).astype(bf16)
        up_ref[:, span] = grad
        for buffer in range(buffers):
            add_up(UP_SUM, buffer, grad[rows_of(buffer, length)].astype(f32), k * wide)


def up_backward(owner, mixed, normed, sides, slope, vectors, wdown, buffers):
    tokens, width = mixed.shape
    units = slope.shape[1]
    return call(
        functools.partial(up_back_kernel, buffers),
        "up_backward",
        [
            ((tokens, width), bf16),
            ((tokens, units), bf16),
            ((tokens, width), f32),
            ((5 * buffers, units), f32),
        ],
        [SMEM] + [VMEM] * 6,
        [VMEM] * 4,
        (owner, mixed, normed, sides, slope, vectors, wdown),
        2 * tokens * width * units,
        20e6,
    )


def hidden_back_kernel(
    buffers, res_in_ref, up_ref, normed_ref, inverse_ref, vectors_ref, wup_ref, wout_ref,
    res_ref, attn_ref, context_ref, sums_ref,
):
    length = res_ref.shape[0] // buffers
    add_up = adder(sums_ref, buffers)
    weight, weight_out = flat(wup_ref[...]), flat(wout_ref[...])
    for buffer in range(buffers):
        rows = rows_of(buffer, length)
        normed = normed_ref[rows]
        grad = res_in_ref[rows] + mm_nt(up_ref[rows], weight)
        add_up(ATTN_GAIN_SUM, buffer, grad * normed)
        add_up(ATTN_SHIFT_SUM, buffer, grad)
        grad = grad * vectors_ref[1:2]
        grad = inverse_ref[rows, 0:1] * (
            grad - row_mean(grad) - normed * row_mean(grad * normed)
        )
        res_ref[rows] = grad
        grad = grad.astype(bf16)
        attn_ref[rows] = grad
        add_up(OUT_SUM, buffer, grad.astype(f32))
        context_ref[rows] = mm_nt(grad, weight_out).astype(bf16)


def hidden_backward(res, up, normed, inverse, vectors, wup, wout, buffers):
    tokens, width = res.shape
    return call(
        functools.partial(hidden_back_kernel, buffers),
        "hidden_backward",
        [
            ((tokens, width), f32),
            ((tokens, width), bf16),
            ((tokens, width), bf16),
            ((3 * buffers, width), f32),
        ],
        [VMEM] * 7,
        [VMEM] * 4,
        (res, up, normed, inverse, vectors, wup, wout),
        2 * tokens * width * (up.shape[1] + width),
        20e6,
    )


def scaled_rows(ref, scale_ref, buffers, span=slice(None)):
    length = ref.shape[0] // buffers
    return jnp.concatenate(
        [
            (ref[rows_of(b, length), span].astype(f32) * scale_ref[b]).astype(bf16)
            for b in range(buffers)
        ]
    )


def place_rows(table_ref, sums_ref, keep_ref, send_ref, start, width):
    rows = keep_ref.shape[1]
    for spot in range(BLOCKS):
        target = keep_ref if spot < HALF else send_ref
        block = pl.ds(pl.multiple_of(table_ref[spot] * rows, 8), rows)
        target[spot % HALF, :, start : start + width] = sums_ref[block, :width].astype(bf16)


def weight_kernel(buffers, count, table_ref, scale_ref, *refs):
    pairs = [refs[2 * k : 2 * k + 2] for k in range(count)]
    keep_ref, send_ref, sums_ref = refs[2 * count :]
    begin = 0
    for left_ref, right_ref in pairs:
        height, columns = left_ref.shape[1], right_ref.shape[1]
        tile = min(height, columns)
        for start in range(0, columns, tile):
            right = scaled_rows(right_ref, scale_ref, buffers, slice(start, start + tile))
            for row in range(0, height, tile):
                sums_ref[row : row + tile] = mm_tn(left_ref[:, row : row + tile], right)
            place_rows(table_ref, sums_ref, keep_ref, send_ref, begin + start, tile)
        begin += columns


def weight_gradient(name, table, scale, pairs, buffers):
    tokens, height = pairs[0][0].shape
    columns = [right.shape[1] for _, right in pairs]
    operands = [part for pair in pairs for part in pair]
    return call(
        functools.partial(weight_kernel, buffers, len(pairs)),
        name,
        [((HALF, height // BLOCKS, sum(columns)), bf16)] * 2,
        [SMEM, SMEM] + [VMEM] * len(operands),
        [VMEM] * 2,
        (table, scale, *operands),
        2 * tokens * height * sum(columns),
        10e6,
        [pltpu.VMEM((height, min(height, columns[0])), f32)],
        limit=LIMIT + 4 if height > 768 else LIMIT,
    )


def small_columns(
    buffers, count, scale_ref, owner_ref, sums_ref, attn_sums_ref, pre_ref, rows_ref, columns_ref, small_ref
):
    width = rows_ref.shape[1]
    rows = width // BLOCKS

    def weigh(ref, kind, columns=width):
        first = kind * buffers
        return sum(ref[first + b : first + b + 1, :columns] * scale_ref[b] for b in range(buffers))

    rows_ref[...] = jnp.zeros_like(rows_ref)
    kinds = [(attn_sums_ref, kind) for kind in (OUT_SUM, ATTN_GAIN_SUM, ATTN_SHIFT_SUM)]
    kinds += [(sums_ref, kind) for kind in (DOWN_SUM, GAIN_SUM, SHIFT_SUM)]
    for k, (ref, kind) in enumerate(kinds):
        rows_ref[k : k + 1] = weigh(ref, kind)
    pre = sum(pre_ref[b : b + 1] * scale_ref[b] for b in range(buffers))
    for at, total in ((QKV_AT, pre), (UP_AT, weigh(sums_ref, UP_SUM, sums_ref.shape[1]))):
        for k in range(total.shape[1] // width):
            rows_ref[at + k : at + k + 1] = total[:, k * width : (k + 1) * width]
    query = lax.broadcasted_iota(jnp.int32, (count, width), 0)
    total = jnp.zeros((count, width), f32)
    for b in range(buffers):
        row = QUERY_SUM * buffers + b
        mine = sums_ref[row : row + 1, :width] * scale_ref[b]
        total += jnp.where(query == owner_ref[b], mine, 0.0)
    rows_ref[QUERY_AT : QUERY_AT + count] = total
    columns_ref[...] = rows_ref[...].T
    lane = lax.broadcasted_iota(jnp.int32, (rows, LINE), 1)
    for block in range(BLOCKS):
        value = columns_ref[block * rows : (block + 1) * rows]
        for at, per in ((QKV_AT, 2), (UP_AT, 4)):
            for c in range(per):
                spot = (block * per + c) * rows
                source = columns_ref[spot % width : spot % width + rows]
                shift = (c - spot // width) % LINE
                if shift:
                    source = pltpu.roll(source, shift, 1)
                value = jnp.where(lane == at + c, source, value)
        small_ref[block * rows : (block + 1) * rows] = value


def attention_back_kernel(buffers, qkv_ref, lse_ref, grad_ref, pre_ref, bias_ref):
    tokens, width = grad_ref.shape
    length, pairs = tokens // buffers, width // PAIR
    scale = 1.0 / math.sqrt(HEAD)

    def step(index, carry):
        rows = pl.ds(pl.multiple_of(index // pairs * length, length), length)
        lane = pl.multiple_of(index % pairs * PAIR, PAIR)
        query = qkv_ref[rows, pl.ds(lane, PAIR)]
        key = qkv_ref[rows, pl.ds(lane + width, PAIR)]
        value = qkv_ref[rows, pl.ds(lane + 2 * width, PAIR)]
        low = head_masks(query.shape)
        query = stacked(query, low)
        grad = stacked(grad_ref[rows, pl.ds(lane, PAIR)], low)
        probs = jnp.exp(mm_nt(key, query) * scale - lse_ref[index])
        grad_probs = mm_nt(value, grad)
        cross = jnp.sum(grad_probs * probs, axis=0, keepdims=True)
        grad_scores = (probs * (grad_probs - cross)).astype(bf16)
        grad_value = mm(probs.astype(bf16), grad)
        grad_key = mm(grad_scores, query) * scale
        grad_query = unstacked(mm_tn(key, grad_scores).T, low, length) * scale
        pre_ref[rows, pl.ds(lane, PAIR)] = grad_query.astype(bf16)
        pre_ref[rows, pl.ds(lane + width, PAIR)] = grad_key.astype(bf16)
        pre_ref[rows, pl.ds(lane + 2 * width, PAIR)] = grad_value.astype(bf16)
        return carry

    lax.fori_loop(0, buffers * pairs, step, 0)
    for buffer in range(buffers):
        rows = rows_of(buffer, length)
        for start, source in ((0, 0), (width, 2 * width)):
            piece = pre_ref[rows, source : source + width].astype(f32)
            bias_ref[buffer : buffer + 1, start : start + width] = jnp.sum(
                piece, axis=0, keepdims=True
            )


def attention_backward(qkv, lse, grad, buffers):
    tokens, width = grad.shape
    length = tokens // buffers
    return call(
        functools.partial(attention_back_kernel, buffers),
        "attention_backward",
        [((tokens, 3 * width), bf16), ((buffers, 2 * width), f32)],
        [VMEM] * 3,
        [VMEM] * 2,
        (qkv, lse, grad),
        10 * tokens * length * width,
        7e6,
        exps=tokens * length * width // HEAD,
    )


def qkv_gradient_kernel(
    buffers, count, table_ref, scale_ref, owner_ref, x_ref, pre_ref, bias_ref, sums_in_ref, attn_sums_ref,
    keep_ref, send_ref, sums_ref, rows_ref, columns_ref, small_ref,
):
    width = x_ref.shape[1]
    for part in range(3):
        right = scaled_rows(pre_ref, scale_ref, buffers, slice(part * width, (part + 1) * width))
        sums_ref[...] = mm_tn(x_ref[...], right)
        place_rows(table_ref, sums_ref, keep_ref, send_ref, part * width, width)
    small_columns(
        buffers, count, scale_ref, owner_ref, sums_in_ref, attn_sums_ref, bias_ref,
        rows_ref, columns_ref, small_ref,
    )
    place_rows(table_ref, small_ref, keep_ref, send_ref, 3 * width, LINE)


def qkv_gradient(table, scale, owner, count, x, pre, pre_sums, sums, attn_sums, buffers):
    tokens, width = x.shape
    blocks = ((HALF, width // BLOCKS, 3 * width + LINE), bf16)
    return call(
        functools.partial(qkv_gradient_kernel, buffers, count),
        "qkv_gradient",
        [blocks, blocks],
        [SMEM] * 3 + [VMEM] * 5,
        [VMEM] * 2,
        (table, scale, owner, x, pre, pre_sums, sums, attn_sums),
        6 * tokens * width * width,
        10e6,
        [
            pltpu.VMEM((width, width), f32),
            pltpu.VMEM((LINE, width), f32),
            pltpu.VMEM((width, LINE), f32),
            pltpu.VMEM((width, LINE), f32),
        ],
    )


def states_kernel(buffers, scale_ref, res_ref, pre_ref, weight_ref, out_ref):
    length = res_ref.shape[0] // buffers
    weight = flat(weight_ref[...])
    for buffer in range(buffers):
        rows = rows_of(buffer, length)
        grad = res_ref[rows] + mm_nt(pre_ref[rows], weight)
        out_ref[rows] = (grad * scale_ref[buffer]).astype(bf16)


def states_gradient(scale, res, pre, weight, buffers):
    tokens, width = res.shape
    return call(
        functools.partial(states_kernel, buffers),
        "states_gradient",
        [((tokens, width), bf16)],
        [SMEM] + [VMEM] * 3,
        [VMEM],
        (scale, res, pre, weight),
        6 * tokens * width * width,
        8e6,
    )[0]


def body(
    slot_states, answer_tags, slot_mask, retrieval, query_emb, qkv_weight, qkv_bias, out_weight,
    out_bias, attn_gain, attn_shift, up_weight, up_bias, down_weight, down_bias, ffn_gain, ffn_shift,
):
    group_count = lax.axis_size(AXES)
    device_index = lax.axis_index(AXES)
    tuned = group_count == BLOCKS
    buffers, length, width = slot_states.shape
    query_count, slot_count = slot_mask.shape
    tokens = buffers * length
    x = slot_states.reshape(tokens, width)

    running = jnp.cumsum(slot_mask.reshape(-1), dtype=jnp.int32)
    slot_ranks = jnp.arange(buffers, dtype=jnp.int32) * group_count + device_index
    places = jnp.sum(
        (running[None, :] <= slot_ranks[:, None]).astype(jnp.int32), axis=1, dtype=jnp.int32
    )
    slot_pick = places[:, None] == jnp.arange(query_count * slot_count, dtype=jnp.int32)[None, :]
    owner = places // slot_count
    owner_mask = owner[:, None] == jnp.arange(query_count, dtype=jnp.int32)[None]
    prior_score = jnp.sum(jnp.where(slot_pick, retrieval.reshape(-1)[None, :], 0.0), axis=1)

    order = Order(tuned)
    if tuned:
        table = position_table(device_index)
        vectors = (out_bias, attn_gain, attn_shift, down_bias, ffn_gain, ffn_shift)
        g1 = Gather(order, pack_first(qkv_weight, vectors, qkv_bias, up_bias, query_emb))
        g2 = Gather(order, jnp.concatenate([out_weight, up_weight], axis=1)[None])
        g3 = Gather(order, down_weight[None])
        g1.start_line()
        g1.join()
        g1.start(SIDE)
        g2.start_line(g1.held)
        g1.join()
        g1.start(OTHER)
        owner = order.place(owner)
        prior_score = order.place(prior_score)
        g2.join()
        g3.start_line(g2.held)
        g1.start_cores()
        g2.start(SIDE, g1.last)
        first = g1.pieces()
        vectors, bias, up_bias_all = unpack_small(table, first, 3 * width, query_count)
    else:
        table = jnp.arange(BLOCKS, dtype=jnp.int32)
        everything = lambda part: lax.all_gather(part, AXES, axis=0, tiled=True).astype(f32)
        first = gather_plain(qkv_weight)
        second = gather_plain(jnp.concatenate([out_weight, up_weight], axis=1))
        third = gather_plain(down_weight)
        vectors = jnp.stack(
            [
                everything(part)
                for part in (out_bias, attn_gain, attn_shift, down_bias, ffn_gain, ffn_shift)
            ]
        )
        bias = everything(qkv_bias)
        bias = jnp.concatenate([bias[:width], jnp.zeros((width,), f32), bias[width:]]).reshape(1, -1)
        up_bias_all = everything(up_bias).reshape(1, -1)
        query_table = lax.all_gather(query_emb, AXES, axis=1, tiled=True).astype(f32)
        vectors = jnp.concatenate([vectors, jnp.zeros((VECTORS - SIX, width), f32), query_table])

    qkv, wqkv = qkv_forward(table, x, bias, first)
    if tuned:
        order.mark(qkv)
        g2.join()
        g2.start(OTHER)
        g3.join()
        g3.start(SIDE)
    context, lse = attention_forward(order.place(qkv), buffers)
    if tuned:
        order.mark(context)
        g2.start_cores()
        g3.join()
        g3.start(OTHER)
        second = g2.pieces()
    hidden, act, hidden_late, act_late, slope, normed, inverse, wout, wup = up_forward(
        table, x, context, vectors, up_bias_all, second
    )
    if tuned:
        order.mark(act)
        g3.start_cores()
        third = g3.pieces()
    mixed, like, normed_out, sides, wdown, mixed_out = down_forward(
        table, owner, hidden, act, vectors, answer_tags, third, buffers
    )

    scores = like[:, 0] + prior_score
    masked = jnp.where(owner_mask, scores[:, None], neg_fill)
    local_peak = jnp.max(masked, axis=0)
    local_total = jnp.sum(jnp.where(owner_mask, jnp.exp(masked - local_peak[None, :]), 0.0), axis=0)
    merged = (local_peak, local_total)
    if tuned:
        order.mark(local_total)
        merged = merge_join(order, merged, merge_start(merged, CORE_BIT))
        got = merge_start(merged, Z_FAR)
    else:
        merged = merge_plain(merged)

    grad_low, grad_up, grad_res, sums = up_backward(
        owner, order.place(mixed), normed_out, sides, slope, vectors, wdown, buffers
    )
    if tuned:
        order.mark(grad_low)
        merged = merge_join(order, merged, got)
        got = merge_start(merged, X_BIT)
    grad_hidden, grad_attn, grad_context, attn_sums = hidden_backward(
        order.place(grad_res), grad_up, normed, inverse, vectors, wup, wout, buffers
    )
    if tuned:
        order.mark(grad_attn)
        merged = merge_join(order, merged, got)
        got = merge_start(merged, Y_BIT)
    grad_pre, pre_sums = attention_backward(qkv, lse, order.place(grad_context), buffers)
    if tuned:
        order.mark(pre_sums)
        merged = merge_join(order, merged, got)
        merged = merge_join(order, merged, merge_start(merged, Z_NEAR))
    totals = merged[0] + jnp.log(merged[1])
    loss = -jnp.sum(totals)
    scale = jnp.sum(
        jnp.where(owner_mask, jnp.exp(scores[:, None] - totals[None, :]), 0.0), axis=1
    )

    halves3 = weight_gradient("down_gradient", table, scale, [(act_late, grad_low)], buffers)
    if tuned:
        order.mark(halves3[1])
        s3 = Scatter(order, *halves3)
        s3.start(CORES)
        s3.join()
        s3.start(OTHER)
    pairs = [(context, grad_attn), (order.place(hidden_late), grad_up)]
    halves2 = weight_gradient("up_gradient", table, scale, pairs, buffers)
    if tuned:
        order.mark(halves2[1])
        s2 = Scatter(order, *halves2)
        s2.start(CORES)
    halves1 = qkv_gradient(
        table, scale, owner, query_count, x, order.place(grad_pre), pre_sums, sums, attn_sums, buffers
    )
    if tuned:
        order.mark(halves1[1])
        s1 = Scatter(order, *halves1)
        s1.start(CORES)
        s2.join()
        s2.start(OTHER)
        s3.join()
        s3.start(SIDE)
    states = states_gradient(scale, grad_hidden, order.place(grad_pre), wqkv, buffers)
    if tuned:
        order.mark(states)
        s1.join()
        s1.start(OTHER)
        s3.start_line()
        s2.join()
        s2.start(SIDE)
        s1.join()
        s1.start(SIDE)
        third_grad = s3.finish()
        order.mark(third_grad)
        s2.start_line()
        s1.start_line()
        second_grad = s2.finish(0, width), s2.finish(width)
        order.mark(second_grad[1])
        first_grad = s1.finish(0, 3 * width)
        small = s1.finish(3 * width)
    else:
        third_grad = scatter_plain(*halves3)
        cut = lambda halves, start, end: scatter_plain(*(half[:, :, start:end] for half in halves))
        second_grad = cut(halves2, 0, width), cut(halves2, width, width + up_weight.shape[1])
        first_grad = cut(halves1, 0, 3 * width)
    if tuned:
        *six, qkv_bias_sum, up_bias_sum, query_sum = split_small(
            small, query_count
        )
    else:
        weigh = lambda part: jnp.sum(scale[:, None] * part, axis=0)
        mine = lambda part: lax.psum_scatter(weigh(part), AXES, scatter_dimension=0, tiled=True)
        rows_for = lambda part, kind: part[kind * buffers : (kind + 1) * buffers, :width]
        six = [mine(rows_for(attn_sums, kind)) for kind in (OUT_SUM, ATTN_GAIN_SUM, ATTN_SHIFT_SUM)]
        six += [mine(rows_for(sums, kind)) for kind in (DOWN_SUM, GAIN_SUM, SHIFT_SUM)]
        qkv_bias_sum, up_bias_sum = mine(pre_sums), mine(sums[:buffers])
        weighed = jnp.where(owner_mask, scale[:, None], 0.0)
        query_sum = jnp.sum(weighed[:, :, None] * rows_for(sums, QUERY_SUM)[:, None, :], axis=0)
        query_sum = lax.psum_scatter(query_sum, AXES, scatter_dimension=1, tiled=True)
    return (
        mixed_out.reshape(slot_states.shape),
        loss,
        states.reshape(slot_states.shape),
        query_sum,
        first_grad,
        qkv_bias_sum,
        second_grad[0],
        six[0],
        six[1],
        six[2],
        second_grad[1],
        up_bias_sum,
        third_grad,
        six[3],
        six[4],
        six[5],
    )


def solution(mesh):
    split = P(AXES)
    in_specs = (split, split, P(), P(), P(None, AXES)) + (split,) * 12
    out_specs = (split, P(), split, P(None, AXES)) + (split,) * 12
    return jax.shard_map(body, mesh=mesh, in_specs=in_specs, out_specs=out_specs, check_vma=False)
```

time: 329 us -> 270 us (0.82)
  waiting for transfers between devices: 136 us -> 94.2 us
  Pallas kernels: 95.1 us -> 80.7 us
  local copies, waits for them, and re-layouts: 27.9 us -> 20.9 us
  starting transfers between devices: 40.6 us -> 46.9 us
    ppermute x38 -> x44, waiting for transfers between devices: 136 us -> 94.2 us  [exchange(): return lax.ppermute(value, AXES, pairs)]
    pallas_call x12 -> x14, Pallas kernels: 95.1 us -> 80.7 us  [call(): pl.pallas_call(kernel, out_shape=[pltpu.HBM(shape, dtype) if spec is HBM...]
    unnamed x58 -> x101, local copies, waits for them, and re-layouts: 11.1 us -> 18.5 us
    slice x23 -> x1, local copies, waits for them, and re-layouts: 7.13 us -> 0.12 us  [body(): scores = like[:, 0] + prior_score]
    ppermute x38 -> x44, starting transfers between devices: 40.6 us -> 46.9 us  [exchange(): return lax.ppermute(value, AXES, pairs)]
    reshape x11 -> x0, local copies, waits for them, and re-layouts: 4.23 us -> none  [the longest x1 0.76 us: body(): up_bias.reshape(rows, 4)]
    another operation x13 -> x1, local copies, waits for them, and re-layouts: 4.58 us -> 0.69 us  [the longest x6 4.48 us: body(): jnp.stack([out_bias, attn_gain, attn_shift, down_bias, ffn_gain, ffn_shif...]
    concatenate x10 -> x3, other arithmetic: 3.79 us -> 0.24 us  [join(): self.held = jnp.concatenate([self.held, *got])]
  transfers between devices with their start and end apart: 38 -> 44, of which waited for: 20 -> 20; matrix products, arithmetic and copies ran while one was open for 8% -> 8% of each run, Pallas kernels for 24% -> 22%
where the time goes in v3:
time: 270 us; the launch traced here: 266 us
  waiting for transfers between devices  94.2 us (35%)
  Pallas kernels  80.7 us (30%)
  starting transfers between devices  46.9 us (17%)
  local copies, waits for them, and re-layouts  20.9 us (8%)
  other arithmetic  19.7 us (7%)
  between operations  3.32 us (1%)
    ppermute x44, waiting for transfers between devices, exchange(): return lax.ppermute(value, AXES, pairs)  94.2 us
    pallas_call x14, Pallas kernels, call(): pl.pallas_call(kernel, out_shape=[pltpu.HBM(shape, dtype) if spec is HBM...  80.7 us
    ppermute x44, starting transfers between devices, exchange(): return lax.ppermute(value, AXES, pairs)  46.9 us
    unnamed x101, local copies, waits for them, and re-layouts  18.5 us
    convert_element_type x9, other arithmetic, add_low(): return (first.astype(f32) + second.astype(f32)).astype(bf16)  11 us
  transfers between devices with their start and end apart: 44, of which 20 were waited for; matrix products, arithmetic and copies ran while one was open for 8% of the time, Pallas kernels for 22%

profile of v3, /device:TPU:0, one launch (start us, length us, event | category | flops | bytes accessed | tf_op | source)
XLA Modules:
  0.0 265.7 jit_solution(4633580608646006036)
XLA Ops:
  1.9 5.1 %collective-permute-start.2 = (bf16[1,24,2432]{2,1,0:T(8,128)(2,1)S(1)}, bf16[1,24,2432]{2,1,0:T(8,128)(2,1)S(1)}, u32[]{:S(2)}, u32[]{:S(2)}) collective-permute-start(bf16[1,24,2432]{2,1,0:T(8,128)(2,1)S(1)} %pack_first.1), channel_id=1, source_target_pairs={{0,6},{1,7},{2,4},{3,5},{4,2},{5,3},{6,0},{7,1},{8,14},{9,15},{10,... | collective-permute-start | bytes 350216 | tf_op jit(solution)/shard_map/ppermute | solution.py:50
  18.6 7.0 %collective-permute-done.3 = bf16[4,24,2432]{2,1,0:T(8,128)(2,1)S(1)} collective-permute-done((bf16[4,24,2432]{2,1,0:T(8,128)(2,1)S(1)}, bf16[4,24,2432]{2,1,0:T(8,128)(2,1)S(1)}, u32[]{:S(2)}, u32[]{:S(2)}) %collective-permute-start.3) | collective-permute-done | bytes 466976 | tf_op jit(solution)/shard_map/ppermute | solution.py:50
  31.8 5.0 %collective-permute-done.7 = bf16[1,24,3840]{2,1,0:T(8,128)(2,1)S(1)} collective-permute-done((bf16[1,24,3840]{2,1,0:T(8,128)(2,1)S(1)}, bf16[1,24,3840]{2,1,0:T(8,128)(2,1)S(1)}, u32[]{:S(2)}, u32[]{:S(2)}) %collective-permute-start.7) | collective-permute-done | bytes 184352 | tf_op jit(solution)/shard_map/ppermute | solution.py:50
  39.8 3.7 %collective-permute-done.5 = bf16[1,24,3840]{2,1,0:T(8,128)(2,1)S(1)} collective-permute-done((bf16[1,24,3840]{2,1,0:T(8,128)(2,1)S(1)}, bf16[1,24,3840]{2,1,0:T(8,128)(2,1)S(1)}, u32[]{:S(2)}, u32[]{:S(2)}) %collective-permute-start.5) | collective-permute-done | bytes 184352 | tf_op jit(solution)/shard_map/ppermute | solution.py:50
  49.4 5.1 %qkv_forward.1 = (bf16[576,2304]{1,0:T(8,128)(2,1)S(1)}, bf16[32,24,2304]{2,1,0:T(8,128)(2,1)S(1)}) custom-call(s32[32]{0:T(128)S(1)} %fusion.5.table_ref, bf16[576,768]{1,0:T(8,128)(2,1)S(1)} %bitcast.150, f32[1,2304]{1,0:T(1,128)S(1)} %get-tuple-element.125.bias_ref, bf16[8,24,2432]{2,1,0:T(8,128)(2,1)} %copy-done.28, bf16[8,24,2432]{2,1,0:T(8,128)(2,1)} %copy-done.29, ...), custom_call_target="tpu_custom_call" | custom-call | flops 40768632 | bytes 200000 | tf_op jit(solution)/shard_map/qkv_forward/pallas_call | solution.py:173
  61.7 4.2 %collective-permute-done.13 = bf16[1,96,768]{2,1,0:T(8,128)(2,1)S(1)} collective-permute-done((bf16[1,96,768]{2,1,0:T(8,128)(2,1)S(1)}, bf16[1,96,768]{2,1,0:T(8,128)(2,1)S(1)}, u32[]{:S(2)}, u32[]{:S(2)}) %collective-permute-start.13) | collective-permute-done | bytes 147488 | tf_op jit(solution)/shard_map/ppermute | solution.py:50
  65.8 4.7 %collective-permute-done.12 = bf16[1,96,768]{2,1,0:T(8,128)(2,1)S(1)} collective-permute-done((bf16[1,96,768]{2,1,0:T(8,128)(2,1)S(1)}, bf16[1,96,768]{2,1,0:T(8,128)(2,1)S(1)}, u32[]{:S(2)}, u32[]{:S(2)}) %collective-permute-start.12) | collective-permute-done | bytes 147488 | tf_op jit(solution)/shard_map/ppermute | solution.py:50
  73.9 9.3 %attention_forward.1 = (bf16[576,768]{1,0:T(8,128)(2,1)S(1)}, f32[12,1,576]{2,1,0:T(1,128)S(1)}) custom-call(bf16[576,2304]{1,0:T(8,128)(2,1)S(1)} %get-tuple-element.133.qkv_ref), custom_call_target="tpu_custom_call" | custom-call | flops 10192158 | bytes 80000 | tf_op jit(solution)/shard_map/attention_forward/pallas_call | solution.py:173
  90.0 11.7 %up_forward.1 = (bf16[576,768]{1,0:T(8,128)(2,1)S(1)}, bf16[576,3072]{1,0:T(8,128)(2,1)S(1)}, bf16[576,768]{1,0:T(8,128)(2,1)}, bf16[576,3072]{1,0:T(8,128)(2,1)...) custom-call(s32[32]{0:T(128)S(1)} %fusion.5.table_ref, ...), custom_call_target="tpu_custom_call" | custom-call | flops 67947728 | bytes 400000 | tf_op jit(solution)/shard_map/up_forward/pallas_call | solution.py:173
  113.5 9.0 %down_forward.1 = (bf16[576,768]{1,0:T(8,128)(2,1)S(1)}, f32[2,128]{1,0:T(2,128)S(1)}, f32[576,768]{1,0:T(8,128)S(1)}, f32[576,128]{1,0:T(8,128)S(1)}, bf16[32,9...) custom-call(s32[32]{0:T(128)S(1)} %fusion.5.table_ref, s32[2]{0:T(128)S(1)} %and_select_fusion.owner_ref, ...), custom_call_target="tpu_custom_call" | custom-call | flops 54358180 | bytes 400000 | tf_op jit(solution)/shard_map/down_forward/pallas_call | solution.py:173
  125.3 5.5 %up_backward.1 = (bf16[576,768]{1,0:T(8,128)(2,1)S(1)}, bf16[576,3072]{1,0:T(8,128)(2,1)S(1)}, f32[576,768]{1,0:T(8,128)S(1)}, f32[10,3072]{1,0:T(8,128)S(1)}) custom-call(s32[2]{0:T(128)S(1)} %and_select_fusion.owner_ref, bf16[576,768]{1,0:T(8,128)(2,1)S(1)} %get-tuple-element.151.mixed_ref, f32[576,768]{1,0:T(8,128)S(1)} %get-tuple-element.152.normed_ref, ...), custom_call_target="tpu_custom_call" | custom-call | flops 54358180 | bytes 400000 | tf_op jit(solution)/shard_map/up_backward/pallas_call | solution.py:173
  131.9 5.7 %hidden_backward.1 = (f32[576,768]{1,0:T(8,128)S(1)}, bf16[576,768]{1,0:T(8,128)(2,1)S(1)}, bf16[576,768]{1,0:T(8,128)(2,1)S(1)}, f32[6,768]{1,0:T(8,128)S(1)}) custom-call(f32[576,768]{1,0:T(8,128)S(1)} %get-tuple-element.159.res_in_ref, bf16[576,3072]{1,0:T(8,128)(2,1)S(1)} %get-tuple-element.160.up_ref.refs_3_, f32[576,768]{1,0:T(8,128)S(1)} %copy-done.13, ...), custom_call_target="tpu_custom_call" | custom-call | flops 67947728 | bytes 400000 | tf_op jit(solution)/shard_map/hidden_backward/pallas_call | solution.py:173
  140.0 10.6 %attention_backward.1 = (bf16[576,2304]{1,0:T(8,128)(2,1)S(1)}, f32[2,1536]{1,0:T(2,128)S(1)}) custom-call(bf16[576,2304]{1,0:T(8,128)(2,1)S(1)} %get-tuple-element.133.qkv_ref, f32[12,1,576]{2,1,0:T(1,128)S(1)} %copy-done.25, bf16[576,768]{1,0:T(8,128)(2,1)S(1)} %get-tuple-element.169.grad_ref), custom_call_target="tpu_custom_call" | custom-call | flops 25480396 | bytes 140000 | tf_op jit(solution)/shard_map/attention_backward/pallas_call | solution.py:173
  151.0 3.4 %collective-permute-done.25 = f32[2,8]{1,0:T(2,128)S(1)} collective-permute-done((f32[2,8]{1,0:T(2,128)S(1)}, f32[2,8]{1,0:T(2,128)S(1)}, u32[]{:S(2)}, u32[]{:S(2)}) %collective-permute-start.25) | collective-permute-done | bytes 96 | tf_op jit(solution)/shard_map/ppermute | solution.py:50
  154.6 4.9 %down_gradient.1 = (bf16[16,96,768]{2,1,0:T(8,128)(2,1)S(1)}, bf16[16,96,768]{2,1,0:T(8,128)(2,1)S(1)}) custom-call(s32[32]{0:T(128)S(1)} %fusion.5.table_ref, f32[2]{0:T(128)S(1)} %select_reduce_fusion.1.scale_ref, bf16[576,3072]{1,0:T(8,128)(2,1)S(1)} %copy-done.5, bf16[576,768]{1,0:T(8,128)(2,1)S(1)} %get-tuple-element.156.refs_1_), custom_call_target="tpu_custom_call" | custom-call | flops 54358180 | bytes 200000 | tf_op jit(solution)/shard_map/down_gradient/pallas_call | solution.py:173
  159.5 4.5 %collective-permute-done.26 = bf16[16,96,768]{2,1,0:T(8,128)(2,1)S(1)} collective-permute-done((bf16[16,96,768]{2,1,0:T(8,128)(2,1)S(1)}, bf16[16,96,768]{2,1,0:T(8,128)(2,1)S(1)}, u32[]{:S(2)}, u32[]{:S(2)}) %collective-permute-start.26) | collective-permute-done | bytes 2359328 | tf_op jit(solution)/shard_map/ppermute | solution.py:50
  166.3 6.0 %up_gradient.1 = (bf16[16,24,3840]{2,1,0:T(8,128)(2,1)S(1)}, bf16[16,24,3840]{2,1,0:T(8,128)(2,1)S(1)}) custom-call(s32[32]{0:T(128)S(1)} %fusion.5.table_ref, f32[2]{0:T(128)S(1)} %select_reduce_fusion.1.scale_ref, bf16[576,768]{1,0:T(8,128)(2,1)S(1)} %copy-done.10, bf16[576,768]{1,0:T(8,128)(2,1)S(1)} %get-tuple-element.165.refs_1_, ...), custom_call_target="tpu_custom_call" | custom-call | flops 67947728 | bytes 200000 | tf_op jit(solution)/shard_map/up_gradient/pallas_call | solution.py:173
  172.5 5.0 %qkv_gradient.1 = (bf16[16,24,2432]{2,1,0:T(8,128)(2,1)S(1)}, bf16[16,24,2432]{2,1,0:T(8,128)(2,1)}) custom-call(s32[32]{0:T(128)S(1)} %fusion.5.table_ref, f32[2]{0:T(128)S(1)} %select_reduce_fusion.1.scale_ref, s32[2]{0:T(128)S(1)} %and_select_fusion.owner_ref, bf16[576,768]{1,0:T(8,128)(2,1)S(1)} %bitcast.152, ...), custom_call_target="tpu_custom_call" | custom-call | flops 40768632 | bytes 200000 | tf_op jit(solution)/shard_map/qkv_gradient/pallas_call | solution.py:173
  185.0 10.8 %collective-permute-done.27 = bf16[8,96,768]{2,1,0:T(8,128)(2,1)} collective-permute-done((bf16[8,96,768]{2,1,0:T(8,128)(2,1)}, bf16[8,96,768]{2,1,0:T(8,128)(2,1)}, u32[]{:S(2)}, u32[]{:S(2)}) %collective-permute-start.27) | collective-permute-done | bytes 1179680 | tf_op jit(solution)/shard_map/ppermute | solution.py:50
  200.3 3.7 %states_gradient.1 = bf16[576,768]{1,0:T(8,128)(2,1)} custom-call(f32[2]{0:T(128)S(1)} %select_reduce_fusion.1.scale_ref, f32[576,768]{1,0:T(8,128)S(1)} %copy-done.15, bf16[576,2304]{1,0:T(8,128)(2,1)S(1)} %copy-done.1, bf16[32,24,2304]{2,1,0:T(8,128)(2,1)S(1)} %copy-done.4), custom_call_target="tpu_custom_call" | custom-call | flops 40768632 | bytes 160000 | tf_op jit(solution)/shard_map/states_gradient/pallas_call | solution.py:173
  207.3 6.8 %collective-permute-done.32 = bf16[4,96,768]{2,1,0:T(8,128)(2,1)S(1)} collective-permute-done((bf16[4,96,768]{2,1,0:T(8,128)(2,1)S(1)}, bf16[4,96,768]{2,1,0:T(8,128)(2,1)S(1)}, u32[]{:S(2)}, u32[]{:S(2)}) %collective-permute-start.32) | collective-permute-done | bytes 589856 | tf_op jit(solution)/shard_map/ppermute | solution.py:50
  221.4 12.5 %collective-permute-done.30 = bf16[8,24,2432]{2,1,0:T(8,128)(2,1)S(1)} collective-permute-done((bf16[8,24,2432]{2,1,0:T(8,128)(2,1)S(1)}, bf16[8,24,2432]{2,1,0:T(8,128)(2,1)S(1)}, u32[]{:S(2)}, u32[]{:S(2)}) %collective-permute-start.30) | collective-permute-done | bytes 933920 | tf_op jit(solution)/shard_map/ppermute | solution.py:50
  244.8 7.6 %collective-permute-done.41 = bf16[1,24,3840]{2,1,0:T(8,128)(2,1)S(1)} collective-permute-done((bf16[1,24,3840]{2,1,0:T(8,128)(2,1)S(1)}, bf16[1,24,3840]{2,1,0:T(8,128)(2,1)S(1)}, u32[]{:S(2)}, u32[]{:S(2)}) %collective-permute-start.41) | collective-permute-done | bytes 184352 | tf_op jit(solution)/shard_map/ppermute | solution.py:50
  256.2 6.1 %collective-permute-done.38 = bf16[1,24,2432]{2,1,0:T(8,128)(2,1)S(1)} collective-permute-done((bf16[1,24,2432]{2,1,0:T(8,128)(2,1)S(1)}, bf16[1,24,2432]{2,1,0:T(8,128)(2,1)S(1)}, u32[]{:S(2)}, u32[]{:S(2)}) %collective-permute-start.38) | collective-permute-done | bytes 116768 | tf_op jit(solution)/shard_map/ppermute | solution.py:50
  (230 shorter events, 104.5 us)
Async XLA Ops:
  25.6 18.0 %collective-permute-start.4 = (bf16[8,24,2432]{2,1,0:T(8,128)(2,1)S(1)}, bf16[8,24,2432]{2,1,0:T(8,128)(2,1)S(1)}, u32[]{:S(2)}, u32[]{:S(2)}) collective-permute-start(bf16[8,24,2432]{2,1,0:T(8,128)(2,1)S(1)} %constant_dynamic-update-slice_fusion.p0), channel_id=1, source_target_pairs={{0,1},{1,0},{2,3},{3,2},{4,5},{5,4},{6,7},{7,6},{8,24},{9,25},{10,... | collective-permute-start | bytes 2801672 | tf_op jit(solution)/shard_map/ppermute | solution.py:50
  29.8 13.7 %collective-permute-start.5 = (bf16[1,24,3840]{2,1,0:T(8,128)(2,1)S(1)}, bf16[1,24,3840]{2,1,0:T(8,128)(2,1)S(1)}, u32[]{:S(2)}, u32[]{:S(2)}) collective-permute-start(bf16[1,24,3840]{2,1,0:T(8,128)(2,1)S(1)} %maximum_bitcast_fusion), channel_id=1, source_target_pairs={{0,4},{1,5},{2,6},{3,7},{4,0},{5,1},{6,2},{7,3},{8,12},{9,13},{10,... | collective-permute-start | bytes 552968 | tf_op jit(solution)/shard_map/ppermute | solution.py:50
  31.7 12.7 %collective-permute-start.8 = (bf16[8,24,2432]{2,1,0:T(8,128)(2,1)S(1)}, bf16[8,24,2432]{2,1,0:T(8,128)(2,1)S(1)}, u32[]{:S(2)}, u32[]{:S(2)}) collective-permute-start(bf16[8,24,2432]{2,1,0:T(8,128)(2,1)S(1)} %constant_dynamic-update-slice_fusion.p0), channel_id=1, source_target_pairs={{0,8},{1,9},{2,10},{3,11},{4,12},{5,13},{6,14},{7,15},{8,0},{9,1},... | collective-permute-start | bytes 2801672 | tf_op jit(solution)/shard_map/ppermute | solution.py:50
  43.7 12.5 %collective-permute-start.11 = (bf16[4,24,3840]{2,1,0:T(8,128)(2,1)S(1)}, bf16[4,24,3840]{2,1,0:T(8,128)(2,1)S(1)}, u32[]{:S(2)}, u32[]{:S(2)}) collective-permute-start(bf16[4,24,3840]{2,1,0:T(8,128)(2,1)S(1)} %pad_maximum_fusion), channel_id=1, source_target_pairs={{0,16},{1,17},{2,18},{3,19},{4,20},{5,21},{6,22},{7,23},{8,9},{9,8... | collective-permute-start | bytes 2211848 | tf_op jit(solution)/shard_map/ppermute | solution.py:50
  56.4 28.2 %collective-permute-start.14 = (bf16[8,24,3840]{2,1,0:T(8,128)(2,1)S(1)}, bf16[8,24,3840]{2,1,0:T(8,128)(2,1)S(1)}, u32[]{:S(2)}, u32[]{:S(2)}) collective-permute-start(bf16[8,24,3840]{2,1,0:T(8,128)(2,1)S(1)} %constant_dynamic-update-slice_fusion.5.p0), channel_id=1, source_target_pairs={{0,1},{1,0},{2,3},{3,2},{4,5},{5,4},{6,7},{7,6},{8,24},{9,25},{10,... | collective-permute-start | bytes 4423688 | tf_op jit(solution)/shard_map/ppermute | solution.py:50
  60.2 12.0 %collective-permute-start.10 = (bf16[1,96,768]{2,1,0:T(8,128)(2,1)S(1)}, bf16[1,96,768]{2,1,0:T(8,128)(2,1)S(1)}, u32[]{:S(2)}, u32[]{:S(2)}) collective-permute-start(bf16[1,96,768]{2,1,0:T(8,128)(2,1)S(1)} %bitcast.158), channel_id=1, source_target_pairs={{0,4},{1,5},{2,6},{3,7},{4,0},{5,1},{6,2},{7,3},{8,12},{9,13},{10,... | collective-permute-start | bytes 442376 | tf_op jit(solution)/shard_map/ppermute | solution.py:50
  72.2 14.2 %collective-permute-start.16 = (bf16[4,96,768]{2,1,0:T(8,128)(2,1)S(1)}, bf16[4,96,768]{2,1,0:T(8,128)(2,1)S(1)}, u32[]{:S(2)}, u32[]{:S(2)}) collective-permute-start(bf16[4,96,768]{2,1,0:T(8,128)(2,1)S(1)} %pad_maximum_fusion.1), channel_id=1, source_target_pairs={{0,16},{1,17},{2,18},{3,19},{4,20},{5,21},{6,22},{7,23},{8,9},{9,8... | collective-permute-start | bytes 1769480 | tf_op jit(solution)/shard_map/ppermute | solution.py:50
  73.9 14.4 %collective-permute-start.15 = (bf16[8,24,3840]{2,1,0:T(8,128)(2,1)S(1)}, bf16[8,24,3840]{2,1,0:T(8,128)(2,1)S(1)}, u32[]{:S(2)}, u32[]{:S(2)}) collective-permute-start(bf16[8,24,3840]{2,1,0:T(8,128)(2,1)S(1)} %constant_dynamic-update-slice_fusion.5.p0), channel_id=1, source_target_pairs={{0,8},{1,9},{2,10},{3,11},{4,12},{5,13},{6,14},{7,15},{8,0},{9,1},... | collective-permute-start | bytes 4423688 | tf_op jit(solution)/shard_map/ppermute | solution.py:50
  87.3 17.0 %collective-permute-start.18 = (bf16[8,96,768]{2,1,0:T(8,128)(2,1)}, bf16[8,96,768]{2,1,0:T(8,128)(2,1)}, u32[]{:S(2)}, u32[]{:S(2)}) collective-permute-start(bf16[8,96,768]{2,1,0:T(8,128)(2,1)} %constant_dynamic-update-slice_fusion.10.p0), channel_id=1, source_target_pairs={{0,1},{1,0},{2,3},{3,2},{4,5},{5,4},{6,7},{7,6},{8,24},{9,25},{10,... | collective-permute-start | bytes 3538952 | tf_op jit(solution)/shard_map/ppermute | solution.py:50
  88.3 21.1 %collective-permute-start.19 = (bf16[8,96,768]{2,1,0:T(8,128)(2,1)}, bf16[8,96,768]{2,1,0:T(8,128)(2,1)}, u32[]{:S(2)}, u32[]{:S(2)}) collective-permute-start(bf16[8,96,768]{2,1,0:T(8,128)(2,1)} %constant_dynamic-update-slice_fusion.10.p0), channel_id=1, source_target_pairs={{0,8},{1,9},{2,10},{3,11},{4,12},{5,13},{6,14},{7,15},{8,0},{9,1},... | collective-permute-start | bytes 3538952 | tf_op jit(solution)/shard_map/ppermute | solution.py:50
  178.9 25.2 %collective-permute-start.29 = (bf16[16,24,2432]{2,1,0:T(8,128)(2,1)}, bf16[16,24,2432]{2,1,0:T(8,128)(2,1)}, u32[]{:S(2)}, u32[]{:S(2)}) collective-permute-start(bf16[16,24,2432]{2,1,0:T(8,128)(2,1)} %get-tuple-element.186), channel_id=1, source_target_pairs={{0,8},{1,9},{2,10},{3,11},{4,12},{5,13},{6,14},{7,15},{8,0},{9,1},... | collective-permute-start | bytes 5603336 | tf_op jit(solution)/shard_map/ppermute | solution.py:50
  179.3 16.5 %collective-permute-start.27 = (bf16[8,96,768]{2,1,0:T(8,128)(2,1)}, bf16[8,96,768]{2,1,0:T(8,128)(2,1)}, u32[]{:S(2)}, u32[]{:S(2)}) collective-permute-start(bf16[8,96,768]{2,1,0:T(8,128)(2,1)} %get-tuple-element.226), channel_id=1, source_target_pairs={{0,1},{1,0},{2,3},{3,2},{4,5},{5,4},{6,7},{7,6},{8,24},{9,25},{10,... | collective-permute-start | bytes 3538952 | tf_op jit(solution)/shard_map/ppermute | solution.py:50
  182.7 36.0 %collective-permute-start.31 = (bf16[8,24,3840]{2,1,0:T(8,128)(2,1)}, bf16[8,24,3840]{2,1,0:T(8,128)(2,1)}, u32[]{:S(2)}, u32[]{:S(2)}) collective-permute-start(bf16[8,24,3840]{2,1,0:T(8,128)(2,1)} %get-tuple-element.225), channel_id=1, source_target_pairs={{0,1},{1,0},{2,3},{3,2},{4,5},{5,4},{6,7},{7,6},{8,24},{9,25},{10,... | collective-permute-start | bytes 4423688 | tf_op jit(solution)/shard_map/ppermute | solution.py:50
  197.8 16.3 %collective-permute-start.32 = (bf16[4,96,768]{2,1,0:T(8,128)(2,1)S(1)}, bf16[4,96,768]{2,1,0:T(8,128)(2,1)S(1)}, u32[]{:S(2)}, u32[]{:S(2)}) collective-permute-start(bf16[4,96,768]{2,1,0:T(8,128)(2,1)S(1)} %get-tuple-element.233), channel_id=1, source_target_pairs={{0,16},{1,17},{2,18},{3,19},{4,20},{5,21},{6,22},{7,23},{8,9},{9,8... | collective-permute-start | bytes 1769480 | tf_op jit(solution)/shard_map/ppermute | solution.py:50
  206.1 27.9 %collective-permute-start.30 = (bf16[8,24,2432]{2,1,0:T(8,128)(2,1)S(1)}, bf16[8,24,2432]{2,1,0:T(8,128)(2,1)S(1)}, u32[]{:S(2)}, u32[]{:S(2)}) collective-permute-start(bf16[8,24,2432]{2,1,0:T(8,128)(2,1)S(1)} %get-tuple-element.228), channel_id=1, source_target_pairs={{0,1},{1,0},{2,3},{3,2},{4,5},{5,4},{6,7},{7,6},{8,24},{9,25},{10,... | collective-permute-start | bytes 2801672 | tf_op jit(solution)/shard_map/ppermute | solution.py:50
  214.3 21.0 %collective-permute-start.35 = (bf16[1,96,768]{2,1,0:T(8,128)(2,1)S(1)}, bf16[1,96,768]{2,1,0:T(8,128)(2,1)S(1)}, u32[]{:S(2)}, u32[]{:S(2)}) collective-permute-start(bf16[1,96,768]{2,1,0:T(8,128)(2,1)S(1)} %get-tuple-element.240), channel_id=1, source_target_pairs={{0,4},{1,5},{2,6},{3,7},{4,0},{5,1},{6,2},{7,3},{8,12},{9,13},{10,... | collective-permute-start | bytes 442376 | tf_op jit(solution)/shard_map/ppermute | solution.py:50
  216.1 19.2 %collective-permute-start.36 = (bf16[1,96,768]{2,1,0:T(8,128)(2,1)S(1)}, bf16[1,96,768]{2,1,0:T(8,128)(2,1)S(1)}, u32[]{:S(2)}, u32[]{:S(2)}) collective-permute-start(bf16[1,96,768]{2,1,0:T(8,128)(2,1)S(1)} %get-tuple-element.241), channel_id=1, source_target_pairs={{0,2},{1,3},{2,0},{3,1},{4,6},{5,7},{6,4},{7,5},{8,10},{9,11},{10,... | collective-permute-start | bytes 442376 | tf_op jit(solution)/shard_map/ppermute | solution.py:50
  216.1 19.2 %collective-permute-start.37 = (bf16[1,96,768]{2,1,0:T(8,128)(2,1)S(1)}, bf16[1,96,768]{2,1,0:T(8,128)(2,1)S(1)}, u32[]{:S(2)}, u32[]{:S(2)}) collective-permute-start(bf16[1,96,768]{2,1,0:T(8,128)(2,1)S(1)} %get-tuple-element.242), channel_id=1, source_target_pairs={{0,6},{1,7},{2,4},{3,5},{4,2},{5,3},{6,0},{7,1},{8,14},{9,15},{10,... | collective-permute-start | bytes 442376 | tf_op jit(solution)/shard_map/ppermute | solution.py:50
  220.4 15.6 %collective-permute-start.34 = (bf16[4,24,3840]{2,1,0:T(8,128)(2,1)S(1)}, bf16[4,24,3840]{2,1,0:T(8,128)(2,1)S(1)}, u32[]{:S(2)}, u32[]{:S(2)}) collective-permute-start(bf16[4,24,3840]{2,1,0:T(8,128)(2,1)S(1)} %get-tuple-element.231), channel_id=1, source_target_pairs={{0,16},{1,17},{2,18},{3,19},{4,20},{5,21},{6,22},{7,23},{8,9},{9,8... | collective-permute-start | bytes 2211848 | tf_op jit(solution)/shard_map/ppermute | solution.py:50
  236.2 19.1 %collective-permute-start.39 = (bf16[1,24,3840]{2,1,0:T(8,128)(2,1)S(1)}, bf16[1,24,3840]{2,1,0:T(8,128)(2,1)S(1)}, u32[]{:S(2)}, u32[]{:S(2)}) collective-permute-start(bf16[1,24,3840]{2,1,0:T(8,128)(2,1)S(1)} %get-tuple-element.236), channel_id=1, source_target_pairs={{0,4},{1,5},{2,6},{3,7},{4,0},{5,1},{6,2},{7,3},{8,12},{9,13},{10,... | collective-permute-start | bytes 552968 | tf_op jit(solution)/shard_map/ppermute | solution.py:50
  238.0 17.3 %collective-permute-start.40 = (bf16[1,24,3840]{2,1,0:T(8,128)(2,1)S(1)}, bf16[1,24,3840]{2,1,0:T(8,128)(2,1)S(1)}, u32[]{:S(2)}, u32[]{:S(2)}) collective-permute-start(bf16[1,24,3840]{2,1,0:T(8,128)(2,1)S(1)} %get-tuple-element.237), channel_id=1, source_target_pairs={{0,2},{1,3},{2,0},{3,1},{4,6},{5,7},{6,4},{7,5},{8,10},{9,11},{10,... | collective-permute-start | bytes 552968 | tf_op jit(solution)/shard_map/ppermute | solution.py:50
  238.0 14.3 %collective-permute-start.41 = (bf16[1,24,3840]{2,1,0:T(8,128)(2,1)S(1)}, bf16[1,24,3840]{2,1,0:T(8,128)(2,1)S(1)}, u32[]{:S(2)}, u32[]{:S(2)}) collective-permute-start(bf16[1,24,3840]{2,1,0:T(8,128)(2,1)S(1)} %get-tuple-element.239), channel_id=1, source_target_pairs={{0,6},{1,7},{2,4},{3,5},{4,2},{5,3},{6,0},{7,1},{8,14},{9,15},{10,... | collective-permute-start | bytes 552968 | tf_op jit(solution)/shard_map/ppermute | solution.py:50
  243.0 19.3 %collective-permute-start.38 = (bf16[1,24,2432]{2,1,0:T(8,128)(2,1)S(1)}, bf16[1,24,2432]{2,1,0:T(8,128)(2,1)S(1)}, u32[]{:S(2)}, u32[]{:S(2)}) collective-permute-start(bf16[1,24,2432]{2,1,0:T(8,128)(2,1)S(1)} %get-tuple-element.243), channel_id=1, source_target_pairs={{0,4},{1,5},{2,6},{3,7},{4,0},{5,1},{6,2},{7,3},{8,12},{9,13},{10,... | collective-permute-start | bytes 350216 | tf_op jit(solution)/shard_map/ppermute | solution.py:50
  244.8 17.5 %collective-permute-start.42 = (bf16[1,24,2432]{2,1,0:T(8,128)(2,1)S(1)}, bf16[1,24,2432]{2,1,0:T(8,128)(2,1)S(1)}, u32[]{:S(2)}, u32[]{:S(2)}) collective-permute-start(bf16[1,24,2432]{2,1,0:T(8,128)(2,1)S(1)} %get-tuple-element.244), channel_id=1, source_target_pairs={{0,2},{1,3},{2,0},{3,1},{4,6},{5,7},{6,4},{7,5},{8,10},{9,11},{10,... | collective-permute-start | bytes 350216 | tf_op jit(solution)/shard_map/ppermute | solution.py:50
  (65 other events, 559.7 us)
